TPU v7x, 32 devices: a whole 2x2x4 slice. The times are simulated.
32 devices in a mesh: fsdp: 16 (over z, y, core), dp: 2 (over x).
Axes of the slice: x: 2, y: 2, z: 4, core: 2. Of those that a mesh axis runs over, the one named last changes fastest.
Arguments:
- inputs: bfloat16 [4096, 8192], P(('fsdp', 'dp')), may hold values from -6 to 6
- grad_value: bfloat16 [4096, 512], P(('fsdp', 'dp')), may hold values from -2 to 2
- w_value: bfloat16 [8192, 512], P('fsdp'), may hold values from -0.0625 to 0.0625
- adapter_down: bfloat16 [16, 8192, 64], P('dp', 'fsdp'), may hold values from -0.19921875 to 0.19921875
- adapter_up: bfloat16 [16, 512, 64], P('dp', 'fsdp'), may hold values from -0.25 to 0.25
- tenant_ids: int32 [32], P(('fsdp', 'dp')), may hold values from 0 to 15, as said below
- slot_table: int32 [16], replicated, may hold values from 0 to 15, each once
Outputs:
- input_gradient_rows: bfloat16 [4096, 8192], P(('fsdp', 'dp'))
- grad_down: bfloat16 [16, 8192, 64], P('dp', 'fsdp')
- grad_up: bfloat16 [16, 512, 64], P('dp', 'fsdp')
Inputs may be any that keep to these rules, and one draw needn't show every extreme that they name: `tenant_ids`: the adapter that every token of a block of 128 tokens uses; within each token group every adapter is used by at least one block. `slot_table`: a permutation of the adapters' slots.
All inputs are finite; a program needn't handle non-finite values.
Results may differ from a plain program's by a relative error of at most 0.017.
Values may be sent and summed in bfloat16 or wider, within the bound.
No kernel may reach another device: no remote copies, remote signals or barrier semaphores. Data moves between devices by JAX's collectives and lax.ppermute only.
A program may use at most 64 MiB of HBM per device.

v0:
```python
import jax
import jax.numpy as jnp
from jax import lax
from jax.sharding import PartitionSpec as P

adapter_scale_factor = 2.0


def pick_slots(tenants, slot_table):
    count = slot_table.shape[0]
    matches = tenants[:, None] == jnp.arange(count, dtype=jnp.int32)[None, :]
    return jnp.sum(jnp.where(matches, slot_table[None, :], 0), axis=1)


def on_device(inputs, grad_value, w_value, adapter_down, adapter_up, tenant_ids, slot_table):
    local_token_count, embedding_width = inputs.shape
    kv_width = grad_value.shape[1]
    blocks_here = tenant_ids.shape[0]
    block_rows = local_token_count // blocks_here
    low_rank = adapter_down.shape[2]
    fsdp_count = lax.axis_size("fsdp")
    dp_count = lax.axis_size("dp")
    adapters = adapter_down.shape[0] * dp_count
    rows_here = w_value.shape[0]
    kv_rows = adapter_up.shape[1]
    group_ids = lax.all_gather(tenant_ids, "fsdp", axis=0, tiled=True)
    order_ids = group_ids.reshape(fsdp_count, blocks_here).T.reshape(-1)
    order_slots = pick_slots(order_ids, slot_table)
    group_down, group_up = (
        lax.all_gather(adapter_down, "dp", axis=0, tiled=True),
        lax.all_gather(adapter_up, "dp", axis=0, tiled=True),
    )
    send_down = jnp.take(group_down, order_slots, axis=0).reshape(
        blocks_here, fsdp_count, rows_here, low_rank
    )
    send_up = jnp.take(group_up, order_slots, axis=0).reshape(
        blocks_here, fsdp_count, kv_rows, low_rank
    )
    got_down, got_up = (
        lax.all_to_all(send_down, "fsdp", split_axis=1, concat_axis=1, tiled=True),
        lax.all_to_all(send_up, "fsdp", split_axis=1, concat_axis=1, tiled=True),
    )
    down_mats = got_down.reshape(blocks_here, embedding_width, low_rank)
    up_mats = got_up.reshape(blocks_here, kv_width, low_rank)
    frozen_weight_gradient = jnp.einsum(
        "tk,rk->tr",
        grad_value,
        lax.all_gather(w_value, "fsdp", axis=0, tiled=True),
        preferred_element_type=jnp.float32,
    ).astype(jnp.bfloat16)
    frozen_weight_gradient = lax.optimization_barrier(frozen_weight_gradient).astype(jnp.float32)
    x_blocks = inputs.reshape(blocks_here, block_rows, embedding_width)
    grad_blocks = grad_value.reshape(blocks_here, block_rows, kv_width)
    hidden_activation = jnp.einsum(
        "jtk,jkr->jtr", grad_blocks, up_mats, preferred_element_type=jnp.float32
    ).astype(jnp.bfloat16)
    inner_rank_product = jnp.einsum(
        "jtd,jdr->jtr", x_blocks, down_mats, preferred_element_type=jnp.float32
    ).astype(jnp.bfloat16)
    adapter_gradient = adapter_scale_factor * jnp.einsum(
        "jtr,jdr->jtd", hidden_activation, down_mats, preferred_element_type=jnp.float32
    )
    input_gradient_rows = (
        frozen_weight_gradient + adapter_gradient.reshape(local_token_count, embedding_width)
    ).astype(jnp.bfloat16)
    partial_down_factor = (
        adapter_scale_factor
        * jnp.einsum(
            "jtd,jtr->jdr", x_blocks, hidden_activation, preferred_element_type=jnp.float32
        )
    ).astype(jnp.bfloat16)
    partial_up_factor = (
        adapter_scale_factor
        * jnp.einsum(
            "jtk,jtr->jkr", grad_blocks, inner_rank_product, preferred_element_type=jnp.float32
        )
    ).astype(jnp.bfloat16)
    back_down, back_up = (
        lax.all_to_all(
            partial_down_factor.reshape(blocks_here, fsdp_count, rows_here, low_rank),
            "fsdp",
            split_axis=1,
            concat_axis=1,
            tiled=True,
        ),
        lax.all_to_all(
            partial_up_factor.reshape(blocks_here, fsdp_count, kv_rows, low_rank),
            "fsdp",
            split_axis=1,
            concat_axis=1,
            tiled=True,
        ),
    )
    onehot = (order_slots[None, :] == jnp.arange(adapters, dtype=jnp.int32)[:, None]).astype(
        jnp.bfloat16
    )
    table_down = jnp.dot(
        onehot,
        back_down.reshape(blocks_here * fsdp_count, rows_here * low_rank),
        preferred_element_type=jnp.float32,
    )
    table_up = jnp.dot(
        onehot,
        back_up.reshape(blocks_here * fsdp_count, kv_rows * low_rank),
        preferred_element_type=jnp.float32,
    )
    summed_down, summed_up = (
        lax.psum_scatter(
            table_down.astype(jnp.bfloat16), "dp", scatter_dimension=0, tiled=True
        ).astype(jnp.float32),
        lax.psum_scatter(
            table_up.astype(jnp.bfloat16), "dp", scatter_dimension=0, tiled=True
        ).astype(jnp.float32),
    )
    grad_down = summed_down.astype(jnp.bfloat16).reshape(adapter_down.shape)
    grad_up = summed_up.astype(jnp.bfloat16).reshape(adapter_up.shape)
    return (input_gradient_rows, grad_down, grad_up)


def solution(mesh):
    in_specs = (
        P(("fsdp", "dp"), None),
        P(("fsdp", "dp"), None),
        P("fsdp", None),
        P("dp", "fsdp", None),
        P("dp", "fsdp", None),
        P(("fsdp", "dp")),
        P(),
    )
    out_specs = (P(("fsdp", "dp"), None), P("dp", "fsdp", None), P("dp", "fsdp", None))
    return jax.shard_map(
        on_device, mesh=mesh, in_specs=in_specs, out_specs=out_specs, check_vma=False
    )
```

profile of v0, /device:TPU:0, one launch (start us, length us, event | category | flops | bytes accessed | tf_op | source)
XLA Modules:
  0.0 211.7 jit_solution(15274528501425204334)
XLA Ops:
  8.0 0.0 all-gather.5.cloned.1.call-start
  8.1 0.7 all-gather.5.cloned.1.call-update
  9.4 1.2 dynamic-slice
  10.6 0.8 dynamic-update-slice
  11.4 13.7 %all-reduce = s32[16]{0:T(128)S(1)} all-reduce(s32[16]{0:T(128)S(1)} %dynamic-update-slice), channel_id=1, replica_groups=mesh['fsdp'=16,'dp'=2] {'fsdp'}, use_global_device_ids=true, to_apply=%add | all-reduce | flops 16 | bytes 128
  25.1 6.5 %all_gather.14 = bf16[16,32,64]{2,1,0:T(8,128)(2,1)S(1)} all-gather(bf16[8,32,64]{2,1,0:T(8,128)(2,1)} %param.11), channel_id=1, replica_groups=mesh['fsdp'=16,'dp'=2] {'dp'}, dimensions={0}, use_global_device_ids=true | all-gather | bytes 98304 | tf_op jit(solution)/shard_map/all_gather | solution.py:31
  31.6 0.8 select_reduce_fusion
  32.5 0.6 gather_fusion
  33.1 0.1 fusion.10
  33.2 0.8 reshape.134
  33.9 3.5 %all-to-all-start = ((bf16[16,2,1024]{2,1,0:T(2,128)(2,1)}), bf16[16,2,1024]{2,1,0:T(2,128)(2,1)S(1)}, u32[]{:S(2)}, u32[]{:S(2)}) async-start(bf16[16,2,1024]{2,1,0:T(2,128)(2,1)} %reshape.134), calls=%async_computation | async-start | bytes 131072 | tf_op jit(solution)/shard_map/all_to_all | solution.py:41
  37.5 0.0 all-gather.5.cloned.1.call-done
  37.5 1.8 gather_fusion.1
  39.3 1.1 fusion.5
  40.5 3.8 %all-to-all-done = bf16[16,2,1024]{2,1,0:T(2,128)(2,1)S(1)} async-done(((bf16[16,2,1024]{2,1,0:T(2,128)(2,1)}), bf16[16,2,1024]{2,1,0:T(2,128)(2,1)S(1)}, u32[]{:S(2)}, u32[]{:S(2)}) %all-to-all-start) | async-done | bytes 65568 | tf_op jit(solution)/shard_map/all_to_all | solution.py:41
  44.3 3.7 %all-to-all-start.1 = ((bf16[1,16,512,64]{2,3,0,1:T(8,128)(2,1)}), bf16[1,16,512,64]{2,3,0,1:T(8,128)(2,1)S(1)}, u32[]{:S(2)}, u32[]{:S(2)}) async-start(bf16[1,16,512,64]{2,3,0,1:T(8,128)(2,1)} %fusion.5), calls=%async_computation.1 | async-start | bytes 2097152 | tf_op jit(solution)/shard_map/all_to_all | solution.py:40
  48.0 0.1 reshape.135
  48.1 0.2 convolution_convert_fusion.4
  48.4 0.4 fusion.2
  48.8 0.4 copy.32
  49.2 1.6 copy.26
  50.7 20.1 %all-to-all-done.1 = bf16[1,16,512,64]{2,3,0,1:T(8,128)(2,1)S(1)} async-done(((bf16[1,16,512,64]{2,3,0,1:T(8,128)(2,1)}), bf16[1,16,512,64]{2,3,0,1:T(8,128)(2,1)S(1)}, u32[]{:S(2)}, u32[]{:S(2)}) %all-to-all-start.1) | async-done | bytes 1048608 | tf_op jit(solution)/shard_map/all_to_all | solution.py:40
  70.9 6.9 %all-to-all-start.2 = ((bf16[1,16,512,64]{2,3,0,1:T(8,128)(2,1)}), bf16[1,16,512,64]{2,3,0,1:T(8,128)(2,1)}, u32[]{:S(2)}, u32[]{:S(2)}) async-start(bf16[1,16,512,64]{2,3,0,1:T(8,128)(2,1)} %copy.26), calls=%async_computation.2 | async-start | bytes 2097152 | tf_op jit(solution)/shard_map/all_to_all | solution.py:79
  77.8 1.3 copy.31
  79.1 1.0 fusion.4
  80.1 0.1 copy.28
  80.2 0.8 reshape.136
  81.0 19.7 %all-to-all-done.2 = bf16[1,16,512,64]{2,3,0,1:T(8,128)(2,1)} async-done(((bf16[1,16,512,64]{2,3,0,1:T(8,128)(2,1)}), bf16[1,16,512,64]{2,3,0,1:T(8,128)(2,1)}, u32[]{:S(2)}, u32[]{:S(2)}) %all-to-all-start.2) | async-done | bytes 1048608 | tf_op jit(solution)/shard_map/all_to_all | solution.py:79
  100.7 6.9 %all-to-all-start.3 = ((bf16[16,2,1024]{2,1,0:T(2,128)(2,1)}), bf16[16,2,1024]{2,1,0:T(2,128)(2,1)S(1)}, u32[]{:S(2)}, u32[]{:S(2)}) async-start(bf16[16,2,1024]{2,1,0:T(2,128)(2,1)} %reshape.136), calls=%async_computation.4 | async-start | bytes 131072 | tf_op jit(solution)/shard_map/all_to_all | solution.py:86
  107.6 0.0 reduce-scatter.5.cloned.1.call-start
  107.7 2.7 %copy.27 = bf16[1,16,512,64]{3,2,1,0:T(8,128)(2,1)} copy(bf16[1,16,512,64]{2,3,0,1:T(8,128)(2,1)} %all-to-all-done.2) | data formatting | bytes 2097152 | tf_op jit(solution)/shard_map/all_to_all | solution.py:79
  110.4 3.7 %reshape.108 = bf16[16,32768]{1,0:T(8,128)(2,1)} reshape(bf16[1,16,512,64]{3,2,1,0:T(8,128)(2,1)} %copy.27) | data formatting | bytes 2097152 | tf_op jit(solution)/shard_map/reshape | solution.py:99
  114.0 0.5 all-to-all-done.3
  114.5 0.1 reshape.137
  114.7 0.2 reshape.111
  114.8 0.8 convolution_convert_fusion.2
  115.6 0.0 reduce-scatter.3.cloned.1.call-start
  115.7 2.6 %convolution_convert_fusion = bf16[16,32768]{1,0:T(8,128)(2,1)} fusion(bf16[16,32768]{1,0:T(8,128)(2,1)} %reshape.108, s32[16]{0:T(128)S(1)} %select_reduce_fusion), kind=kOutput, calls=%fused_computation.2 | convolution fusion | flops 17301760 | bytes 2097216 | tf_op jit(solution)/shard_map/dot_general | solution.py:97
  118.3 0.0 all-gather.3.cloned.1.call-start
  118.4 0.5 all-gather.3.cloned.1.call-update
  118.9 7.6 %reduce-scatter.5.cloned.1.call-done = bf16[8,2048]{1,0:T(8,128)(2,1)} async-done(((bf16[16,2048]{1,0:T(8,128)(2,1)}), bf16[8,2048]{1,0:T(8,128)(2,1)}) %reduce-scatter.5.cloned.1.call-update) | async-done | bytes 32784 | tf_op jit(solution)/shard_map/reduce_scatter | solution.py:111
  126.5 1.5 reshape.112
  128.1 21.7 %reduce-scatter.3.cloned.1.call-done = bf16[8,32768]{1,0:T(8,128)(2,1)} async-done(((bf16[16,32768]{1,0:T(8,128)(2,1)}), bf16[8,32768]{1,0:T(8,128)(2,1)}) %reduce-scatter.3.cloned.1.call-update) | async-done | bytes 524304 | tf_op jit(solution)/shard_map/reduce_scatter | solution.py:108
  149.7 3.0 %reshape.109 = bf16[8,512,64]{2,1,0:T(8,128)(2,1)} reshape(bf16[8,32768]{1,0:T(8,128)(2,1)} %reduce-scatter.3.cloned.1.call-done) | data formatting | bytes 1048576 | tf_op jit(solution)/shard_map/reshape | solution.py:115
  152.8 2.3 %copy.30 = bf16[8,512,64]{1,2,0:T(8,128)(2,1)} copy(bf16[8,512,64]{2,1,0:T(8,128)(2,1)} %reshape.109) | data formatting | bytes 1048576
  155.1 41.2 %all-gather.3.cloned.1.call-done = bf16[8192,512]{1,0:T(8,128)(2,1)} async-done(((bf16[512,512]{1,0:T(8,128)(2,1)}), bf16[8192,512]{1,0:T(8,128)(2,1)}) %all-gather.3.cloned.1.call-update) | async-done | bytes 8388624 | tf_op jit(solution)/shard_map/all_gather | solution.py:48
  196.3 6.2 %convolution_convert_fusion.1 = bf16[128,8192]{1,0:T(8,128)(2,1)S(1)} fusion(bf16[128,512]{1,0:T(8,128)(2,1)S(1)} %copy-done.2, bf16[8192,512]{1,0:T(8,128)(2,1)} %all-gather.3.cloned.1.call-done), kind=kOutput, calls=%fused_computation.5 | convolution fusion | flops 1074790400 | bytes 10616832 | tf_op jit(solution)/shard_map/tk,rk->tr/dot_general | solution.py:45
  202.5 2.1 fusion.1
  (12 shorter events, 0.1 us)
Async XLA Ops:
  8.0 40.3 %copy-start = (bf16[128,8192]{1,0:T(8,128)(2,1)S(1)}, bf16[128,8192]{1,0:T(8,128)(2,1)}, u32[]{:S(2)}) copy-start(bf16[128,8192]{1,0:T(8,128)(2,1)} %param.7) | copy-start | bytes 6291460
  8.0 29.5 %all-gather.5.cloned.1.call-start = ((), (), s32[]{:S(2)}) async-start(), calls=%async_computation.7 | async-start | bytes 1572864 | tf_op jit(solution)/shard_map/all_gather | solution.py:30
  33.9 10.4 %all-to-all-start = ((bf16[16,2,1024]{2,1,0:T(2,128)(2,1)}), bf16[16,2,1024]{2,1,0:T(2,128)(2,1)S(1)}, u32[]{:S(2)}, u32[]{:S(2)}) async-start(bf16[16,2,1024]{2,1,0:T(2,128)(2,1)} %reshape.134), calls=%async_computation | async-start | bytes 131072 | tf_op jit(solution)/shard_map/all_to_all | solution.py:41
  39.3 8.8 %copy-start.2 = (bf16[128,512]{1,0:T(8,128)(2,1)S(1)}, bf16[128,512]{1,0:T(8,128)(2,1)}, u32[]{:S(2)}) copy-start(bf16[128,512]{1,0:T(8,128)(2,1)} %param.8) | copy-start | bytes 393220
  44.3 26.6 %all-to-all-start.1 = ((bf16[1,16,512,64]{2,3,0,1:T(8,128)(2,1)}), bf16[1,16,512,64]{2,3,0,1:T(8,128)(2,1)S(1)}, u32[]{:S(2)}, u32[]{:S(2)}) async-start(bf16[1,16,512,64]{2,3,0,1:T(8,128)(2,1)} %fusion.5), calls=%async_computation.1 | async-start | bytes 2097152 | tf_op jit(solution)/shard_map/all_to_all | solution.py:40
  70.9 6.9 %copy-start.1 = (bf16[1,16,512,64]{2,3,0,1:T(8,128)(2,1)}, bf16[1,16,512,64]{2,3,0,1:T(8,128)(2,1)S(1)}, u32[]{:S(2)}) copy-start(bf16[1,16,512,64]{2,3,0,1:T(8,128)(2,1)S(1)} %all-to-all-done.1) | copy-start | bytes 3145732
  70.9 29.9 %all-to-all-start.2 = ((bf16[1,16,512,64]{2,3,0,1:T(8,128)(2,1)}), bf16[1,16,512,64]{2,3,0,1:T(8,128)(2,1)}, u32[]{:S(2)}, u32[]{:S(2)}) async-start(bf16[1,16,512,64]{2,3,0,1:T(8,128)(2,1)} %copy.26), calls=%async_computation.2 | async-start | bytes 2097152 | tf_op jit(solution)/shard_map/all_to_all | solution.py:79
  100.7 13.8 %all-to-all-start.3 = ((bf16[16,2,1024]{2,1,0:T(2,128)(2,1)}), bf16[16,2,1024]{2,1,0:T(2,128)(2,1)S(1)}, u32[]{:S(2)}, u32[]{:S(2)}) async-start(bf16[16,2,1024]{2,1,0:T(2,128)(2,1)} %reshape.136), calls=%async_computation.4 | async-start | bytes 131072 | tf_op jit(solution)/shard_map/all_to_all | solution.py:86
  107.6 18.9 %reduce-scatter.5.cloned.1.call-start = ((), (), s32[]{:S(2)}) async-start(), calls=%async_computation.9 | async-start | bytes 98304 | tf_op jit(solution)/shard_map/reduce_scatter | solution.py:111
  115.6 34.1 %reduce-scatter.3.cloned.1.call-start = ((), (), s32[]{:S(2)}) async-start(), calls=%async_computation.8 | async-start | bytes 1572864 | tf_op jit(solution)/shard_map/reduce_scatter | solution.py:108
  118.3 78.0 %all-gather.3.cloned.1.call-start = ((), (), s32[]{:S(2)}) async-start(), calls=%async_computation.6 | async-start | bytes 8912896 | tf_op jit(solution)/shard_map/all_gather | solution.py:48
Sparse Core Ops, SparseCore 0:
  10.4 25.3 all-gather.4
  115.8 10.7 reduce-scatter.4
  129.4 20.3 reduce-scatter.2
Sparse Core Ops, SparseCore 1:
  121.0 75.3 all-gather.2
where the time goes:
time: 213 us; the launch traced here: 212 us
  waiting for transfers between devices  116 us (54%)
  local copies, waits for them, and re-layouts  23 us (11%)
  starting transfers between devices  21.1 us (10%)
  blocking collectives  20.2 us (9%)
  between operations  16 us (8%)
  matrix products  13.3 us (6%)
    all_gather x1, waiting for transfers between devices, on_device(): lax.all_gather(w_value, 'fsdp', axis=0, tiled=True)  41.2 us
    reduce_scatter x1, waiting for transfers between devices, on_device(): lax.psum_scatter(table_down.astype(jnp.bfloat16), 'dp', scatter_dimension...  21.7 us
    all_to_all x1, waiting for transfers between devices, on_device(): lax.all_to_all(send_down, 'fsdp', split_axis=1, concat_axis=1, tiled=True)  20.1 us
    all_to_all x1, waiting for transfers between devices, on_device(): lax.all_to_all(partial_down_factor.reshape(blocks_here, fsdp_count, rows_...  19.7 us
    unnamed x1, blocking collectives  13.7 us
    unnamed x16, local copies, waits for them, and re-layouts  7.85 us
    reduce_scatter x1, waiting for transfers between devices, on_device(): lax.psum_scatter(table_up.astype(jnp.bfloat16), 'dp', scatter_dimension=0...  7.62 us
    all_to_all x1, starting transfers between devices, on_device(): lax.all_to_all(partial_down_factor.reshape(blocks_here, fsdp_count, rows_...  6.87 us
  transfers between devices with their start and end apart: 8, of which 7 were waited for; matrix products, arithmetic and copies ran while one was open for 14% of the time, Pallas kernels for 0%

commit v1 on v0

v1 whole, which is shorter than its diff:
```python
import functools

import jax
import jax.numpy as jnp
from jax import lax
from jax.experimental import pallas as pl
from jax.experimental.pallas import tpu as pltpu
from jax.sharding import PartitionSpec as P

adapter_scale_factor = 2.0
lanes = 128
BF16, F32 = jnp.bfloat16, jnp.float32
NT = (((1,), (1,)), ((), ()))
TN = (((0,), (0,)), ((), ()))
NN = (((1,), (0,)), ((), ()))


def params():
    return pltpu.CompilerParams(vmem_limit_bytes=40 * 1024 * 1024)


def cost(flops, nbytes):
    return pl.CostEstimate(flops=flops, bytes_accessed=nbytes, transcendentals=0)


def dot(a, b, dims):
    return lax.dot_general(a, b, dims, preferred_element_type=F32)


def packed_rows(kv_rows):
    if kv_rows % 32 == 0:
        return kv_rows // 2, 2
    return -(-kv_rows // 16) * 16, 1


def pack_up(block):
    kv_rows, rank = block.shape
    rows, groups = packed_rows(kv_rows)
    if groups == 2:
        return jnp.concatenate([block[:rows], block[rows:]], axis=1)
    block = jnp.concatenate([block, jnp.zeros((kv_rows, lanes - rank), block.dtype)], axis=1)
    if rows == kv_rows:
        return block
    return jnp.concatenate([block, jnp.zeros((rows - kv_rows, lanes), block.dtype)], axis=0)


def unpack_up(packed, kv_rows, rank):
    rows, groups = packed_rows(kv_rows)
    if groups == 2:
        return jnp.concatenate([packed[:, :rank], packed[:, rank:]], axis=0)
    return packed[:kv_rows, :rank]


def wide(ref, index, first, count, rank):
    return jnp.concatenate(
        [
            ref[index, pl.ds(pl.multiple_of((first + j) * rank, 16), rank), :]
            for j in range(count)
        ],
        axis=1,
    )


def select_kernel(dp_count, ids, table, *refs):
    downs, ups, out = refs[:dp_count], refs[dp_count : 2 * dp_count], refs[-1]
    own, rank, rows = downs[0].shape
    here = lax.axis_index("dp")
    cut = rows // lanes * rank

    @pl.loop(0, out.shape[0])
    def _(k):
        slot = table[ids[k]]
        place = slot % own
        step = (slot // own) ^ here
        for j in range(dp_count):

            @pl.when(step == j)
            def _():
                for c in range(rows // lanes):
                    out[k, c * rank : (c + 1) * rank, :] = downs[j][
                        place, :, c * lanes : (c + 1) * lanes
                    ]
                out[k, cut:, :] = pack_up(ups[j][place])


def middle_kernel(kv_rows, rank, x, g, got, hidden_out, back):
    fsdp_count = got.shape[0]
    tiles = x.shape[1] // fsdp_count // lanes
    rows = tiles * lanes
    cut = tiles * rank
    up = jnp.concatenate(
        [unpack_up(got[f, cut:, :], kv_rows, rank) for f in range(fsdp_count)], axis=0
    )
    hidden = dot(g[...], up, NN).astype(BF16)
    hidden_out[...] = hidden
    inner = jnp.zeros((x.shape[0], rank), F32)
    for f in range(fsdp_count):
        x_part = x[:, f * rows : (f + 1) * rows]
        inner += dot(x_part, wide(got, f, 0, tiles, rank), NT)
        down = (adapter_scale_factor * dot(hidden, x_part, TN)).astype(BF16)
        for c in range(tiles):
            back[f, c * rank : (c + 1) * rank, :] = down[:, c * lanes : (c + 1) * lanes]
    part_up = (adapter_scale_factor * dot(g[...], inner.astype(BF16), TN)).astype(BF16)
    for f in range(fsdp_count):
        back[f, cut:, :] = pack_up(part_up[f * kv_rows : (f + 1) * kv_rows])


def base_kernel(g_counts, w_count, *refs):
    gs, ws = refs[: len(g_counts)], refs[len(g_counts) : len(g_counts) + w_count]
    outs = refs[len(g_counts) + w_count :]
    at = 0
    cols = ws[0].shape[0]
    for ref, count in zip(gs, g_counts):
        rows = ref.shape[0] // count
        for n in range(count):
            for k in range(w_count):
                outs[at][:, k * cols : (k + 1) * cols] = dot(
                    ref[n * rows : (n + 1) * rows, :], ws[k][...], NT
                ).astype(BF16)
            at += 1


def out_kernel(rels, layers, inner_count, split, rows, rank, hidden, got, *refs):
    pieces, out = refs[:-1], refs[-1]
    f_here = lax.axis_index("fsdp")
    d_here = lax.axis_index("dp") % split
    cols = rows // split
    tiles = cols // lanes
    h = hidden[...]
    for (i_rel, d_rel), piece in zip(rels, pieces):
        d = d_here ^ d_rel
        for k in range(layers):
            f = f_here ^ (k * inner_count + i_rel)
            adapter = wide(got, f, d * tiles, tiles, rank)
            low = adapter_scale_factor * dot(h, adapter, NN)
            start = pl.multiple_of(f * rows + d * cols, lanes)
            out[:, pl.ds(start, cols)] = (
                piece[:, k * cols : (k + 1) * cols].astype(F32) + low
            ).astype(BF16)


def sort_kernel(dp_count, own, ids, table, got, *sends):
    here = lax.axis_index("dp")

    @pl.loop(0, got.shape[0])
    def _(k):
        slot = table[ids[k]]
        place = slot % own
        step = (slot // own) ^ here
        for j in range(1, dp_count):

            @pl.when(step == j)
            def _():
                sends[j - 1][place] = got[k]


def sum_kernel(dp_count, kv_rows, ids, table, got, *refs):
    received, (down, up) = refs[: dp_count - 1], refs[dp_count - 1 :]
    own, rank, rows = down.shape
    here = lax.axis_index("dp")
    tiles = rows // lanes

    @pl.loop(0, got.shape[0])
    def _(k):
        slot = table[ids[k]]
        place = slot % own

        @pl.when(slot // own == here)
        def _():
            total = got[k].astype(F32)
            for ref in received:
                total += ref[place].astype(F32)
            total = total.astype(BF16)
            for c in range(tiles):
                down[place, :, c * lanes : (c + 1) * lanes] = total[c * rank : (c + 1) * rank]
            up[place] = unpack_up(total[tiles * rank :], kv_rows, rank)


def vmem(count):
    return [pl.BlockSpec(memory_space=pltpu.VMEM)] * count


def smem(count):
    return [pl.BlockSpec(memory_space=pltpu.SMEM)] * count


def xor_pairs(count, bits):
    return [(n, n ^ bits) for n in range(count)]


def on_device(inputs, grad_value, w_value, adapter_down, adapter_up, tenant_ids, slot_table):
    tokens, width = inputs.shape
    kv_width = grad_value.shape[1]
    own, rows, rank = adapter_down.shape
    kv_rows = adapter_up.shape[1]
    fsdp_count = lax.axis_size("fsdp")
    dp_count = lax.axis_size("dp")
    inner_count = 1
    while inner_count * inner_count < fsdp_count:
        inner_count *= 2
    layers = fsdp_count // inner_count
    split = 1
    while split * 2 <= dp_count and rows // (split * 2) >= lanes:
        split *= 2
    cols = rows // split
    tall = rows // lanes * rank + packed_rows(kv_rows)[0]

    down_t = adapter_down.transpose(0, 2, 1)
    downs, ups = [down_t], [adapter_up]
    for j in range(1, dp_count):
        downs.append(lax.ppermute(down_t, "dp", xor_pairs(dp_count, j)))
        ups.append(lax.ppermute(adapter_up, "dp", xor_pairs(dp_count, j)))
    ids = lax.all_to_all(
        jnp.broadcast_to(tenant_ids[:, None], (fsdp_count, 1)), "fsdp", 0, 0, tiled=True
    ).reshape(-1)

    w_here = lax.dynamic_slice_in_dim(w_value, lax.axis_index("dp") % split * cols, cols, 0)
    ws = [w_here] + [
        lax.ppermute(w_here, "fsdp", xor_pairs(fsdp_count, k * inner_count))
        for k in range(1, layers)
    ]
    gs, g_counts, rels = [grad_value], [1], [(0, 0)]
    held = grad_value
    bit = 1
    while bit < split:
        new = lax.ppermute(held, "dp", xor_pairs(dp_count, bit))
        gs, g_counts = gs + [new], g_counts + [len(rels)]
        rels = rels + [(i, d | bit) for i, d in rels]
        held = jnp.concatenate([held, new], axis=0)
        bit *= 2
    bit = inner_count // 2
    while bit >= 1:
        new = lax.ppermute(held, "fsdp", xor_pairs(fsdp_count, bit))
        gs, g_counts = gs + [new], g_counts + [len(rels)]
        rels = rels + [(i | bit, d) for i, d in rels]
        bit //= 2
        if bit >= 1:
            held = jnp.concatenate([held, new], axis=0)
    piece = jax.ShapeDtypeStruct((tokens, layers * cols), BF16)
    pieces = pl.pallas_call(
        functools.partial(base_kernel, g_counts, layers),
        out_shape=[piece] * len(rels),
        in_specs=vmem(len(gs) + layers),
        out_specs=vmem(len(rels)),
        compiler_params=params(),
        cost_estimate=cost(2 * tokens * width * kv_width, 4 * tokens * width),
        name="base",
    )(*gs, *ws)
    total = fsdp_count * dp_count
    pieces = [pieces[0]] + [
        lax.ppermute(p, ("fsdp", "dp"), xor_pairs(total, i * dp_count + d))
        for (i, d), p in zip(rels[1:], pieces[1:])
    ]

    box = jax.ShapeDtypeStruct((fsdp_count, tall, lanes), BF16)
    box_bytes = 2 * fsdp_count * tall * lanes
    sent = pl.pallas_call(
        functools.partial(select_kernel, dp_count),
        out_shape=box,
        in_specs=smem(2) + vmem(2 * dp_count),
        out_specs=pl.BlockSpec(memory_space=pltpu.VMEM),
        compiler_params=params(),
        cost_estimate=cost(0, 2 * box_bytes),
        name="select",
    )(ids, slot_table, *downs, *ups)
    got = lax.all_to_all(sent, "fsdp", 0, 0, tiled=True)

    hidden, back = pl.pallas_call(
        functools.partial(middle_kernel, kv_rows, rank),
        out_shape=[jax.ShapeDtypeStruct((tokens, rank), BF16), box],
        in_specs=vmem(3),
        out_specs=vmem(2),
        compiler_params=params(),
        cost_estimate=cost(4 * tokens * width * rank, 2 * tokens * width + 2 * box_bytes),
        name="middle",
    )(inputs, grad_value, got)
    returned = lax.all_to_all(back, "fsdp", 0, 0, tiled=True)

    input_gradient_rows = pl.pallas_call(
        functools.partial(out_kernel, rels, layers, inner_count, split, rows, rank),
        out_shape=jax.ShapeDtypeStruct((tokens, width), BF16),
        in_specs=vmem(2 + len(rels)),
        out_specs=pl.BlockSpec(memory_space=pltpu.VMEM),
        compiler_params=params(),
        cost_estimate=cost(2 * tokens * width * rank, 4 * tokens * width + box_bytes),
        name="rows",
    )(hidden, got, *pieces)

    sends = pl.pallas_call(
        functools.partial(sort_kernel, dp_count, own),
        out_shape=[jax.ShapeDtypeStruct((own, tall, lanes), BF16)] * (dp_count - 1),
        in_specs=smem(2) + vmem(1),
        out_specs=vmem(dp_count - 1),
        compiler_params=params(),
        cost_estimate=cost(0, 2 * box_bytes),
        name="sort",
    )(ids, slot_table, returned)
    received = [
        lax.ppermute(s, "dp", xor_pairs(dp_count, j + 1)) for j, s in enumerate(sends)
    ]
    grad_down_t, grad_up = pl.pallas_call(
        functools.partial(sum_kernel, dp_count, kv_rows),
        out_shape=[
            jax.ShapeDtypeStruct((own, rank, rows), BF16),
            jax.ShapeDtypeStruct(adapter_up.shape, BF16),
        ],
        in_specs=smem(2) + vmem(dp_count),
        out_specs=vmem(2),
        compiler_params=params(),
        cost_estimate=cost(0, 2 * box_bytes),
        name="sums",
    )(ids, slot_table, returned, *received)
    return (input_gradient_rows, grad_down_t.transpose(0, 2, 1), grad_up)


def solution(mesh):
    in_specs = (
        P(("fsdp", "dp"), None),
        P(("fsdp", "dp"), None),
        P("fsdp", None),
        P("dp", "fsdp", None),
        P("dp", "fsdp", None),
        P(("fsdp", "dp")),
        P(),
    )
    out_specs = (P(("fsdp", "dp"), None), P("dp", "fsdp", None), P("dp", "fsdp", None))
    return jax.shard_map(
        on_device, mesh=mesh, in_specs=in_specs, out_specs=out_specs, check_vma=False
    )
```

time: 213 us -> 149 us (0.70)
  waiting for transfers between devices: 116 us -> 62.9 us
  blocking collectives: 20.2 us -> 47 us
  local copies, waits for them, and re-layouts: 23 us -> 4.19 us
  between operations: 16 us -> 1.4 us
  matrix products: 13.3 us -> 0 us
  Pallas kernels: 0 us -> 12.3 us
    ppermute x0 -> x16, waiting for transfers between devices: none -> 62.9 us  [the longest x3 24 us: on_device(): lax.ppermute(w_here, 'fsdp', xor_pairs(fsdp_count, k * inner_count))]
    all_to_all x0 -> x2, blocking collectives: none -> 47 us  [the longest x1 34.4 us: on_device(): got = lax.all_to_all(sent, 'fsdp', 0, 0, tiled=True)]
    all_to_all x4 -> x1, waiting for transfers between devices: 44.2 us -> 0.01 us  [on_device(): returned = lax.all_to_all(back, 'fsdp', 0, 0, tiled=True)]
    all_gather x2 -> x0, waiting for transfers between devices: 41.2 us -> none  [the longest x1 41.2 us: on_device(): lax.all_gather(w_value, 'fsdp', axis=0, tiled=True)]
    reduce_scatter x2 -> x0, waiting for transfers between devices: 29.3 us -> none  [the longest x1 21.7 us: on_device(): lax.psum_scatter(table_down.astype(jnp.bfloat16), 'dp', scatter_dimension...]
    all_to_all x4 -> x1, starting transfers between devices: 20.9 us -> 3.7 us  [on_device(): returned = lax.all_to_all(back, 'fsdp', 0, 0, tiled=True)]
    ppermute x0 -> x16, starting transfers between devices: none -> 16 us  [the longest x3 4.45 us: on_device(): lax.ppermute(w_here, 'fsdp', xor_pairs(fsdp_count, k * inner_count))]
    unnamed x1 -> x0, blocking collectives: 13.7 us -> none
  transfers between devices with their start and end apart: 8 -> 17, of which waited for: 7 -> 9; matrix products, arithmetic and copies ran while one was open for 14% -> 1% of each run, Pallas kernels for 0% -> 5%
where the time goes in v1:
time: 149 us
  waiting for transfers between devices  62.9 us (42%)
  blocking collectives  47 us (32%)
  starting transfers between devices  19.7 us (13%)
  Pallas kernels  12.3 us (8%)
  local copies, waits for them, and re-layouts  4.19 us (3%)
    all_to_all x1, blocking collectives, on_device(): got = lax.all_to_all(sent, 'fsdp', 0, 0, tiled=True)  34.4 us
    ppermute x3, waiting for transfers between devices, on_device(): lax.ppermute(w_here, 'fsdp', xor_pairs(fsdp_count, k * inner_count))  24 us
    ppermute x7, waiting for transfers between devices, on_device(): lax.ppermute(p, ('fsdp', 'dp'), xor_pairs(total, i * dp_count + d))  23.5 us
    all_to_all x1, blocking collectives, on_device(): lax.all_to_all(jnp.broadcast_to(tenant_ids[:, None], (fsdp_count, 1)), 'f...  12.6 us
    ppermute x2, waiting for transfers between devices, on_device(): new = lax.ppermute(held, 'fsdp', xor_pairs(fsdp_count, bit))  11.2 us
    ppermute x3, starting transfers between devices, on_device(): lax.ppermute(w_here, 'fsdp', xor_pairs(fsdp_count, k * inner_count))  4.45 us
    ppermute x1, waiting for transfers between devices, on_device(): new = lax.ppermute(held, 'dp', xor_pairs(dp_count, bit))  4.2 us
    unnamed x20, local copies, waits for them, and re-layouts  4.16 us
  transfers between devices with their start and end apart: 17, of which 9 were waited for; matrix products, arithmetic and copies ran while one was open for 1% of the time, Pallas kernels for 5%

profile of v1, /device:TPU:0, one launch (start us, length us, event | category | flops | bytes accessed | tf_op | source)
XLA Modules:
  0.0 148.6 jit_solution(4610180577215978722)
XLA Ops:
  0.6 0.0 copy-start
  0.6 3.0 %collective-permute-start = (bf16[8,64,512]{2,1,0:T(8,128)(2,1)}, bf16[8,64,512]{2,1,0:T(8,128)(2,1)S(1)}, u32[]{:S(2)}, u32[]{:S(2)}) collective-permute-start(bf16[8,64,512]{2,1,0:T(8,128)(2,1)} %bitcast.4), channel_id=1, source_target_pairs={{0,1},{1,0},{2,3},{3,2},{4,5},{5,4},{6,7},{7,6},{8,9},{9,8},{10,11... | collective-permute-start | bytes 1572872 | tf_op jit(solution)/shard_map/ppermute | solution.py:211
  3.6 0.1 collective-permute-start.1
  4.4 12.6 %all_to_all.16 = s32[16,1,1]{2,1,0:T(1,128)S(1)} all-to-all(s32[16,1,1]{2,1,0:T(1,128)S(1)} %broadcast_in_dim.9), channel_id=1, replica_groups=mesh['fsdp'=16,'dp'=2] {'fsdp'}, dimensions={0} | all-to-all | bytes 128 | tf_op jit(solution)/shard_map/all_to_all | solution.py:213
  17.0 0.4 reduce.ids
  17.4 0.0 collective-permute-done.1.refs_3_
  17.4 0.0 collective-permute-done.refs_1_
  17.4 0.0 copy-start.4
  17.4 1.0 copy-done.4
  18.4 0.8 copy-done.5
  19.3 0.7 copy-done.8
  19.9 1.7 %select.3 = bf16[16,272,128]{2,1,0:T(8,128)(2,1)S(1)} custom-call(s32[16]{0:T(128)S(1)} %reduce.ids, s32[16]{0:T(128)S(1)} %copy-done.8, bf16[8,64,512]{2,1,0:T(8,128)(2,1)S(1)} %bitcast.5, bf16[8,64,512]{2,1,0:T(8,128)(2,1)S(1)} %collective-permute-done.refs_1_, bf16[8,32,64]{2,1,0:T(8,128)(2,1)S(1)} %copy-done.5, ...), custom_call_target="tpu_custom_call" | custom-call | bytes 2228224 | tf_op jit(solution)/shard_map/select/pallas_call | solution.py:257
  21.6 34.4 %all_to_all.17.got = bf16[16,272,128]{2,1,0:T(8,128)(2,1)S(1)} all-to-all(bf16[16,272,128]{2,1,0:T(8,128)(2,1)S(1)} %select.3), channel_id=1, replica_groups=mesh['fsdp'=16,'dp'=2] {'fsdp'}, dimensions={0} | all-to-all | bytes 2228224 | tf_op jit(solution)/shard_map/all_to_all | solution.py:266
  56.1 1.3 middle.1
  57.4 0.0 copy-start.3
  57.4 1.0 copy-done.3
  58.4 0.6 copy-done.6
  59.0 3.7 %all-to-all-start.2 = ((bf16[16,272,128]{2,1,0:T(8,128)(2,1)}), bf16[16,272,128]{2,1,0:T(8,128)(2,1)S(1)}, u32[]{:S(2)}, u32[]{:S(2)}) async-start(bf16[16,272,128]{2,1,0:T(8,128)(2,1)} %copy-done.3), calls=%async_computation.2 | async-start | bytes 2228224 | tf_op jit(solution)/shard_map/all_to_all | solution.py:277
  62.7 0.0 copy-start.9
  62.7 1.6 %collective-permute-start.2 = (bf16[128,512]{1,0:T(8,128)(2,1)S(1)}, bf16[128,512]{1,0:T(8,128)(2,1)S(1)}, u32[]{:S(2)}, u32[]{:S(2)}) collective-permute-start(bf16[128,512]{1,0:T(8,128)(2,1)S(1)} %copy-done.2), channel_id=1, source_target_pairs={{0,1},{1,0},{2,3},{3,2},{4,5},{5,4},{6,7},{7,6},{8,9},{9,8},{10,11... | collective-permute-start | bytes 393224 | tf_op jit(solution)/shard_map/ppermute | solution.py:226
  64.3 4.2 %collective-permute-done.2.refs_1_ = bf16[128,512]{1,0:T(8,128)(2,1)S(1)} collective-permute-done((bf16[128,512]{1,0:T(8,128)(2,1)S(1)}, bf16[128,512]{1,0:T(8,128)(2,1)S(1)}, u32[]{:S(2)}, u32[]{:S(2)}) %collective-permute-start.2) | collective-permute-done | bytes 131104 | tf_op jit(solution)/shard_map/ppermute | solution.py:226
  68.5 1.7 %collective-permute-start.3 = (bf16[256,512]{1,0:T(8,128)(2,1)S(1)}, bf16[256,512]{1,0:T(8,128)(2,1)S(1)}, u32[]{:S(2)}, u32[]{:S(2)}) collective-permute-start(bf16[256,512]{1,0:T(8,128)(2,1)S(1)} %pad_maximum_fusion.1), channel_id=1, source_target_pairs={{0,4},{2,6},{4,0},{6,2},{8,12},{10,14},{12,8},{14,10},{16,20},{18,... | collective-permute-start | bytes 786440 | tf_op jit(solution)/shard_map/ppermute | solution.py:233
  70.2 11.2 %collective-permute-done.3.refs_2_ = bf16[256,512]{1,0:T(8,128)(2,1)S(1)} collective-permute-done((bf16[256,512]{1,0:T(8,128)(2,1)S(1)}, bf16[256,512]{1,0:T(8,128)(2,1)S(1)}, u32[]{:S(2)}, u32[]{:S(2)}) %collective-permute-start.3) | collective-permute-done | bytes 262176 | tf_op jit(solution)/shard_map/ppermute | solution.py:233
  81.4 0.8 pad_maximum_fusion
  82.3 3.8 %collective-permute-start.7 = (bf16[256,512]{1,0:T(8,128)(2,1)S(1)}, bf16[256,512]{1,0:T(8,128)(2,1)}, u32[]{:S(2)}, u32[]{:S(2)}) collective-permute-start(bf16[256,512]{1,0:T(8,128)(2,1)S(1)} %constant_dynamic-slice_fusion.refs_4_), channel_id=1, source_target_pairs={{0,24},{2,26},{4,28},{6,30},{8,16},{10,18},{12,20},{14,22},{16,8},... | collective-permute-start | bytes 786440 | tf_op jit(solution)/shard_map/ppermute | solution.py:219
  86.1 0.7 collective-permute-start.5
  86.7 0.0 all-to-all-done.2.got
  86.7 1.0 sort.1
  87.7 0.0 copy-start.7
  87.7 1.6 %collective-permute-start.15 = (bf16[8,272,128]{2,1,0:T(8,128)(2,1)S(1)}, bf16[8,272,128]{2,1,0:T(8,128)(2,1)S(1)}, u32[]{:S(2)}, u32[]{:S(2)}) collective-permute-start(bf16[8,272,128]{2,1,0:T(8,128)(2,1)S(1)} %sort.1), channel_id=1, source_target_pairs={{0,1},{1,0},{2,3},{3,2},{4,5},{5,4},{6,7},{7,6},{8,9},{9,8},{10,11... | collective-permute-start | bytes 1671176 | tf_op jit(solution)/shard_map/ppermute | solution.py:299
  89.3 4.3 %collective-permute-done.7.refs_7_ = bf16[256,512]{1,0:T(8,128)(2,1)} collective-permute-done((bf16[256,512]{1,0:T(8,128)(2,1)S(1)}, bf16[256,512]{1,0:T(8,128)(2,1)}, u32[]{:S(2)}, u32[]{:S(2)}) %collective-permute-start.7) | collective-permute-done | bytes 262176 | tf_op jit(solution)/shard_map/ppermute | solution.py:219
  93.6 19.7 %collective-permute-done.6.refs_6_ = bf16[256,512]{1,0:T(8,128)(2,1)} collective-permute-done((bf16[256,512]{1,0:T(8,128)(2,1)S(1)}, bf16[256,512]{1,0:T(8,128)(2,1)}, u32[]{:S(2)}, u32[]{:S(2)}) %collective-permute-start.6) | collective-permute-done | bytes 262176 | tf_op jit(solution)/shard_map/ppermute | solution.py:219
  113.3 4.1 %base.1 = (bf16[128,1024]{1,0:T(8,128)(2,1)S(1)}, bf16[128,1024]{1,0:T(8,128)(2,1)S(1)}, bf16[128,1024]{1,0:T(8,128)(2,1)S(1)}, bf16[128,1024]{1,0:T(8,128)(2,1)...) custom-call(bf16[128,512]{1,0:T(8,128)(2,1)S(1)} %copy-done.2, ...), custom_call_target="tpu_custom_call" | custom-call | flops 1073741824 | bytes 4194304 | tf_op jit(solution)/shard_map/base/pallas_call | solution.py:240
  117.3 1.6 %collective-permute-start.8 = (bf16[128,1024]{1,0:T(8,128)(2,1)S(1)}, bf16[128,1024]{1,0:T(8,128)(2,1)S(1)}, u32[]{:S(2)}, u32[]{:S(2)}) collective-permute-start(bf16[128,1024]{1,0:T(8,128)(2,1)S(1)} %get-tuple-element.17), channel_id=1, source_target_pairs={{0,1},{1,0},{2,3},{3,2},{4,5},{5,4},{6,7},{7,6},{8,9},{9,8},{10,11... | collective-permute-start | bytes 786440 | tf_op jit(solution)/shard_map/ppermute | solution.py:251
  118.9 1.5 collective-permute-start.9
  120.4 0.5 collective-permute-start.10
  120.9 0.0 collective-permute-start.11
  120.9 5.7 %collective-permute-done.8.refs_1_ = bf16[128,1024]{1,0:T(8,128)(2,1)S(1)} collective-permute-done((bf16[128,1024]{1,0:T(8,128)(2,1)S(1)}, bf16[128,1024]{1,0:T(8,128)(2,1)S(1)}, u32[]{:S(2)}, u32[]{:S(2)}) %collective-permute-start.8) | collective-permute-done | bytes 262176 | tf_op jit(solution)/shard_map/ppermute | solution.py:251
  126.6 0.0 collective-permute-start.12
  126.6 4.5 %collective-permute-done.9.refs_2_ = bf16[128,1024]{1,0:T(8,128)(2,1)S(1)} collective-permute-done((bf16[128,1024]{1,0:T(8,128)(2,1)S(1)}, bf16[128,1024]{1,0:T(8,128)(2,1)S(1)}, u32[]{:S(2)}, u32[]{:S(2)}) %collective-permute-start.9) | collective-permute-done | bytes 262176 | tf_op jit(solution)/shard_map/ppermute | solution.py:251
  131.1 0.0 collective-permute-start.13
  131.1 1.9 %collective-permute-done.10.refs_3_ = bf16[128,1024]{1,0:T(8,128)(2,1)S(1)} collective-permute-done((bf16[128,1024]{1,0:T(8,128)(2,1)S(1)}, bf16[128,1024]{1,0:T(8,128)(2,1)S(1)}, u32[]{:S(2)}, u32[]{:S(2)}) %collective-permute-start.10) | collective-permute-done | bytes 262176 | tf_op jit(solution)/shard_map/ppermute | solution.py:251
  133.0 0.0 collective-permute-start.14
  133.0 0.0 collective-permute-done.11.refs_4_
  133.0 2.9 %collective-permute-done.12.refs_5_ = bf16[128,1024]{1,0:T(8,128)(2,1)S(1)} collective-permute-done((bf16[128,1024]{1,0:T(8,128)(2,1)S(1)}, bf16[128,1024]{1,0:T(8,128)(2,1)S(1)}, u32[]{:S(2)}, u32[]{:S(2)}) %collective-permute-start.12) | collective-permute-done | bytes 262176 | tf_op jit(solution)/shard_map/ppermute | solution.py:251
  136.0 8.4 %collective-permute-done.13.refs_6_ = bf16[128,1024]{1,0:T(8,128)(2,1)S(1)} collective-permute-done((bf16[128,1024]{1,0:T(8,128)(2,1)S(1)}, bf16[128,1024]{1,0:T(8,128)(2,1)S(1)}, u32[]{:S(2)}, u32[]{:S(2)}) %collective-permute-start.13) | collective-permute-done | bytes 262176 | tf_op jit(solution)/shard_map/ppermute | solution.py:251
  144.4 2.1 %rows.1 = bf16[128,8192]{1,0:T(8,128)(2,1)} custom-call(bf16[128,64]{1,0:T(8,128)(2,1)S(1)} %copy-done.7, bf16[16,272,128]{2,1,0:T(8,128)(2,1)S(1)} %all_to_all.17.got, bf16[128,1024]{1,0:T(8,128)(2,1)S(1)} %get-tuple-element.16.refs_0_, bf16[128,1024]{1,0:T(8,128)(2,1)S(1)} %collective-permute-done.8.refs_1_, ...), custom_call_target="tpu_custom_call" | custom-call | flops 134217728 | bytes 5308416 | tf_op jit(solution)/shard_map/rows/pallas_call | solution.py:279
  146.5 2.1 %sums.1 = (bf16[8,64,512]{2,1,0:T(8,128)(2,1)}, bf16[8,32,64]{2,1,0:T(8,128)(2,1)}) custom-call(s32[16]{0:T(128)S(1)} %reduce.ids, s32[16]{0:T(128)S(1)} %copy-done.9, bf16[16,272,128]{2,1,0:T(8,128)(2,1)S(1)} %all-to-all-done.2.got, bf16[8,272,128]{2,1,0:T(8,128)(2,1)S(1)} %collective-permute-done.15.refs_0_), custom_call_target="tpu_custom_call" | custom-call | bytes 2228224 | tf_op jit(solution)/shard_map/sums/pallas_call | solution.py:301
  (19 shorter events, 0.1 us)
Async XLA Ops:
  0.6 81.6 %copy-start = (bf16[512,512]{1,0:T(8,128)(2,1)S(1)}, bf16[512,512]{1,0:T(8,128)(2,1)}, u32[]{:S(2)}) copy-start(bf16[512,512]{1,0:T(8,128)(2,1)} %param.9) | copy-start | bytes 1572868
  0.6 16.7 %collective-permute-start = (bf16[8,64,512]{2,1,0:T(8,128)(2,1)}, bf16[8,64,512]{2,1,0:T(8,128)(2,1)S(1)}, u32[]{:S(2)}, u32[]{:S(2)}) collective-permute-start(bf16[8,64,512]{2,1,0:T(8,128)(2,1)} %bitcast.4), channel_id=1, source_target_pairs={{0,1},{1,0},{2,3},{3,2},{4,5},{5,4},{6,7},{7,6},{8,9},{9,8},{10,11... | collective-permute-start | bytes 1572872 | tf_op jit(solution)/shard_map/ppermute | solution.py:211
  3.6 13.7 %collective-permute-start.1 = (bf16[8,32,64]{2,1,0:T(8,128)(2,1)}, bf16[8,32,64]{2,1,0:T(8,128)(2,1)S(1)}, u32[]{:S(2)}, u32[]{:S(2)}) collective-permute-start(bf16[8,32,64]{2,1,0:T(8,128)(2,1)} %refs_2_.1), channel_id=1, source_target_pairs={{0,1},{1,0},{2,3},{3,2},{4,5},{5,4},{6,7},{7,6},{8,9},{9,8},{10,11... | collective-permute-start | bytes 98312 | tf_op jit(solution)/shard_map/ppermute | solution.py:212
  17.4 1.0 copy-start.4
  18.4 0.8 copy-start.5
  19.3 0.7 copy-start.8
  21.6 34.4 %copy-start.1 = (bf16[128,8192]{1,0:T(8,128)(2,1)S(1)}, bf16[128,8192]{1,0:T(8,128)(2,1)}, u32[]{:S(2)}) copy-start(bf16[128,8192]{1,0:T(8,128)(2,1)} %x.1) | copy-start | bytes 6291460
  21.6 34.4 %copy-start.2 = (bf16[128,512]{1,0:T(8,128)(2,1)S(1)}, bf16[128,512]{1,0:T(8,128)(2,1)}, u32[]{:S(2)}) copy-start(bf16[128,512]{1,0:T(8,128)(2,1)} %refs_0_.1) | copy-start | bytes 393220
  57.4 1.0 copy-start.3
  58.4 0.6 copy-start.6
  59.0 27.7 %all-to-all-start.2 = ((bf16[16,272,128]{2,1,0:T(8,128)(2,1)}), bf16[16,272,128]{2,1,0:T(8,128)(2,1)S(1)}, u32[]{:S(2)}, u32[]{:S(2)}) async-start(bf16[16,272,128]{2,1,0:T(8,128)(2,1)} %copy-done.3), calls=%async_computation.2 | async-start | bytes 2228224 | tf_op jit(solution)/shard_map/all_to_all | solution.py:277
  62.7 24.0 %copy-start.9 = (s32[16]{0:T(128)S(1)}, s32[16]{0:T(128)}, u32[]{:S(2)}) copy-start(s32[16]{0:T(128)} %table.5) | copy-start | bytes 196
  62.7 5.8 %collective-permute-start.2 = (bf16[128,512]{1,0:T(8,128)(2,1)S(1)}, bf16[128,512]{1,0:T(8,128)(2,1)S(1)}, u32[]{:S(2)}, u32[]{:S(2)}) collective-permute-start(bf16[128,512]{1,0:T(8,128)(2,1)S(1)} %copy-done.2), channel_id=1, source_target_pairs={{0,1},{1,0},{2,3},{3,2},{4,5},{5,4},{6,7},{7,6},{8,9},{9,8},{10,11... | collective-permute-start | bytes 393224 | tf_op jit(solution)/shard_map/ppermute | solution.py:226
  68.5 12.9 %collective-permute-start.3 = (bf16[256,512]{1,0:T(8,128)(2,1)S(1)}, bf16[256,512]{1,0:T(8,128)(2,1)S(1)}, u32[]{:S(2)}, u32[]{:S(2)}) collective-permute-start(bf16[256,512]{1,0:T(8,128)(2,1)S(1)} %pad_maximum_fusion.1), channel_id=1, source_target_pairs={{0,4},{2,6},{4,0},{6,2},{8,12},{10,14},{12,8},{14,10},{16,20},{18,... | collective-permute-start | bytes 786440 | tf_op jit(solution)/shard_map/ppermute | solution.py:233
  82.2 31.0 %collective-permute-start.4 = (bf16[512,512]{1,0:T(8,128)(2,1)}, bf16[512,512]{1,0:T(8,128)(2,1)}, u32[]{:S(2)}, u32[]{:S(2)}) collective-permute-start(bf16[512,512]{1,0:T(8,128)(2,1)} %pad_maximum_fusion), channel_id=1, source_target_pairs={{0,2},{2,0},{4,6},{6,4},{8,10},{10,8},{12,14},{14,12},{16,18},{18,... | collective-permute-start | bytes 1572872 | tf_op jit(solution)/shard_map/ppermute | solution.py:233
  82.3 11.3 %collective-permute-start.7 = (bf16[256,512]{1,0:T(8,128)(2,1)S(1)}, bf16[256,512]{1,0:T(8,128)(2,1)}, u32[]{:S(2)}, u32[]{:S(2)}) collective-permute-start(bf16[256,512]{1,0:T(8,128)(2,1)S(1)} %constant_dynamic-slice_fusion.refs_4_), channel_id=1, source_target_pairs={{0,24},{2,26},{4,28},{6,30},{8,16},{10,18},{12,20},{14,22},{16,8},... | collective-permute-start | bytes 786440 | tf_op jit(solution)/shard_map/ppermute | solution.py:219
  86.1 27.2 %collective-permute-start.6 = (bf16[256,512]{1,0:T(8,128)(2,1)S(1)}, bf16[256,512]{1,0:T(8,128)(2,1)}, u32[]{:S(2)}, u32[]{:S(2)}) collective-permute-start(bf16[256,512]{1,0:T(8,128)(2,1)S(1)} %constant_dynamic-slice_fusion.refs_4_), channel_id=1, source_target_pairs={{0,16},{2,18},{4,20},{6,22},{8,24},{10,26},{12,28},{14,30},{16,0},... | collective-permute-start | bytes 786440 | tf_op jit(solution)/shard_map/ppermute | solution.py:219
  86.1 27.2 %collective-permute-start.5 = (bf16[256,512]{1,0:T(8,128)(2,1)S(1)}, bf16[256,512]{1,0:T(8,128)(2,1)}, u32[]{:S(2)}, u32[]{:S(2)}) collective-permute-start(bf16[256,512]{1,0:T(8,128)(2,1)S(1)} %constant_dynamic-slice_fusion.refs_4_), channel_id=1, source_target_pairs={{0,8},{2,10},{4,12},{6,14},{8,0},{10,2},{12,4},{14,6},{16,24},{18,... | collective-permute-start | bytes 786440 | tf_op jit(solution)/shard_map/ppermute | solution.py:219
  87.7 56.7 %copy-start.7 = (bf16[128,64]{1,0:T(8,128)(2,1)S(1)}, bf16[128,64]{1,0:T(8,128)(2,1)}, u32[]{:S(2)}) copy-start(bf16[128,64]{1,0:T(8,128)(2,1)} %copy-done.6) | copy-start | bytes 49156
  87.7 58.8 %collective-permute-start.15 = (bf16[8,272,128]{2,1,0:T(8,128)(2,1)S(1)}, bf16[8,272,128]{2,1,0:T(8,128)(2,1)S(1)}, u32[]{:S(2)}, u32[]{:S(2)}) collective-permute-start(bf16[8,272,128]{2,1,0:T(8,128)(2,1)S(1)} %sort.1), channel_id=1, source_target_pairs={{0,1},{1,0},{2,3},{3,2},{4,5},{5,4},{6,7},{7,6},{8,9},{9,8},{10,11... | collective-permute-start | bytes 1671176 | tf_op jit(solution)/shard_map/ppermute | solution.py:299
  117.3 9.3 %collective-permute-start.8 = (bf16[128,1024]{1,0:T(8,128)(2,1)S(1)}, bf16[128,1024]{1,0:T(8,128)(2,1)S(1)}, u32[]{:S(2)}, u32[]{:S(2)}) collective-permute-start(bf16[128,1024]{1,0:T(8,128)(2,1)S(1)} %get-tuple-element.17), channel_id=1, source_target_pairs={{0,1},{1,0},{2,3},{3,2},{4,5},{5,4},{6,7},{7,6},{8,9},{9,8},{10,11... | collective-permute-start | bytes 786440 | tf_op jit(solution)/shard_map/ppermute | solution.py:251
  118.9 12.2 %collective-permute-start.9 = (bf16[128,1024]{1,0:T(8,128)(2,1)S(1)}, bf16[128,1024]{1,0:T(8,128)(2,1)S(1)}, u32[]{:S(2)}, u32[]{:S(2)}) collective-permute-start(bf16[128,1024]{1,0:T(8,128)(2,1)S(1)} %get-tuple-element.18), channel_id=1, source_target_pairs={{0,4},{1,5},{2,6},{3,7},{4,0},{5,1},{6,2},{7,3},{8,12},{9,13},{10,... | collective-permute-start | bytes 786440 | tf_op jit(solution)/shard_map/ppermute | solution.py:251
  120.4 12.7 %collective-permute-start.10 = (bf16[128,1024]{1,0:T(8,128)(2,1)S(1)}, bf16[128,1024]{1,0:T(8,128)(2,1)S(1)}, u32[]{:S(2)}, u32[]{:S(2)}) collective-permute-start(bf16[128,1024]{1,0:T(8,128)(2,1)S(1)} %get-tuple-element.19), channel_id=1, source_target_pairs={{0,5},{1,4},{2,7},{3,6},{4,1},{5,0},{6,3},{7,2},{8,13},{9,12},{10,... | collective-permute-start | bytes 786440 | tf_op jit(solution)/shard_map/ppermute | solution.py:251
  120.9 12.2 %collective-permute-start.11 = (bf16[128,1024]{1,0:T(8,128)(2,1)S(1)}, bf16[128,1024]{1,0:T(8,128)(2,1)S(1)}, u32[]{:S(2)}, u32[]{:S(2)}) collective-permute-start(bf16[128,1024]{1,0:T(8,128)(2,1)S(1)} %get-tuple-element.20), channel_id=1, source_target_pairs={{0,2},{1,3},{2,0},{3,1},{4,6},{5,7},{6,4},{7,5},{8,10},{9,11},{10,... | collective-permute-start | bytes 786440 | tf_op jit(solution)/shard_map/ppermute | solution.py:251
  126.6 9.3 %collective-permute-start.12 = (bf16[128,1024]{1,0:T(8,128)(2,1)S(1)}, bf16[128,1024]{1,0:T(8,128)(2,1)S(1)}, u32[]{:S(2)}, u32[]{:S(2)}) collective-permute-start(bf16[128,1024]{1,0:T(8,128)(2,1)S(1)} %get-tuple-element.21), channel_id=1, source_target_pairs={{0,3},{1,2},{2,1},{3,0},{4,7},{5,6},{6,5},{7,4},{8,11},{9,10},{10,... | collective-permute-start | bytes 786440 | tf_op jit(solution)/shard_map/ppermute | solution.py:251
  131.1 13.3 %collective-permute-start.13 = (bf16[128,1024]{1,0:T(8,128)(2,1)S(1)}, bf16[128,1024]{1,0:T(8,128)(2,1)S(1)}, u32[]{:S(2)}, u32[]{:S(2)}) collective-permute-start(bf16[128,1024]{1,0:T(8,128)(2,1)S(1)} %get-tuple-element.22), channel_id=1, source_target_pairs={{0,6},{1,7},{2,4},{3,5},{4,2},{5,3},{6,0},{7,1},{8,14},{9,15},{10,... | collective-permute-start | bytes 786440 | tf_op jit(solution)/shard_map/ppermute | solution.py:251
  133.0 11.4 %collective-permute-start.14 = (bf16[128,1024]{1,0:T(8,128)(2,1)S(1)}, bf16[128,1024]{1,0:T(8,128)(2,1)S(1)}, u32[]{:S(2)}, u32[]{:S(2)}) collective-permute-start(bf16[128,1024]{1,0:T(8,128)(2,1)S(1)} %get-tuple-element.23), channel_id=1, source_target_pairs={{0,7},{1,6},{2,5},{3,4},{4,3},{5,2},{6,1},{7,0},{8,15},{9,14},{10,... | collective-permute-start | bytes 786440 | tf_op jit(solution)/shard_map/ppermute | solution.py:251

commit v2 on v1

--- a/solution.py
+++ b/solution.py
@@ -1,4 +1,5 @@
 import functools
+import math
 
 import jax
 import jax.numpy as jnp
@@ -9,6 +10,7 @@
 
 adapter_scale_factor = 2.0
 lanes = 128
+base_weight = 12
 BF16, F32 = jnp.bfloat16, jnp.float32
 NT = (((1,), (1,)), ((), ()))
 TN = (((0,), (0,)), ((), ()))
@@ -129,8 +131,8 @@
     h = hidden[...]
     for (i_rel, d_rel), piece in zip(rels, pieces):
         d = d_here ^ d_rel
-        for k in range(layers):
-            f = f_here ^ (k * inner_count + i_rel)
+        for k in range(2 * layers):
+            f = f_here ^ (k % layers * inner_count + k // layers + i_rel)
             adapter = wide(got, f, d * tiles, tiles, rank)
             low = adapter_scale_factor * dot(h, adapter, NN)
             start = pl.multiple_of(f * rows + d * cols, lanes)
@@ -182,6 +184,20 @@
 
 def smem(count):
     return [pl.BlockSpec(memory_space=pltpu.SMEM)] * count
+
+
+def bits(count):
+    return [1 << n for n in range(count.bit_length() - 1)]
+
+
+def axis_count(axis):
+    names = (axis,) if isinstance(axis, str) else axis
+    return math.prod(lax.axis_size(name) for name in names)
+
+
+def exchange(name, array, axis, bits):
+    with jax.named_scope(name):
+        return lax.ppermute(array, axis, xor_pairs(axis_count(axis), bits))
 
 
 def xor_pairs(count, bits):
@@ -208,49 +224,26 @@
     down_t = adapter_down.transpose(0, 2, 1)
     downs, ups = [down_t], [adapter_up]
     for j in range(1, dp_count):
-        downs.append(lax.ppermute(down_t, "dp", xor_pairs(dp_count, j)))
-        ups.append(lax.ppermute(adapter_up, "dp", xor_pairs(dp_count, j)))
-    ids = lax.all_to_all(
-        jnp.broadcast_to(tenant_ids[:, None], (fsdp_count, 1)), "fsdp", 0, 0, tiled=True
-    ).reshape(-1)
+        downs.append(exchange("down_dp", down_t, "dp", j))
+        ups.append(exchange("up_dp", adapter_up, "dp", j))
+    with jax.named_scope("ids"):
+        ids = lax.all_to_all(
+            jnp.broadcast_to(tenant_ids[:, None, None], (fsdp_count, 1, lanes)), "fsdp", 0, 0, tiled=True
+        )[:, 0, 0]
 
     w_here = lax.dynamic_slice_in_dim(w_value, lax.axis_index("dp") % split * cols, cols, 0)
-    ws = [w_here] + [
-        lax.ppermute(w_here, "fsdp", xor_pairs(fsdp_count, k * inner_count))
-        for k in range(1, layers)
-    ]
-    gs, g_counts, rels = [grad_value], [1], [(0, 0)]
-    held = grad_value
-    bit = 1
-    while bit < split:
-        new = lax.ppermute(held, "dp", xor_pairs(dp_count, bit))
+    ws = [w_here] + [None] * (layers - 1)
+    for bit in bits(layers):
+        ws[bit] = exchange("w_layers", w_here, "fsdp", bit * inner_count)
+    gs, g_counts, rels, held = [grad_value], [1], [(0, 0)], grad_value
+    stages = [("fsdp", bit) for bit in bits(inner_count)[1:]] + [("dp", bit) for bit in bits(split)]
+    for n, (axis, bit) in enumerate(stages):
+        new = exchange("g_" + axis, held, axis, bit)
         gs, g_counts = gs + [new], g_counts + [len(rels)]
-        rels = rels + [(i, d | bit) for i, d in rels]
-        held = jnp.concatenate([held, new], axis=0)
-        bit *= 2
-    bit = inner_count // 2
-    while bit >= 1:
-        new = lax.ppermute(held, "fsdp", xor_pairs(fsdp_count, bit))
-        gs, g_counts = gs + [new], g_counts + [len(rels)]
-        rels = rels + [(i | bit, d) for i, d in rels]
-        bit //= 2
-        if bit >= 1:
+        rels = rels + [(i | bit, d) if axis == "fsdp" else (i, d | bit) for i, d in rels]
+        if n + 1 < len(stages):
             held = jnp.concatenate([held, new], axis=0)
-    piece = jax.ShapeDtypeStruct((tokens, layers * cols), BF16)
-    pieces = pl.pallas_call(
-        functools.partial(base_kernel, g_counts, layers),
-        out_shape=[piece] * len(rels),
-        in_specs=vmem(len(gs) + layers),
-        out_specs=vmem(len(rels)),
-        compiler_params=params(),
-        cost_estimate=cost(2 * tokens * width * kv_width, 4 * tokens * width),
-        name="base",
-    )(*gs, *ws)
-    total = fsdp_count * dp_count
-    pieces = [pieces[0]] + [
-        lax.ppermute(p, ("fsdp", "dp"), xor_pairs(total, i * dp_count + d))
-        for (i, d), p in zip(rels[1:], pieces[1:])
-    ]
+    ids, downs, ups, gs, ws = lax.optimization_barrier((ids, downs, ups, gs, ws))
 
     box = jax.ShapeDtypeStruct((fsdp_count, tall, lanes), BF16)
     box_bytes = 2 * fsdp_count * tall * lanes
@@ -263,7 +256,30 @@
         cost_estimate=cost(0, 2 * box_bytes),
         name="select",
     )(ids, slot_table, *downs, *ups)
-    got = lax.all_to_all(sent, "fsdp", 0, 0, tiled=True)
+    with jax.named_scope("adapters_to_blocks"):
+        got = lax.all_to_all(sent, "fsdp", 0, 0, tiled=True)
+    for bit in reversed(bits(layers)):
+        for k in range(0, layers, 2 * bit):
+            if ws[k + bit] is None:
+                ws[k + bit] = exchange("w_last", ws[k], "fsdp", bit * inner_count)
+    ws = ws + [exchange("w_core", w, "fsdp", 1) for w in ws]
+
+    pieces = pl.pallas_call(
+        functools.partial(base_kernel, g_counts, len(ws)),
+        out_shape=[jax.ShapeDtypeStruct((tokens, len(ws) * cols), BF16)] * len(rels),
+        in_specs=vmem(len(gs) + len(ws)),
+        out_specs=vmem(len(rels)),
+        compiler_params=params(),
+        cost_estimate=cost(
+            base_weight * 2 * tokens * width * kv_width, base_weight * 4 * tokens * width
+        ),
+        name="base",
+    )(*gs, *ws)
+    pieces = [pieces[0]] + [
+        exchange("pieces%d%d" % (i, d), p, ("fsdp", "dp"), i * dp_count + d)
+        for (i, d), p in zip(rels[1:], pieces[1:])
+    ]
+    got, pieces[:-1] = lax.optimization_barrier((got, pieces[:-1]))
 
     hidden, back = pl.pallas_call(
         functools.partial(middle_kernel, kv_rows, rank),
@@ -274,7 +290,9 @@
         cost_estimate=cost(4 * tokens * width * rank, 2 * tokens * width + 2 * box_bytes),
         name="middle",
     )(inputs, grad_value, got)
-    returned = lax.all_to_all(back, "fsdp", 0, 0, tiled=True)
+    with jax.named_scope("gradients_back"):
+        returned = lax.all_to_all(back, "fsdp", 0, 0, tiled=True)
+    returned, pieces = lax.optimization_barrier((returned, pieces))
 
     input_gradient_rows = pl.pallas_call(
         functools.partial(out_kernel, rels, layers, inner_count, split, rows, rank),
@@ -296,8 +314,9 @@
         name="sort",
     )(ids, slot_table, returned)
     received = [
-        lax.ppermute(s, "dp", xor_pairs(dp_count, j + 1)) for j, s in enumerate(sends)
+        exchange("grads_dp", s, "dp", j + 1) for j, s in enumerate(sends)
     ]
+    received, input_gradient_rows = lax.optimization_barrier((received, input_gradient_rows))
     grad_down_t, grad_up = pl.pallas_call(
         functools.partial(sum_kernel, dp_count, kv_rows),
         out_shape=[

time: 149 us -> 115 us (0.77)
  blocking collectives: 47 us -> 0 us
  starting transfers between devices: 19.7 us -> 35.9 us
  waiting for transfers between devices: 62.9 us -> 55.6 us
  local copies, waits for them, and re-layouts: 4.19 us -> 7.85 us
    all_to_all x2 -> x0, blocking collectives: 47 us -> none  [the longest x1 34.4 us: on_device(): got = lax.all_to_all(sent, 'fsdp', 0, 0, tiled=True)]
    ppermute x16 -> x15, waiting for transfers between devices: 62.9 us -> 48.1 us  [exchange(): return lax.ppermute(array, axis, xor_pairs(axis_count(axis), bits))]
    all_to_all x0 -> x2, starting transfers between devices: none -> 10.2 us  [the longest x1 5.34 us: on_device(): lax.all_to_all(jnp.broadcast_to(tenant_ids[:, None, None], (fsdp_count, 1...]
    all_to_all x0 -> x2, waiting for transfers between devices: none -> 4.77 us  [the longest x1 4.76 us: on_device(): lax.all_to_all(jnp.broadcast_to(tenant_ids[:, None, None], (fsdp_count, 1...]
    ppermute x16 -> x15, starting transfers between devices: 16 us -> 20.4 us  [exchange(): return lax.ppermute(array, axis, xor_pairs(axis_count(axis), bits))]
    all_to_all x1, waiting for transfers between devices: 0.01 us -> 2.79 us  [on_device(): returned = lax.all_to_all(back, 'fsdp', 0, 0, tiled=True)]
    unnamed x20 -> x36, local copies, waits for them, and re-layouts: 4.16 us -> 6.85 us
    all_to_all x1, starting transfers between devices: 3.7 us -> 5.31 us  [on_device(): returned = lax.all_to_all(back, 'fsdp', 0, 0, tiled=True)]
  transfers between devices with their start and end apart: 17 -> 18, of which waited for: 9 -> 8; matrix products, arithmetic and copies ran while one was open for 1% -> 2% of each run, Pallas kernels for 5% -> 7%
where the time goes in v2:
time: 115 us; the launch traced here: 114 us
  waiting for transfers between devices  55.6 us (48%)
  starting transfers between devices  35.9 us (31%)
  Pallas kernels  12 us (10%)
  local copies, waits for them, and re-layouts  7.85 us (7%)
  between operations  1.48 us (1%)
    ppermute x15, waiting for transfers between devices, exchange(): return lax.ppermute(array, axis, xor_pairs(axis_count(axis), bits))  48.1 us
    ppermute x15, starting transfers between devices, exchange(): return lax.ppermute(array, axis, xor_pairs(axis_count(axis), bits))  20.4 us
    unnamed x36, local copies, waits for them, and re-layouts  6.85 us
    all_to_all x1, starting transfers between devices, on_device(): lax.all_to_all(jnp.broadcast_to(tenant_ids[:, None, None], (fsdp_count, 1...  5.34 us
    all_to_all x1, starting transfers between devices, on_device(): returned = lax.all_to_all(back, 'fsdp', 0, 0, tiled=True)  5.31 us
    all_to_all x1, starting transfers between devices, on_device(): got = lax.all_to_all(sent, 'fsdp', 0, 0, tiled=True)  4.89 us
    all_to_all x1, waiting for transfers between devices, on_device(): lax.all_to_all(jnp.broadcast_to(tenant_ids[:, None, None], (fsdp_count, 1...  4.76 us
    pallas_call x1, Pallas kernels, on_device(): pl.pallas_call(functools.partial(base_kernel, g_counts, len(ws)), out_sha...  2.79 us
  transfers between devices with their start and end apart: 18, of which 8 were waited for; matrix products, arithmetic and copies ran while one was open for 2% of the time, Pallas kernels for 7%

profile of v2, /device:TPU:0, one launch (start us, length us, event | category | flops | bytes accessed | tf_op | source)
XLA Modules:
  0.0 113.7 jit_solution(13859466806282304006)
XLA Ops:
  0.6 0.0 copy-start
  0.7 3.0 %collective-permute-start = (bf16[8,64,512]{2,1,0:T(8,128)(2,1)}, bf16[8,64,512]{2,1,0:T(8,128)(2,1)S(1)}, u32[]{:S(2)}, u32[]{:S(2)}) collective-permute-start(bf16[8,64,512]{2,1,0:T(8,128)(2,1)} %bitcast.4), channel_id=1, source_target_pairs={{0,1},{1,0},{2,3},{3,2},{4,5},{5,4},{6,7},{7,6},{8,9},{9,8},{10,11... | collective-permute-start | bytes 1572872 | tf_op jit(solution)/shard_map/down_dp/ppermute | solution.py:200
  3.7 1.5 %collective-permute-start.2 = (bf16[128,512]{1,0:T(8,128)(2,1)}, bf16[128,512]{1,0:T(8,128)(2,1)S(1)}, u32[]{:S(2)}, u32[]{:S(2)}) collective-permute-start(bf16[128,512]{1,0:T(8,128)(2,1)} %g.1), channel_id=1, source_target_pairs={{0,4},{2,6},{4,0},{6,2},{8,12},{10,14},{12,8},{14,10},{16,20},{18,... | collective-permute-start | bytes 393224 | tf_op jit(solution)/shard_map/g_fsdp/ppermute | solution.py:200
  5.2 2.7 %collective-permute-start.5 = (bf16[256,512]{1,0:T(8,128)(2,1)S(1)}, bf16[256,512]{1,0:T(8,128)(2,1)S(1)}, u32[]{:S(2)}, u32[]{:S(2)}) collective-permute-start(bf16[256,512]{1,0:T(8,128)(2,1)S(1)} %constant_dynamic-slice_fusion.refs_3_), channel_id=1, source_target_pairs={{0,16},{2,18},{4,20},{6,22},{8,24},{10,26},{12,28},{14,30},{16,0},... | collective-permute-start | bytes 786440 | tf_op jit(solution)/shard_map/w_layers/ppermute | solution.py:200
  7.9 1.6 %collective-permute-start.4 = (bf16[256,512]{1,0:T(8,128)(2,1)S(1)}, bf16[256,512]{1,0:T(8,128)(2,1)S(1)}, u32[]{:S(2)}, u32[]{:S(2)}) collective-permute-start(bf16[256,512]{1,0:T(8,128)(2,1)S(1)} %constant_dynamic-slice_fusion.refs_3_), channel_id=1, source_target_pairs={{0,8},{2,10},{4,12},{6,14},{8,0},{10,2},{12,4},{14,6},{16,24},{18,... | collective-permute-start | bytes 786440 | tf_op jit(solution)/shard_map/w_layers/ppermute | solution.py:200
  9.5 0.0 collective-permute-done.2.refs_1_
  9.5 0.9 pad_maximum_fusion
  10.4 0.6 collective-permute-start.3
  11.6 0.6 broadcast_in_dim.9
  12.2 5.3 %all-to-all-start = ((s32[16,1,128]{2,1,0:T(1,128)}), s32[16,1,128]{2,1,0:T(1,128)S(1)}, u32[]{:S(2)}, u32[]{:S(2)}) async-start(s32[16,1,128]{2,1,0:T(1,128)} %broadcast_in_dim.9), calls=%async_computation | async-start | bytes 16384 | tf_op jit(solution)/shard_map/ids/all_to_all | solution.py:230
  17.6 1.6 %collective-permute-start.1 = (bf16[8,32,64]{2,1,0:T(8,128)(2,1)S(1)}, bf16[8,32,64]{2,1,0:T(8,128)(2,1)S(1)}, u32[]{:S(2)}, u32[]{:S(2)}) collective-permute-start(bf16[8,32,64]{2,1,0:T(8,128)(2,1)S(1)} %copy-done.11), channel_id=1, source_target_pairs={{0,1},{1,0},{2,3},{3,2},{4,5},{5,4},{6,7},{7,6},{8,9},{9,8},{10,11... | collective-permute-start | bytes 98312 | tf_op jit(solution)/shard_map/up_dp/ppermute | solution.py:200
  19.2 4.8 %all-to-all-done = s32[16,1,128]{2,1,0:T(1,128)S(1)} async-done(((s32[16,1,128]{2,1,0:T(1,128)}), s32[16,1,128]{2,1,0:T(1,128)S(1)}, u32[]{:S(2)}, u32[]{:S(2)}) %all-to-all-start) | async-done | bytes 8224 | tf_op jit(solution)/shard_map/ids/all_to_all | solution.py:230
  23.9 0.4 slice_reduce_fusion.ids
  24.3 0.0 collective-permute-done.3.refs_2_
  24.3 0.0 copy-start.14
  24.4 0.6 collective-permute-start.6
  24.9 2.7 %select.3 = bf16[16,272,128]{2,1,0:T(8,128)(2,1)} custom-call(s32[16]{0:T(128)S(1)} %slice_reduce_fusion.ids, s32[16]{0:T(128)S(1)} %copy-done.12, bf16[8,64,512]{2,1,0:T(8,128)(2,1)S(1)} %bitcast.5, bf16[8,64,512]{2,1,0:T(8,128)(2,1)S(1)} %collective-permute-done.refs_1_, bf16[8,32,64]{2,1,0:T(8,128)(2,1)S(1)} %copy-done.11, ...), custom_call_target="tpu_custom_call" | custom-call | bytes 2228224 | tf_op jit(solution)/shard_map/select/pallas_call | solution.py:250
  27.6 4.9 %all-to-all-start.1 = ((bf16[16,272,128]{2,1,0:T(8,128)(2,1)}), bf16[16,272,128]{2,1,0:T(8,128)(2,1)S(1)}, u32[]{:S(2)}, u32[]{:S(2)}) async-start(bf16[16,272,128]{2,1,0:T(8,128)(2,1)} %select.3), calls=%async_computation.1 | async-start | bytes 2228224 | tf_op jit(solution)/shard_map/adapters_to_blocks/all_to_all | solution.py:260
  32.5 0.4 collective-permute-start.9
  32.9 0.2 collective-permute-start.7
  33.1 0.3 collective-permute-start.8
  33.5 0.0 collective-permute-done.6.refs_6_
  33.5 0.2 collective-permute-start.10
  33.6 0.7 copy-done.16
  34.3 0.2 collective-permute-done.7.refs_7_
  34.5 0.4 collective-permute-done.8.refs_8_
  34.9 0.4 collective-permute-done.10.refs_10_
  35.3 0.9 copy-done.15
  36.2 0.9 copy-done.17
  37.2 2.8 %base.1 = (bf16[128,2048]{1,0:T(8,128)(2,1)S(1)}, bf16[128,2048]{1,0:T(8,128)(2,1)S(1)}, bf16[128,2048]{1,0:T(8,128)(2,1)S(1)}, bf16[128,2048]{1,0:T(8,128)(2,1)S(1)}) custom-call(bf16[128,512]{1,0:T(8,128)(2,1)S(1)} %copy-done.3, bf16[128,512]{1,0:T(8,128)(2,1)S(1)} %collective-permute-done.2.refs_1_, bf16[256,512]{1,0:T(8,128)(2,1)S(1)} %copy-done.15, ...), custom_call_target="tpu_custom_call" | custom-call | flops 12884901888 | bytes 50331648 | tf_op jit(solution)/shard_map/base/pallas_call | solution.py:267
  40.0 1.9 %collective-permute-start.11 = (bf16[128,2048]{1,0:T(8,128)(2,1)S(1)}, bf16[128,2048]{1,0:T(8,128)(2,1)S(1)}, u32[]{:S(2)}, u32[]{:S(2)}) collective-permute-start(bf16[128,2048]{1,0:T(8,128)(2,1)S(1)} %get-tuple-element.45), channel_id=1, source_target_pairs={{0,4},{1,5},{2,6},{3,7},{4,0},{5,1},{6,2},{7,3},{8,12},{9,13},{10,... | collective-permute-start | bytes 1572872 | tf_op jit(solution)/shard_map/pieces20/ppermute | solution.py:200
  41.9 1.5 %collective-permute-start.12 = (bf16[128,2048]{1,0:T(8,128)(2,1)S(1)}, bf16[128,2048]{1,0:T(8,128)(2,1)S(1)}, u32[]{:S(2)}, u32[]{:S(2)}) collective-permute-start(bf16[128,2048]{1,0:T(8,128)(2,1)S(1)} %get-tuple-element.46), channel_id=1, source_target_pairs={{0,1},{1,0},{2,3},{3,2},{4,5},{5,4},{6,7},{7,6},{8,9},{9,8},{10,11... | collective-permute-start | bytes 1572872 | tf_op jit(solution)/shard_map/pieces01/ppermute | solution.py:200
  43.4 16.5 %collective-permute-done.11.refs_1_ = bf16[128,2048]{1,0:T(8,128)(2,1)S(1)} collective-permute-done((bf16[128,2048]{1,0:T(8,128)(2,1)S(1)}, bf16[128,2048]{1,0:T(8,128)(2,1)S(1)}, u32[]{:S(2)}, u32[]{:S(2)}) %collective-permute-start.11) | collective-permute-done | bytes 524320 | tf_op jit(solution)/shard_map/pieces20/ppermute | solution.py:200
  59.9 0.8 copy-done.7
  60.7 1.6 %copy-done.1 = bf16[128,8192]{1,0:T(8,128)(2,1)S(1)} copy-done((bf16[128,8192]{1,0:T(8,128)(2,1)S(1)}, bf16[128,8192]{1,0:T(8,128)(2,1)}, u32[]{:S(2)}) %copy-start.1) | copy-done | bytes 2097176
  62.3 1.3 %middle.1 = (bf16[128,64]{1,0:T(8,128)(2,1)S(1)}, bf16[16,272,128]{2,1,0:T(8,128)(2,1)S(1)}) custom-call(bf16[128,8192]{1,0:T(8,128)(2,1)S(1)} %copy-done.1, bf16[128,512]{1,0:T(8,128)(2,1)S(1)} %copy-done.3, bf16[16,272,128]{2,1,0:T(8,128)(2,1)S(1)} %all-to-all-done.1.got), custom_call_target="tpu_custom_call" | custom-call | flops 268435456 | bytes 4325376 | tf_op jit(solution)/shard_map/middle/pallas_call | solution.py:284
  63.6 0.0 copy-start.2
  63.6 1.0 copy-done.2
  64.6 5.3 %all-to-all-start.2 = ((bf16[16,272,128]{2,1,0:T(8,128)(2,1)}), bf16[16,272,128]{2,1,0:T(8,128)(2,1)S(1)}, u32[]{:S(2)}, u32[]{:S(2)}) async-start(bf16[16,272,128]{2,1,0:T(8,128)(2,1)} %copy-done.2), calls=%async_computation.2 | async-start | bytes 2228224 | tf_op jit(solution)/shard_map/gradients_back/all_to_all | solution.py:294
  69.9 2.9 %collective-permute-start.13 = (bf16[128,2048]{1,0:T(8,128)(2,1)}, bf16[128,2048]{1,0:T(8,128)(2,1)S(1)}, u32[]{:S(2)}, u32[]{:S(2)}) collective-permute-start(bf16[128,2048]{1,0:T(8,128)(2,1)} %copy-done.13), channel_id=1, source_target_pairs={{0,5},{1,4},{2,7},{3,6},{4,1},{5,0},{6,3},{7,2},{8,13},{9,12},{10,... | collective-permute-start | bytes 1572872 | tf_op jit(solution)/shard_map/pieces21/ppermute | solution.py:200
  72.8 19.2 %collective-permute-done.13.refs_3_ = bf16[128,2048]{1,0:T(8,128)(2,1)S(1)} collective-permute-done((bf16[128,2048]{1,0:T(8,128)(2,1)}, bf16[128,2048]{1,0:T(8,128)(2,1)S(1)}, u32[]{:S(2)}, u32[]{:S(2)}) %collective-permute-start.13) | collective-permute-done | bytes 524320 | tf_op jit(solution)/shard_map/pieces21/ppermute | solution.py:200
  92.0 0.8 copy-done.9
  92.8 2.8 %all-to-all-done.2.got = bf16[16,272,128]{2,1,0:T(8,128)(2,1)S(1)} async-done(((bf16[16,272,128]{2,1,0:T(8,128)(2,1)}), bf16[16,272,128]{2,1,0:T(8,128)(2,1)S(1)}, u32[]{:S(2)}, u32[]{:S(2)}) %all-to-all-start.2) | async-done | bytes 1114144 | tf_op jit(solution)/shard_map/gradients_back/all_to_all | solution.py:294
  95.6 1.0 sort.1
  96.6 1.6 %collective-permute-start.14 = (bf16[8,272,128]{2,1,0:T(8,128)(2,1)S(1)}, bf16[8,272,128]{2,1,0:T(8,128)(2,1)S(1)}, u32[]{:S(2)}, u32[]{:S(2)}) collective-permute-start(bf16[8,272,128]{2,1,0:T(8,128)(2,1)S(1)} %sort.1), channel_id=1, source_target_pairs={{0,1},{1,0},{2,3},{3,2},{4,5},{5,4},{6,7},{7,6},{8,9},{9,8},{10,11... | collective-permute-start | bytes 1671176 | tf_op jit(solution)/shard_map/grads_dp/ppermute | solution.py:200
  98.1 2.1 %rows.1 = bf16[128,8192]{1,0:T(8,128)(2,1)} custom-call(bf16[128,64]{1,0:T(8,128)(2,1)S(1)} %get-tuple-element.54.hidden, bf16[16,272,128]{2,1,0:T(8,128)(2,1)S(1)} %all-to-all-done.1.got, bf16[128,2048]{1,0:T(8,128)(2,1)S(1)} %get-tuple-element.55.refs_0_, bf16[128,2048]{1,0:T(8,128)(2,1)S(1)} %copy-done.6, bf16[128,2048]{1,0:T(8,128)(2,1)S(1)} %copy-done.8, ...), custom_call_target="tpu_custom_call" | custom-call | flops 134217728 | bytes 5308416 | tf_op jit(solution)/shard_map/rows/pallas_call | solution.py:297
  100.2 11.4 %collective-permute-done.14.refs_0_ = bf16[8,272,128]{2,1,0:T(8,128)(2,1)S(1)} collective-permute-done((bf16[8,272,128]{2,1,0:T(8,128)(2,1)S(1)}, bf16[8,272,128]{2,1,0:T(8,128)(2,1)S(1)}, u32[]{:S(2)}, u32[]{:S(2)}) %collective-permute-start.14) | collective-permute-done | bytes 557088 | tf_op jit(solution)/shard_map/grads_dp/ppermute | solution.py:200
  111.6 2.1 %sums.1 = (bf16[8,64,512]{2,1,0:T(8,128)(2,1)}, bf16[8,32,64]{2,1,0:T(8,128)(2,1)}) custom-call(s32[16]{0:T(128)S(1)} %slice_reduce_fusion.ids, s32[16]{0:T(128)S(1)} %copy-done.12, bf16[16,272,128]{2,1,0:T(8,128)(2,1)S(1)} %all-to-all-done.2.got, bf16[8,272,128]{2,1,0:T(8,128)(2,1)S(1)} %collective-permute-done.14.refs_0_), custom_call_target="tpu_custom_call" | custom-call | bytes 2228224 | tf_op jit(solution)/shard_map/sums/pallas_call | solution.py:320
  (34 shorter events, 0.1 us)
Async XLA Ops:
  0.6 4.6 %copy-start = (bf16[512,512]{1,0:T(8,128)(2,1)S(1)}, bf16[512,512]{1,0:T(8,128)(2,1)}, u32[]{:S(2)}) copy-start(bf16[512,512]{1,0:T(8,128)(2,1)} %param.9) | copy-start | bytes 1572868
  0.6 24.3 %copy-start.4 = (bf16[8,512,64]{1,2,0:T(8,128)(2,1)S(1)}, bf16[8,512,64]{1,2,0:T(8,128)(2,1)}, u32[]{:S(2)}) copy-start(bf16[8,512,64]{1,2,0:T(8,128)(2,1)} %param.10) | copy-start | bytes 1572868
  0.7 16.9 %copy-start.11 = (bf16[8,32,64]{2,1,0:T(8,128)(2,1)S(1)}, bf16[8,32,64]{2,1,0:T(8,128)(2,1)}, u32[]{:S(2)}) copy-start(bf16[8,32,64]{2,1,0:T(8,128)(2,1)} %refs_2_) | copy-start | bytes 98308
  0.7 24.3 %copy-start.12 = (s32[16]{0:T(128)S(1)}, s32[16]{0:T(128)}, u32[]{:S(2)}) copy-start(s32[16]{0:T(128)} %table.5) | copy-start | bytes 196
  0.7 23.7 %collective-permute-start = (bf16[8,64,512]{2,1,0:T(8,128)(2,1)}, bf16[8,64,512]{2,1,0:T(8,128)(2,1)S(1)}, u32[]{:S(2)}, u32[]{:S(2)}) collective-permute-start(bf16[8,64,512]{2,1,0:T(8,128)(2,1)} %bitcast.4), channel_id=1, source_target_pairs={{0,1},{1,0},{2,3},{3,2},{4,5},{5,4},{6,7},{7,6},{8,9},{9,8},{10,11... | collective-permute-start | bytes 1572872 | tf_op jit(solution)/shard_map/down_dp/ppermute | solution.py:200
  3.7 5.8 %collective-permute-start.2 = (bf16[128,512]{1,0:T(8,128)(2,1)}, bf16[128,512]{1,0:T(8,128)(2,1)S(1)}, u32[]{:S(2)}, u32[]{:S(2)}) collective-permute-start(bf16[128,512]{1,0:T(8,128)(2,1)} %g.1), channel_id=1, source_target_pairs={{0,4},{2,6},{4,0},{6,2},{8,12},{10,14},{12,8},{14,10},{16,20},{18,... | collective-permute-start | bytes 393224 | tf_op jit(solution)/shard_map/g_fsdp/ppermute | solution.py:200
  5.2 19.1 %collective-permute-start.5 = (bf16[256,512]{1,0:T(8,128)(2,1)S(1)}, bf16[256,512]{1,0:T(8,128)(2,1)S(1)}, u32[]{:S(2)}, u32[]{:S(2)}) collective-permute-start(bf16[256,512]{1,0:T(8,128)(2,1)S(1)} %constant_dynamic-slice_fusion.refs_3_), channel_id=1, source_target_pairs={{0,16},{2,18},{4,20},{6,22},{8,24},{10,26},{12,28},{14,30},{16,0},... | collective-permute-start | bytes 786440 | tf_op jit(solution)/shard_map/w_layers/ppermute | solution.py:200
  7.9 16.4 %collective-permute-start.4 = (bf16[256,512]{1,0:T(8,128)(2,1)S(1)}, bf16[256,512]{1,0:T(8,128)(2,1)S(1)}, u32[]{:S(2)}, u32[]{:S(2)}) collective-permute-start(bf16[256,512]{1,0:T(8,128)(2,1)S(1)} %constant_dynamic-slice_fusion.refs_3_), channel_id=1, source_target_pairs={{0,8},{2,10},{4,12},{6,14},{8,0},{10,2},{12,4},{14,6},{16,24},{18,... | collective-permute-start | bytes 786440 | tf_op jit(solution)/shard_map/w_layers/ppermute | solution.py:200
  10.4 13.9 %collective-permute-start.3 = (bf16[256,512]{1,0:T(8,128)(2,1)S(1)}, bf16[256,512]{1,0:T(8,128)(2,1)S(1)}, u32[]{:S(2)}, u32[]{:S(2)}) collective-permute-start(bf16[256,512]{1,0:T(8,128)(2,1)S(1)} %pad_maximum_fusion), channel_id=1, source_target_pairs={{0,1},{1,0},{2,3},{3,2},{4,5},{5,4},{6,7},{7,6},{8,9},{9,8},{10,11... | collective-permute-start | bytes 786440 | tf_op jit(solution)/shard_map/g_dp/ppermute | solution.py:200
  12.2 11.7 %all-to-all-start = ((s32[16,1,128]{2,1,0:T(1,128)}), s32[16,1,128]{2,1,0:T(1,128)S(1)}, u32[]{:S(2)}, u32[]{:S(2)}) async-start(s32[16,1,128]{2,1,0:T(1,128)} %broadcast_in_dim.9), calls=%async_computation | async-start | bytes 16384 | tf_op jit(solution)/shard_map/ids/all_to_all | solution.py:230
  17.6 6.7 %collective-permute-start.1 = (bf16[8,32,64]{2,1,0:T(8,128)(2,1)S(1)}, bf16[8,32,64]{2,1,0:T(8,128)(2,1)S(1)}, u32[]{:S(2)}, u32[]{:S(2)}) collective-permute-start(bf16[8,32,64]{2,1,0:T(8,128)(2,1)S(1)} %copy-done.11), channel_id=1, source_target_pairs={{0,1},{1,0},{2,3},{3,2},{4,5},{5,4},{6,7},{7,6},{8,9},{9,8},{10,11... | collective-permute-start | bytes 98312 | tf_op jit(solution)/shard_map/up_dp/ppermute | solution.py:200
  24.3 3.3 %copy-start.14 = (bf16[256,512]{1,0:T(8,128)(2,1)}, bf16[256,512]{1,0:T(8,128)(2,1)S(1)}, u32[]{:S(2)}) copy-start(bf16[256,512]{1,0:T(8,128)(2,1)S(1)} %collective-permute-done.3.refs_2_) | copy-start | bytes 786436
  24.4 9.1 %collective-permute-start.6 = (bf16[256,512]{1,0:T(8,128)(2,1)S(1)}, bf16[256,512]{1,0:T(8,128)(2,1)S(1)}, u32[]{:S(2)}, u32[]{:S(2)}) collective-permute-start(bf16[256,512]{1,0:T(8,128)(2,1)S(1)} %collective-permute-done.5.refs_5_), channel_id=1, source_target_pairs={{0,8},{2,10},{4,12},{6,14},{8,0},{10,2},{12,4},{14,6},{16,24},{18,... | collective-permute-start | bytes 786440 | tf_op jit(solution)/shard_map/w_last/ppermute | solution.py:200
  27.6 7.6 %copy-start.3 = (bf16[128,512]{1,0:T(8,128)(2,1)S(1)}, bf16[128,512]{1,0:T(8,128)(2,1)}, u32[]{:S(2)}) copy-start(bf16[128,512]{1,0:T(8,128)(2,1)} %g.1) | copy-start | bytes 393220
  27.6 33.1 %all-to-all-start.1 = ((bf16[16,272,128]{2,1,0:T(8,128)(2,1)}), bf16[16,272,128]{2,1,0:T(8,128)(2,1)S(1)}, u32[]{:S(2)}, u32[]{:S(2)}) async-start(bf16[16,272,128]{2,1,0:T(8,128)(2,1)} %select.3), calls=%async_computation.1 | async-start | bytes 2228224 | tf_op jit(solution)/shard_map/adapters_to_blocks/all_to_all | solution.py:260
  32.5 2.4 %collective-permute-start.9 = (bf16[256,512]{1,0:T(8,128)(2,1)S(1)}, bf16[256,512]{1,0:T(8,128)(2,1)S(1)}, u32[]{:S(2)}, u32[]{:S(2)}) collective-permute-start(bf16[256,512]{1,0:T(8,128)(2,1)S(1)} %collective-permute-done.5.refs_5_), channel_id=1, source_target_pairs={{0,2},{2,0},{4,6},{6,4},{8,10},{10,8},{12,14},{14,12},{16,18},{18,... | collective-permute-start | bytes 786440 | tf_op jit(solution)/shard_map/w_core/ppermute | solution.py:200
  32.9 1.6 %collective-permute-start.7 = (bf16[256,512]{1,0:T(8,128)(2,1)S(1)}, bf16[256,512]{1,0:T(8,128)(2,1)S(1)}, u32[]{:S(2)}, u32[]{:S(2)}) collective-permute-start(bf16[256,512]{1,0:T(8,128)(2,1)S(1)} %constant_dynamic-slice_fusion.refs_3_), channel_id=1, source_target_pairs={{0,2},{2,0},{4,6},{6,4},{8,10},{10,8},{12,14},{14,12},{16,18},{18,... | collective-permute-start | bytes 786440 | tf_op jit(solution)/shard_map/w_core/ppermute | solution.py:200
  33.1 1.8 %collective-permute-start.8 = (bf16[256,512]{1,0:T(8,128)(2,1)S(1)}, bf16[256,512]{1,0:T(8,128)(2,1)S(1)}, u32[]{:S(2)}, u32[]{:S(2)}) collective-permute-start(bf16[256,512]{1,0:T(8,128)(2,1)S(1)} %collective-permute-done.4.refs_4_), channel_id=1, source_target_pairs={{0,2},{2,0},{4,6},{6,4},{8,10},{10,8},{12,14},{14,12},{16,18},{18,... | collective-permute-start | bytes 786440 | tf_op jit(solution)/shard_map/w_core/ppermute | solution.py:200
  33.5 1.8 %collective-permute-start.10 = (bf16[256,512]{1,0:T(8,128)(2,1)S(1)}, bf16[256,512]{1,0:T(8,128)(2,1)S(1)}, u32[]{:S(2)}, u32[]{:S(2)}) collective-permute-start(bf16[256,512]{1,0:T(8,128)(2,1)S(1)} %collective-permute-done.6.refs_6_), channel_id=1, source_target_pairs={{0,2},{2,0},{4,6},{6,4},{8,10},{10,8},{12,14},{14,12},{16,18},{18,... | collective-permute-start | bytes 786440 | tf_op jit(solution)/shard_map/w_core/ppermute | solution.py:200
  33.6 0.7 copy-start.16
  35.3 1.0 copy-start.15
  36.2 0.9 copy-start.17
  40.0 19.9 %copy-start.13 = (bf16[128,2048]{1,0:T(8,128)(2,1)}, bf16[128,2048]{1,0:T(8,128)(2,1)S(1)}, u32[]{:S(2)}) copy-start(bf16[128,2048]{1,0:T(8,128)(2,1)S(1)} %get-tuple-element.52) | copy-start | bytes 1572868
  40.0 19.9 %collective-permute-start.11 = (bf16[128,2048]{1,0:T(8,128)(2,1)S(1)}, bf16[128,2048]{1,0:T(8,128)(2,1)S(1)}, u32[]{:S(2)}, u32[]{:S(2)}) collective-permute-start(bf16[128,2048]{1,0:T(8,128)(2,1)S(1)} %get-tuple-element.45), channel_id=1, source_target_pairs={{0,4},{1,5},{2,6},{3,7},{4,0},{5,1},{6,2},{7,3},{8,12},{9,13},{10,... | collective-permute-start | bytes 1572872 | tf_op jit(solution)/shard_map/pieces20/ppermute | solution.py:200
  41.9 18.0 %collective-permute-start.12 = (bf16[128,2048]{1,0:T(8,128)(2,1)S(1)}, bf16[128,2048]{1,0:T(8,128)(2,1)S(1)}, u32[]{:S(2)}, u32[]{:S(2)}) collective-permute-start(bf16[128,2048]{1,0:T(8,128)(2,1)S(1)} %get-tuple-element.46), channel_id=1, source_target_pairs={{0,1},{1,0},{2,3},{3,2},{4,5},{5,4},{6,7},{7,6},{8,9},{9,8},{10,11... | collective-permute-start | bytes 1572872 | tf_op jit(solution)/shard_map/pieces01/ppermute | solution.py:200
  59.9 3.7 %copy-start.5 = (bf16[128,2048]{1,0:T(8,128)(2,1)}, bf16[128,2048]{1,0:T(8,128)(2,1)S(1)}, u32[]{:S(2)}) copy-start(bf16[128,2048]{1,0:T(8,128)(2,1)S(1)} %collective-permute-done.11.refs_1_) | copy-start | bytes 1572868
  59.9 0.8 copy-start.7
  60.7 1.6 %copy-start.1 = (bf16[128,8192]{1,0:T(8,128)(2,1)S(1)}, bf16[128,8192]{1,0:T(8,128)(2,1)}, u32[]{:S(2)}) copy-start(bf16[128,8192]{1,0:T(8,128)(2,1)} %x.1) | copy-start | bytes 6291460
  63.6 1.0 copy-start.2
  64.6 31.0 %all-to-all-start.2 = ((bf16[16,272,128]{2,1,0:T(8,128)(2,1)}), bf16[16,272,128]{2,1,0:T(8,128)(2,1)S(1)}, u32[]{:S(2)}, u32[]{:S(2)}) async-start(bf16[16,272,128]{2,1,0:T(8,128)(2,1)} %copy-done.2), calls=%async_computation.2 | async-start | bytes 2228224 | tf_op jit(solution)/shard_map/gradients_back/all_to_all | solution.py:294
  69.9 22.1 %collective-permute-start.13 = (bf16[128,2048]{1,0:T(8,128)(2,1)}, bf16[128,2048]{1,0:T(8,128)(2,1)S(1)}, u32[]{:S(2)}, u32[]{:S(2)}) collective-permute-start(bf16[128,2048]{1,0:T(8,128)(2,1)} %copy-done.13), channel_id=1, source_target_pairs={{0,5},{1,4},{2,7},{3,6},{4,1},{5,0},{6,3},{7,2},{8,13},{9,12},{10,... | collective-permute-start | bytes 1572872 | tf_op jit(solution)/shard_map/pieces21/ppermute | solution.py:200
  92.0 0.8 copy-start.9
  95.6 2.5 %copy-start.6 = (bf16[128,2048]{1,0:T(8,128)(2,1)S(1)}, bf16[128,2048]{1,0:T(8,128)(2,1)}, u32[]{:S(2)}) copy-start(bf16[128,2048]{1,0:T(8,128)(2,1)} %copy-done.5) | copy-start | bytes 1572868
  95.6 2.5 %copy-start.8 = (bf16[128,2048]{1,0:T(8,128)(2,1)S(1)}, bf16[128,2048]{1,0:T(8,128)(2,1)}, u32[]{:S(2)}) copy-start(bf16[128,2048]{1,0:T(8,128)(2,1)} %copy-done.7) | copy-start | bytes 1572868
  95.6 2.5 %copy-start.10 = (bf16[128,2048]{1,0:T(8,128)(2,1)S(1)}, bf16[128,2048]{1,0:T(8,128)(2,1)}, u32[]{:S(2)}) copy-start(bf16[128,2048]{1,0:T(8,128)(2,1)} %copy-done.9) | copy-start | bytes 1572868
  96.6 15.0 %collective-permute-start.14 = (bf16[8,272,128]{2,1,0:T(8,128)(2,1)S(1)}, bf16[8,272,128]{2,1,0:T(8,128)(2,1)S(1)}, u32[]{:S(2)}, u32[]{:S(2)}) collective-permute-start(bf16[8,272,128]{2,1,0:T(8,128)(2,1)S(1)} %sort.1), channel_id=1, source_target_pairs={{0,1},{1,0},{2,3},{3,2},{4,5},{5,4},{6,7},{7,6},{8,9},{9,8},{10,11... | collective-permute-start | bytes 1671176 | tf_op jit(solution)/shard_map/grads_dp/ppermute | solution.py:200

commit v3 on v2

--- a/solution.py
+++ b/solution.py
@@ -10,7 +10,8 @@
 
 adapter_scale_factor = 2.0
 lanes = 128
-base_weight = 12
+base_weight = 11
+store_parts = 4
 BF16, F32 = jnp.bfloat16, jnp.float32
 NT = (((1,), (1,)), ((), ()))
 TN = (((0,), (0,)), ((), ()))
@@ -85,7 +86,7 @@
                 out[k, cut:, :] = pack_up(ups[j][place])
 
 
-def middle_kernel(kv_rows, rank, x, g, got, hidden_out, back):
+def middle_kernel(kv_rows, rank, halves, x, g, got, hidden_out, back, out, up_out, sems):
     fsdp_count = got.shape[0]
     tiles = x.shape[1] // fsdp_count // lanes
     rows = tiles * lanes
@@ -96,15 +97,38 @@
     hidden = dot(g[...], up, NN).astype(BF16)
     hidden_out[...] = hidden
     inner = jnp.zeros((x.shape[0], rank), F32)
+    stores = []
+    step = max(1, fsdp_count // store_parts)
     for f in range(fsdp_count):
         x_part = x[:, f * rows : (f + 1) * rows]
         inner += dot(x_part, wide(got, f, 0, tiles, rank), NT)
         down = (adapter_scale_factor * dot(hidden, x_part, TN)).astype(BF16)
         for c in range(tiles):
-            back[f, c * rank : (c + 1) * rank, :] = down[:, c * lanes : (c + 1) * lanes]
+            half, at = c * halves // tiles, c % (tiles // halves) * rank
+            out[f * halves + half, at : at + rank, :] = down[:, c * lanes : (c + 1) * lanes]
+        if (f + 1) % step == 0:
+            here = pl.ds((f + 1 - step) * halves, step * halves)
+            stores.append(
+                pltpu.make_async_copy(
+                    out.at[here], back.at[here, 0 : out.shape[1], :], sems.at[len(stores)]
+                )
+            )
+            stores[-1].start()
     part_up = (adapter_scale_factor * dot(g[...], inner.astype(BF16), TN)).astype(BF16)
     for f in range(fsdp_count):
-        back[f, cut:, :] = pack_up(part_up[f * kv_rows : (f + 1) * kv_rows])
+        packed = pack_up(part_up[f * kv_rows : (f + 1) * kv_rows])
+        for half in range(halves):
+            up_out[f * halves + half] = packed
+    stores.append(
+        pltpu.make_async_copy(
+            up_out,
+            back.at[:, out.shape[1] : out.shape[1] + up_out.shape[1], :],
+            sems.at[len(stores)],
+        )
+    )
+    stores[-1].start()
+    for store in stores:
+        store.wait()
 
 
 def base_kernel(g_counts, w_count, *refs):
@@ -178,6 +202,42 @@
             up[place] = unpack_up(total[tiles * rank :], kv_rows, rank)
 
 
+def sum_halves_kernel(dp_count, kv_rows, *refs):
+    slots, got, (own_down, *sends, up, place_of) = (
+        refs[:dp_count], refs[dp_count], refs[dp_count + 1 :],
+    )
+    own, rank, width = own_down.shape
+    tiles = width // lanes
+    here = lax.axis_index("dp")
+
+    @pl.loop(0, slots[0].shape[0])
+    def _(k):
+        for j in range(dp_count):
+            place_of[j, slots[j][k]] = k * dp_count + (here ^ j)
+
+    for step, out in enumerate([own_down, *sends]):
+
+        @pl.loop(0, own)
+        def _(place):
+            slot = (here ^ step) * own + place
+            total = got[place_of[0, slot]].astype(F32)
+            for j in range(1, dp_count):
+                total += got[place_of[j, slot]].astype(F32)
+            total = total.astype(BF16)
+            for c in range(tiles):
+                out[place, :, c * lanes : (c + 1) * lanes] = total[c * rank : (c + 1) * rank]
+            if step == 0:
+                up[place] = unpack_up(total[tiles * rank :], kv_rows, rank)
+
+
+def join_kernel(dp_count, *refs):
+    parts, out = refs[:-1], refs[-1]
+    width = parts[0].shape[2]
+    here = lax.axis_index("dp")
+    for step, part in enumerate(parts):
+        out[:, :, pl.ds(pl.multiple_of((here ^ step) * width, lanes), width)] = part[...]
+
+
 def vmem(count):
     return [pl.BlockSpec(memory_space=pltpu.VMEM)] * count
 
@@ -243,7 +303,7 @@
         rels = rels + [(i | bit, d) if axis == "fsdp" else (i, d | bit) for i, d in rels]
         if n + 1 < len(stages):
             held = jnp.concatenate([held, new], axis=0)
-    ids, downs, ups, gs, ws = lax.optimization_barrier((ids, downs, ups, gs, ws))
+    ids, downs, ups, gs = lax.optimization_barrier((ids, downs, ups, gs))
 
     box = jax.ShapeDtypeStruct((fsdp_count, tall, lanes), BF16)
     box_bytes = 2 * fsdp_count * tall * lanes
@@ -271,7 +331,7 @@
         out_specs=vmem(len(rels)),
         compiler_params=params(),
         cost_estimate=cost(
-            base_weight * 2 * tokens * width * kv_width, base_weight * 4 * tokens * width
+            12 * 2 * tokens * width * kv_width, 12 * 4 * tokens * width
         ),
         name="base",
     )(*gs, *ws)
@@ -281,17 +341,40 @@
     ]
     got, pieces[:-1] = lax.optimization_barrier((got, pieces[:-1]))
 
+    tiles = rows // lanes
+    halves = dp_count if tiles % dp_count == 0 else 1
+    cut = tiles // halves * rank
+    small = packed_rows(kv_rows)[0]
+    back_shape = (fsdp_count * halves, cut + small, lanes)
     hidden, back = pl.pallas_call(
-        functools.partial(middle_kernel, kv_rows, rank),
-        out_shape=[jax.ShapeDtypeStruct((tokens, rank), BF16), box],
+        functools.partial(middle_kernel, kv_rows, rank, halves),
+        out_shape=[
+            jax.ShapeDtypeStruct((tokens, rank), BF16),
+            pltpu.HBM(back_shape, BF16),
+        ],
         in_specs=vmem(3),
-        out_specs=vmem(2),
+        out_specs=vmem(1) + [pl.BlockSpec(memory_space=pltpu.HBM)],
+        scratch_shapes=[
+            pltpu.VMEM((fsdp_count * halves, cut, lanes), BF16),
+            pltpu.VMEM((fsdp_count * halves, small, lanes), BF16),
+            pltpu.SemaphoreType.DMA((store_parts + 1,)),
+        ],
         compiler_params=params(),
         cost_estimate=cost(4 * tokens * width * rank, 2 * tokens * width + 2 * box_bytes),
         name="middle",
     )(inputs, grad_value, got)
     with jax.named_scope("gradients_back"):
-        returned = lax.all_to_all(back, "fsdp", 0, 0, tiled=True)
+        axes = "fsdp" if halves == 1 else ("fsdp", "dp")
+        returned = lax.all_to_all(back, axes, 0, 0, tiled=True)
+    if halves > 1:
+        slots = jnp.sum(
+            jnp.where(
+                ids[:, None] == jnp.arange(slot_table.shape[0])[None, :], slot_table[None, :], 0
+            ),
+            axis=1,
+        )
+        all_slots = [slots] + [exchange("slots_dp", slots, "dp", j) for j in range(1, dp_count)]
+        returned, all_slots = lax.optimization_barrier((returned, all_slots))
     returned, pieces = lax.optimization_barrier((returned, pieces))
 
     input_gradient_rows = pl.pallas_call(
@@ -304,31 +387,57 @@
         name="rows",
     )(hidden, got, *pieces)
 
-    sends = pl.pallas_call(
-        functools.partial(sort_kernel, dp_count, own),
-        out_shape=[jax.ShapeDtypeStruct((own, tall, lanes), BF16)] * (dp_count - 1),
-        in_specs=smem(2) + vmem(1),
-        out_specs=vmem(dp_count - 1),
-        compiler_params=params(),
-        cost_estimate=cost(0, 2 * box_bytes),
-        name="sort",
-    )(ids, slot_table, returned)
-    received = [
-        exchange("grads_dp", s, "dp", j + 1) for j, s in enumerate(sends)
-    ]
-    received, input_gradient_rows = lax.optimization_barrier((received, input_gradient_rows))
-    grad_down_t, grad_up = pl.pallas_call(
-        functools.partial(sum_kernel, dp_count, kv_rows),
-        out_shape=[
-            jax.ShapeDtypeStruct((own, rank, rows), BF16),
-            jax.ShapeDtypeStruct(adapter_up.shape, BF16),
-        ],
-        in_specs=smem(2) + vmem(dp_count),
-        out_specs=vmem(2),
-        compiler_params=params(),
-        cost_estimate=cost(0, 2 * box_bytes),
-        name="sums",
-    )(ids, slot_table, returned, *received)
+    if halves > 1:
+        part = (own, rank, rows // halves)
+        *sums, grad_up = pl.pallas_call(
+            functools.partial(sum_halves_kernel, dp_count, kv_rows),
+            out_shape=[jax.ShapeDtypeStruct(part, BF16)] * dp_count
+            + [jax.ShapeDtypeStruct(adapter_up.shape, BF16)],
+            in_specs=smem(dp_count) + vmem(1),
+            out_specs=vmem(dp_count + 1),
+            scratch_shapes=[pltpu.SMEM((dp_count, own * dp_count), jnp.int32)],
+            compiler_params=params(),
+            cost_estimate=cost(0, 2 * box_bytes),
+            name="sum_halves",
+        )(*all_slots, returned)
+        received = [exchange("grads_dp", s, "dp", j) for j, s in enumerate(sums[1:], 1)]
+        received, input_gradient_rows = lax.optimization_barrier((received, input_gradient_rows))
+        grad_down_t = pl.pallas_call(
+            functools.partial(join_kernel, dp_count),
+            out_shape=jax.ShapeDtypeStruct((own, rank, rows), BF16),
+            in_specs=vmem(dp_count),
+            out_specs=pl.BlockSpec(memory_space=pltpu.VMEM),
+            compiler_params=params(),
+            cost_estimate=cost(0, 4 * own * rank * rows),
+            name="join",
+        )(sums[0], *received)
+    else:
+        sends = pl.pallas_call(
+            functools.partial(sort_kernel, dp_count, own),
+            out_shape=[jax.ShapeDtypeStruct((own, tall, lanes), BF16)] * (dp_count - 1),
+            in_specs=smem(2) + vmem(1),
+            out_specs=vmem(dp_count - 1),
+            compiler_params=params(),
+            cost_estimate=cost(0, 2 * box_bytes),
+            name="sort",
+        )(ids, slot_table, returned)
+        received = [
+            exchange("grads_dp", s, "dp", j + 1) for j, s in enumerate(sends)
+        ]
+        received, input_gradient_rows = lax.optimization_barrier((received, input_gradient_rows))
+        grad_down_t, grad_up = pl.pallas_call(
+            functools.partial(sum_kernel, dp_count, kv_rows),
+            out_shape=[
+                jax.ShapeDtypeStruct((own, rank, rows), BF16),
+                jax.ShapeDtypeStruct(adapter_up.shape, BF16),
+            ],
+            in_specs=smem(2) + vmem(dp_count),
+            out_specs=vmem(2),
+            compiler_params=params(),
+            cost_estimate=cost(0, 2 * box_bytes),
+            name="sums",
+        )(ids, slot_table, returned, *received)
+
     return (input_gradient_rows, grad_down_t.transpose(0, 2, 1), grad_up)
 
 

time: 115 us -> 118 us (1.026)
  waiting for transfers between devices: 55.6 us -> 58.8 us
  starting transfers between devices: 35.9 us -> 33.7 us
  Pallas kernels: 12 us -> 13.5 us
    ppermute x15 -> x16, waiting for transfers between devices: 48.1 us -> 51.6 us  [exchange(): return lax.ppermute(array, axis, xor_pairs(axis_count(axis), bits))]
    ppermute x15 -> x16, starting transfers between devices: 20.4 us -> 20.3 us  [exchange(): return lax.ppermute(array, axis, xor_pairs(axis_count(axis), bits))]
    unnamed x36 -> x32, local copies, waits for them, and re-layouts: 6.85 us -> 6.78 us
  transfers between devices with their start and end apart: 18 -> 19, of which waited for: 8 -> 7; matrix products, arithmetic and copies ran while one was open for 2% -> 2% of each run, Pallas kernels for 7% -> 7%
where the time goes in v3:
time: 118 us; the launch traced here: 117 us
  waiting for transfers between devices  58.8 us (50%)
  starting transfers between devices  33.7 us (29%)
  Pallas kernels  13.5 us (11%)
  local copies, waits for them, and re-layouts  7.78 us (7%)
  other arithmetic  1.8 us (2%)
  between operations  1.47 us (1%)
    ppermute x16, waiting for transfers between devices, exchange(): return lax.ppermute(array, axis, xor_pairs(axis_count(axis), bits))  51.6 us
    ppermute x16, starting transfers between devices, exchange(): return lax.ppermute(array, axis, xor_pairs(axis_count(axis), bits))  20.3 us
    unnamed x32, local copies, waits for them, and re-layouts  6.78 us
    all_to_all x1, waiting for transfers between devices, on_device(): lax.all_to_all(jnp.broadcast_to(tenant_ids[:, None, None], (fsdp_count, 1...  5.32 us
    all_to_all x1, starting transfers between devices, on_device(): lax.all_to_all(jnp.broadcast_to(tenant_ids[:, None, None], (fsdp_count, 1...  4.82 us
    all_to_all x1, starting transfers between devices, on_device(): returned = lax.all_to_all(back, axes, 0, 0, tiled=True)  4.7 us
    all_to_all x1, starting transfers between devices, on_device(): got = lax.all_to_all(sent, 'fsdp', 0, 0, tiled=True)  3.88 us
    pallas_call x1, Pallas kernels, on_device(): pl.pallas_call(functools.partial(out_kernel, rels, layers, inner_count, s...  3.11 us
  transfers between devices with their start and end apart: 19, of which 7 were waited for; matrix products, arithmetic and copies ran while one was open for 2% of the time, Pallas kernels for 7%

profile of v3, /device:TPU:0, one launch (start us, length us, event | category | flops | bytes accessed | tf_op | source)
XLA Modules:
  0.0 117.0 jit_solution(457867389941288745)
XLA Ops:
  0.6 0.0 copy-start
  0.7 3.0 %collective-permute-start.2 = (bf16[128,512]{1,0:T(8,128)(2,1)}, bf16[128,512]{1,0:T(8,128)(2,1)S(1)}, u32[]{:S(2)}, u32[]{:S(2)}) collective-permute-start(bf16[128,512]{1,0:T(8,128)(2,1)} %g.1), channel_id=1, source_target_pairs={{0,4},{2,6},{4,0},{6,2},{8,12},{10,14},{12,8},{14,10},{16,20},{18,... | collective-permute-start | bytes 393224 | tf_op jit(solution)/shard_map/g_fsdp/ppermute | solution.py:260
  3.7 1.5 %collective-permute-start = (bf16[8,64,512]{2,1,0:T(8,128)(2,1)}, bf16[8,64,512]{2,1,0:T(8,128)(2,1)S(1)}, u32[]{:S(2)}, u32[]{:S(2)}) collective-permute-start(bf16[8,64,512]{2,1,0:T(8,128)(2,1)} %bitcast.4), channel_id=1, source_target_pairs={{0,1},{1,0},{2,3},{3,2},{4,5},{5,4},{6,7},{7,6},{8,9},{9,8},{10,11... | collective-permute-start | bytes 1572872 | tf_op jit(solution)/shard_map/down_dp/ppermute | solution.py:260
  5.2 2.7 %collective-permute-start.5 = (bf16[256,512]{1,0:T(8,128)(2,1)S(1)}, bf16[256,512]{1,0:T(8,128)(2,1)S(1)}, u32[]{:S(2)}, u32[]{:S(2)}) collective-permute-start(bf16[256,512]{1,0:T(8,128)(2,1)S(1)} %constant_dynamic-slice_fusion.refs_3_), channel_id=1, source_target_pairs={{0,16},{2,18},{4,20},{6,22},{8,24},{10,26},{12,28},{14,30},{16,0},... | collective-permute-start | bytes 786440 | tf_op jit(solution)/shard_map/w_layers/ppermute | solution.py:260
  7.9 0.0 collective-permute-done.2.refs_1_
  7.9 1.6 %pad_maximum_fusion = bf16[256,512]{1,0:T(8,128)(2,1)} fusion(bf16[128,512]{1,0:T(8,128)(2,1)S(1)} %collective-permute-done.2.refs_1_, bf16[128,512]{1,0:T(8,128)(2,1)} %g.1), kind=kLoop, calls=%fused_computation | loop fusion | flops 524288 | bytes 524288 | tf_op jit(solution)/shard_map/concatenate | solution.py:305
  9.5 1.2 %collective-permute-start.3 = (bf16[256,512]{1,0:T(8,128)(2,1)}, bf16[256,512]{1,0:T(8,128)(2,1)S(1)}, u32[]{:S(2)}, u32[]{:S(2)}) collective-permute-start(bf16[256,512]{1,0:T(8,128)(2,1)} %pad_maximum_fusion), channel_id=1, source_target_pairs={{0,1},{1,0},{2,3},{3,2},{4,5},{5,4},{6,7},{7,6},{8,9},{9,8},{10,11... | collective-permute-start | bytes 786440 | tf_op jit(solution)/shard_map/g_dp/ppermute | solution.py:260
  10.7 1.6 %collective-permute-start.4 = (bf16[256,512]{1,0:T(8,128)(2,1)S(1)}, bf16[256,512]{1,0:T(8,128)(2,1)S(1)}, u32[]{:S(2)}, u32[]{:S(2)}) collective-permute-start(bf16[256,512]{1,0:T(8,128)(2,1)S(1)} %constant_dynamic-slice_fusion.refs_3_), channel_id=1, source_target_pairs={{0,8},{2,10},{4,12},{6,14},{8,0},{10,2},{12,4},{14,6},{16,24},{18,... | collective-permute-start | bytes 786440 | tf_op jit(solution)/shard_map/w_layers/ppermute | solution.py:260
  12.3 7.1 %collective-permute-done.5.refs_5_ = bf16[256,512]{1,0:T(8,128)(2,1)S(1)} collective-permute-done((bf16[256,512]{1,0:T(8,128)(2,1)S(1)}, bf16[256,512]{1,0:T(8,128)(2,1)S(1)}, u32[]{:S(2)}, u32[]{:S(2)}) %collective-permute-start.5) | collective-permute-done | bytes 262176 | tf_op jit(solution)/shard_map/w_layers/ppermute | solution.py:260
  19.4 0.6 collective-permute-start.6
  20.6 0.6 broadcast_in_dim.24
  21.2 4.8 %all-to-all-start = ((s32[16,1,128]{2,1,0:T(1,128)}), s32[16,1,128]{2,1,0:T(1,128)S(1)}, u32[]{:S(2)}, u32[]{:S(2)}) async-start(s32[16,1,128]{2,1,0:T(1,128)} %broadcast_in_dim.24), calls=%async_computation | async-start | bytes 16384 | tf_op jit(solution)/shard_map/ids/all_to_all | solution.py:290
  26.1 1.0 collective-permute-start.1
  27.1 5.3 %all-to-all-done = s32[16,1,128]{2,1,0:T(1,128)S(1)} async-done(((s32[16,1,128]{2,1,0:T(1,128)}), s32[16,1,128]{2,1,0:T(1,128)S(1)}, u32[]{:S(2)}, u32[]{:S(2)}) %all-to-all-start) | async-done | bytes 8224 | tf_op jit(solution)/shard_map/ids/all_to_all | solution.py:290
  32.4 0.4 slice_reduce_fusion.ids
  32.8 0.0 copy-start.8
  32.8 0.8 copy-done.8
  33.7 0.7 copy-done.9
  34.3 2.7 %select.3 = bf16[16,272,128]{2,1,0:T(8,128)(2,1)} custom-call(s32[16]{0:T(128)S(1)} %slice_reduce_fusion.ids, s32[16]{0:T(128)S(1)} %copy-done.9, bf16[8,64,512]{2,1,0:T(8,128)(2,1)S(1)} %bitcast.5, bf16[8,64,512]{2,1,0:T(8,128)(2,1)S(1)} %collective-permute-done.refs_1_, bf16[8,32,64]{2,1,0:T(8,128)(2,1)S(1)} %copy-done.8, ...), custom_call_target="tpu_custom_call" | custom-call | bytes 2228224 | tf_op jit(solution)/shard_map/select/pallas_call | solution.py:310
  37.0 3.9 %all-to-all-start.1 = ((bf16[16,272,128]{2,1,0:T(8,128)(2,1)}), bf16[16,272,128]{2,1,0:T(8,128)(2,1)S(1)}, u32[]{:S(2)}, u32[]{:S(2)}) async-start(bf16[16,272,128]{2,1,0:T(8,128)(2,1)} %select.3), calls=%async_computation.1 | async-start | bytes 2228224 | tf_op jit(solution)/shard_map/adapters_to_blocks/all_to_all | solution.py:320
  40.9 0.4 collective-permute-start.7
  41.3 0.2 collective-permute-start.9
  41.5 0.3 collective-permute-start.8
  41.8 0.7 copy-done.12
  42.5 0.2 collective-permute-start.10
  42.7 0.7 copy-done.14
  43.4 0.7 collective-permute-done.10.refs_10_
  44.1 0.9 copy-done.13
  45.0 0.9 copy-done.15
  46.0 2.8 %base.1 = (bf16[128,2048]{1,0:T(8,128)(2,1)S(1)}, bf16[128,2048]{1,0:T(8,128)(2,1)S(1)}, bf16[128,2048]{1,0:T(8,128)(2,1)S(1)}, bf16[128,2048]{1,0:T(8,128)(2,1)S(1)}) custom-call(bf16[128,512]{1,0:T(8,128)(2,1)S(1)} %copy-done.2, bf16[128,512]{1,0:T(8,128)(2,1)S(1)} %collective-permute-done.2.refs_1_, bf16[256,512]{1,0:T(8,128)(2,1)S(1)} %collective-permute-done.3.refs_2_, ...), custom_call_target="tpu_custom_call" | custom-call | flops 12884901888 | bytes 50331648 | tf_op jit(solution)/shard_map/base/pallas_call | solution.py:327
  48.8 1.7 %collective-permute-start.11 = (bf16[128,2048]{1,0:T(8,128)(2,1)S(1)}, bf16[128,2048]{1,0:T(8,128)(2,1)S(1)}, u32[]{:S(2)}, u32[]{:S(2)}) collective-permute-start(bf16[128,2048]{1,0:T(8,128)(2,1)S(1)} %get-tuple-element.43), channel_id=1, source_target_pairs={{0,4},{1,5},{2,6},{3,7},{4,0},{5,1},{6,2},{7,3},{8,12},{9,13},{10,... | collective-permute-start | bytes 1572872 | tf_op jit(solution)/shard_map/pieces20/ppermute | solution.py:260
  50.5 1.0 collective-permute-start.12
  51.5 16.8 %collective-permute-done.11.refs_1_ = bf16[128,2048]{1,0:T(8,128)(2,1)S(1)} collective-permute-done((bf16[128,2048]{1,0:T(8,128)(2,1)S(1)}, bf16[128,2048]{1,0:T(8,128)(2,1)S(1)}, u32[]{:S(2)}, u32[]{:S(2)}) %collective-permute-start.11) | collective-permute-done | bytes 524320 | tf_op jit(solution)/shard_map/pieces20/ppermute | solution.py:260
  68.4 0.0 copy-start.1
  68.4 1.9 %copy-done.1 = bf16[128,8192]{1,0:T(8,128)(2,1)S(1)} copy-done((bf16[128,8192]{1,0:T(8,128)(2,1)S(1)}, bf16[128,8192]{1,0:T(8,128)(2,1)}, u32[]{:S(2)}) %copy-start.1) | copy-done | bytes 2097176
  70.3 2.0 %middle.1 = (bf16[128,64]{1,0:T(8,128)(2,1)S(1)}, bf16[32,144,128]{2,1,0:T(8,128)(2,1)}) custom-call(bf16[128,8192]{1,0:T(8,128)(2,1)S(1)} %copy-done.1, bf16[128,512]{1,0:T(8,128)(2,1)S(1)} %copy-done.2, bf16[16,272,128]{2,1,0:T(8,128)(2,1)S(1)} %all-to-all-done.1.got), custom_call_target="tpu_custom_call" | custom-call | flops 268435456 | bytes 4325376 | tf_op jit(solution)/shard_map/middle/pallas_call | solution.py:349
  72.4 0.0 copy-start.10
  72.4 4.7 %all-to-all-start.2 = ((bf16[32,144,128]{2,1,0:T(8,128)(2,1)}), bf16[32,144,128]{2,1,0:T(8,128)(2,1)S(1)}, u32[]{:S(2)}, u32[]{:S(2)}) async-start(bf16[32,144,128]{2,1,0:T(8,128)(2,1)} %get-tuple-element.46), calls=%async_computation.2 | async-start | bytes 2359296 | tf_op jit(solution)/shard_map/gradients_back/all_to_all | solution.py:368
  77.1 2.7 %collective-permute-start.14 = (bf16[128,2048]{1,0:T(8,128)(2,1)}, bf16[128,2048]{1,0:T(8,128)(2,1)}, u32[]{:S(2)}, u32[]{:S(2)}) collective-permute-start(bf16[128,2048]{1,0:T(8,128)(2,1)} %copy-done.11), channel_id=1, source_target_pairs={{0,5},{1,4},{2,7},{3,6},{4,1},{5,0},{6,3},{7,2},{8,13},{9,12},{10,... | collective-permute-start | bytes 1572872 | tf_op jit(solution)/shard_map/pieces21/ppermute | solution.py:260
  79.8 0.2 select_reduce_fusion.refs_0_
  80.0 0.6 collective-permute-start.13
  80.6 23.7 %collective-permute-done.13.refs_1_ = s32[16]{0:T(128)S(1)} collective-permute-done((s32[16]{0:T(128)S(1)}, s32[16]{0:T(128)S(1)}, u32[]{:S(2)}, u32[]{:S(2)}) %collective-permute-start.13) | collective-permute-done | bytes 96 | tf_op jit(solution)/shard_map/slots_dp/ppermute | solution.py:260
  104.3 1.8 %all-to-all-done.2.refs_2_ = bf16[32,144,128]{2,1,0:T(8,128)(2,1)S(1)} async-done(((bf16[32,144,128]{2,1,0:T(8,128)(2,1)}), bf16[32,144,128]{2,1,0:T(8,128)(2,1)S(1)}, u32[]{:S(2)}, u32[]{:S(2)}) %all-to-all-start.2) | async-done | bytes 1179680 | tf_op jit(solution)/shard_map/gradients_back/all_to_all | solution.py:368
  106.2 2.0 %sum_halves.1 = (bf16[8,64,256]{2,1,0:T(8,128)(2,1)S(1)}, bf16[8,64,256]{2,1,0:T(8,128)(2,1)S(1)}, bf16[8,32,64]{2,1,0:T(8,128)(2,1)}) custom-call(s32[16]{0:T(128)S(1)} %select_reduce_fusion.refs_0_, s32[16]{0:T(128)S(1)} %collective-permute-done.13.refs_1_, bf16[32,144,128]{2,1,0:T(8,128)(2,1)S(1)} %all-to-all-done.2.refs_2_), custom_call_target="tpu_custom_call" | custom-call | bytes 2228224 | tf_op jit(solution)/shard_map/sum_halves/pallas_call | solution.py:392
  108.2 1.5 %collective-permute-start.15 = (bf16[8,64,256]{2,1,0:T(8,128)(2,1)S(1)}, bf16[8,64,256]{2,1,0:T(8,128)(2,1)S(1)}, u32[]{:S(2)}, u32[]{:S(2)}) collective-permute-start(bf16[8,64,256]{2,1,0:T(8,128)(2,1)S(1)} %get-tuple-element.55), channel_id=1, source_target_pairs={{0,1},{1,0},{2,3},{3,2},{4,5},{5,4},{6,7},{7,6},{8,9},{9,8},{10,11... | collective-permute-start | bytes 786440 | tf_op jit(solution)/shard_map/grads_dp/ppermute | solution.py:260
  109.7 3.1 %rows.1 = bf16[128,8192]{1,0:T(8,128)(2,1)} custom-call(bf16[128,64]{1,0:T(8,128)(2,1)S(1)} %get-tuple-element.56.hidden, bf16[16,272,128]{2,1,0:T(8,128)(2,1)S(1)} %all-to-all-done.1.got, bf16[128,2048]{1,0:T(8,128)(2,1)S(1)} %get-tuple-element.57.refs_0_, bf16[128,2048]{1,0:T(8,128)(2,1)S(1)} %copy-done.5, bf16[128,2048]{1,0:T(8,128)(2,1)S(1)} %copy-done.7, ...), custom_call_target="tpu_custom_call" | custom-call | flops 134217728 | bytes 5308416 | tf_op jit(solution)/shard_map/rows/pallas_call | solution.py:380
  112.8 3.3 %collective-permute-done.15.refs_1_ = bf16[8,64,256]{2,1,0:T(8,128)(2,1)S(1)} collective-permute-done((bf16[8,64,256]{2,1,0:T(8,128)(2,1)S(1)}, bf16[8,64,256]{2,1,0:T(8,128)(2,1)S(1)}, u32[]{:S(2)}, u32[]{:S(2)}) %collective-permute-start.15) | collective-permute-done | bytes 262176 | tf_op jit(solution)/shard_map/grads_dp/ppermute | solution.py:260
  116.2 0.8 join.1
  (33 shorter events, 0.1 us)
Async XLA Ops:
  0.6 4.6 %copy-start = (bf16[512,512]{1,0:T(8,128)(2,1)S(1)}, bf16[512,512]{1,0:T(8,128)(2,1)}, u32[]{:S(2)}) copy-start(bf16[512,512]{1,0:T(8,128)(2,1)} %param.9) | copy-start | bytes 1572868
  0.6 32.2 %copy-start.3 = (bf16[8,512,64]{1,2,0:T(8,128)(2,1)S(1)}, bf16[8,512,64]{1,2,0:T(8,128)(2,1)}, u32[]{:S(2)}) copy-start(bf16[8,512,64]{1,2,0:T(8,128)(2,1)} %param.10) | copy-start | bytes 1572868
  0.7 7.2 %collective-permute-start.2 = (bf16[128,512]{1,0:T(8,128)(2,1)}, bf16[128,512]{1,0:T(8,128)(2,1)S(1)}, u32[]{:S(2)}, u32[]{:S(2)}) collective-permute-start(bf16[128,512]{1,0:T(8,128)(2,1)} %g.1), channel_id=1, source_target_pairs={{0,4},{2,6},{4,0},{6,2},{8,12},{10,14},{12,8},{14,10},{16,20},{18,... | collective-permute-start | bytes 393224 | tf_op jit(solution)/shard_map/g_fsdp/ppermute | solution.py:260
  3.7 29.1 %collective-permute-start = (bf16[8,64,512]{2,1,0:T(8,128)(2,1)}, bf16[8,64,512]{2,1,0:T(8,128)(2,1)S(1)}, u32[]{:S(2)}, u32[]{:S(2)}) collective-permute-start(bf16[8,64,512]{2,1,0:T(8,128)(2,1)} %bitcast.4), channel_id=1, source_target_pairs={{0,1},{1,0},{2,3},{3,2},{4,5},{5,4},{6,7},{7,6},{8,9},{9,8},{10,11... | collective-permute-start | bytes 1572872 | tf_op jit(solution)/shard_map/down_dp/ppermute | solution.py:260
  5.2 14.2 %collective-permute-start.5 = (bf16[256,512]{1,0:T(8,128)(2,1)S(1)}, bf16[256,512]{1,0:T(8,128)(2,1)S(1)}, u32[]{:S(2)}, u32[]{:S(2)}) collective-permute-start(bf16[256,512]{1,0:T(8,128)(2,1)S(1)} %constant_dynamic-slice_fusion.refs_3_), channel_id=1, source_target_pairs={{0,16},{2,18},{4,20},{6,22},{8,24},{10,26},{12,28},{14,30},{16,0},... | collective-permute-start | bytes 786440 | tf_op jit(solution)/shard_map/w_layers/ppermute | solution.py:260
  9.5 23.3 %collective-permute-start.3 = (bf16[256,512]{1,0:T(8,128)(2,1)}, bf16[256,512]{1,0:T(8,128)(2,1)S(1)}, u32[]{:S(2)}, u32[]{:S(2)}) collective-permute-start(bf16[256,512]{1,0:T(8,128)(2,1)} %pad_maximum_fusion), channel_id=1, source_target_pairs={{0,1},{1,0},{2,3},{3,2},{4,5},{5,4},{6,7},{7,6},{8,9},{9,8},{10,11... | collective-permute-start | bytes 786440 | tf_op jit(solution)/shard_map/g_dp/ppermute | solution.py:260
  10.7 30.8 %collective-permute-start.4 = (bf16[256,512]{1,0:T(8,128)(2,1)S(1)}, bf16[256,512]{1,0:T(8,128)(2,1)S(1)}, u32[]{:S(2)}, u32[]{:S(2)}) collective-permute-start(bf16[256,512]{1,0:T(8,128)(2,1)S(1)} %constant_dynamic-slice_fusion.refs_3_), channel_id=1, source_target_pairs={{0,8},{2,10},{4,12},{6,14},{8,0},{10,2},{12,4},{14,6},{16,24},{18,... | collective-permute-start | bytes 786440 | tf_op jit(solution)/shard_map/w_layers/ppermute | solution.py:260
  19.4 23.2 %collective-permute-start.6 = (bf16[256,512]{1,0:T(8,128)(2,1)S(1)}, bf16[256,512]{1,0:T(8,128)(2,1)S(1)}, u32[]{:S(2)}, u32[]{:S(2)}) collective-permute-start(bf16[256,512]{1,0:T(8,128)(2,1)S(1)} %collective-permute-done.5.refs_5_), channel_id=1, source_target_pairs={{0,8},{2,10},{4,12},{6,14},{8,0},{10,2},{12,4},{14,6},{16,24},{18,... | collective-permute-start | bytes 786440 | tf_op jit(solution)/shard_map/w_last/ppermute | solution.py:260
  21.2 11.2 %all-to-all-start = ((s32[16,1,128]{2,1,0:T(1,128)}), s32[16,1,128]{2,1,0:T(1,128)S(1)}, u32[]{:S(2)}, u32[]{:S(2)}) async-start(s32[16,1,128]{2,1,0:T(1,128)} %broadcast_in_dim.24), calls=%async_computation | async-start | bytes 16384 | tf_op jit(solution)/shard_map/ids/all_to_all | solution.py:290
  26.1 6.7 %collective-permute-start.1 = (bf16[8,32,64]{2,1,0:T(8,128)(2,1)}, bf16[8,32,64]{2,1,0:T(8,128)(2,1)S(1)}, u32[]{:S(2)}, u32[]{:S(2)}) collective-permute-start(bf16[8,32,64]{2,1,0:T(8,128)(2,1)} %refs_2_), channel_id=1, source_target_pairs={{0,1},{1,0},{2,3},{3,2},{4,5},{5,4},{6,7},{7,6},{8,9},{9,8},{10,11... | collective-permute-start | bytes 98312 | tf_op jit(solution)/shard_map/up_dp/ppermute | solution.py:260
  32.8 0.8 copy-start.8
  33.7 0.7 copy-start.9
  37.0 7.1 %copy-start.2 = (bf16[128,512]{1,0:T(8,128)(2,1)S(1)}, bf16[128,512]{1,0:T(8,128)(2,1)}, u32[]{:S(2)}) copy-start(bf16[128,512]{1,0:T(8,128)(2,1)} %g.1) | copy-start | bytes 393220
  37.0 31.3 %all-to-all-start.1 = ((bf16[16,272,128]{2,1,0:T(8,128)(2,1)}), bf16[16,272,128]{2,1,0:T(8,128)(2,1)S(1)}, u32[]{:S(2)}, u32[]{:S(2)}) async-start(bf16[16,272,128]{2,1,0:T(8,128)(2,1)} %select.3), calls=%async_computation.1 | async-start | bytes 2228224 | tf_op jit(solution)/shard_map/adapters_to_blocks/all_to_all | solution.py:320
  40.9 2.5 %collective-permute-start.7 = (bf16[256,512]{1,0:T(8,128)(2,1)S(1)}, bf16[256,512]{1,0:T(8,128)(2,1)S(1)}, u32[]{:S(2)}, u32[]{:S(2)}) collective-permute-start(bf16[256,512]{1,0:T(8,128)(2,1)S(1)} %constant_dynamic-slice_fusion.refs_3_), channel_id=1, source_target_pairs={{0,2},{2,0},{4,6},{6,4},{8,10},{10,8},{12,14},{14,12},{16,18},{18,... | collective-permute-start | bytes 786440 | tf_op jit(solution)/shard_map/w_core/ppermute | solution.py:260
  41.3 2.1 %collective-permute-start.9 = (bf16[256,512]{1,0:T(8,128)(2,1)S(1)}, bf16[256,512]{1,0:T(8,128)(2,1)S(1)}, u32[]{:S(2)}, u32[]{:S(2)}) collective-permute-start(bf16[256,512]{1,0:T(8,128)(2,1)S(1)} %collective-permute-done.5.refs_5_), channel_id=1, source_target_pairs={{0,2},{2,0},{4,6},{6,4},{8,10},{10,8},{12,14},{14,12},{16,18},{18,... | collective-permute-start | bytes 786440 | tf_op jit(solution)/shard_map/w_core/ppermute | solution.py:260
  41.5 1.9 %collective-permute-start.8 = (bf16[256,512]{1,0:T(8,128)(2,1)S(1)}, bf16[256,512]{1,0:T(8,128)(2,1)S(1)}, u32[]{:S(2)}, u32[]{:S(2)}) collective-permute-start(bf16[256,512]{1,0:T(8,128)(2,1)S(1)} %collective-permute-done.4.refs_4_), channel_id=1, source_target_pairs={{0,2},{2,0},{4,6},{6,4},{8,10},{10,8},{12,14},{14,12},{16,18},{18,... | collective-permute-start | bytes 786440 | tf_op jit(solution)/shard_map/w_core/ppermute | solution.py:260
  41.8 0.7 copy-start.12
  42.5 1.5 %collective-permute-start.10 = (bf16[256,512]{1,0:T(8,128)(2,1)S(1)}, bf16[256,512]{1,0:T(8,128)(2,1)S(1)}, u32[]{:S(2)}, u32[]{:S(2)}) collective-permute-start(bf16[256,512]{1,0:T(8,128)(2,1)S(1)} %collective-permute-done.6.refs_6_), channel_id=1, source_target_pairs={{0,2},{2,0},{4,6},{6,4},{8,10},{10,8},{12,14},{14,12},{16,18},{18,... | collective-permute-start | bytes 786440 | tf_op jit(solution)/shard_map/w_core/ppermute | solution.py:260
  42.7 0.7 copy-start.14
  44.1 1.0 copy-start.13
  45.0 0.9 copy-start.15
  48.8 19.6 %copy-start.11 = (bf16[128,2048]{1,0:T(8,128)(2,1)}, bf16[128,2048]{1,0:T(8,128)(2,1)S(1)}, u32[]{:S(2)}) copy-start(bf16[128,2048]{1,0:T(8,128)(2,1)S(1)} %get-tuple-element.53) | copy-start | bytes 1572868
  48.8 19.5 %collective-permute-start.11 = (bf16[128,2048]{1,0:T(8,128)(2,1)S(1)}, bf16[128,2048]{1,0:T(8,128)(2,1)S(1)}, u32[]{:S(2)}, u32[]{:S(2)}) collective-permute-start(bf16[128,2048]{1,0:T(8,128)(2,1)S(1)} %get-tuple-element.43), channel_id=1, source_target_pairs={{0,4},{1,5},{2,6},{3,7},{4,0},{5,1},{6,2},{7,3},{8,12},{9,13},{10,... | collective-permute-start | bytes 1572872 | tf_op jit(solution)/shard_map/pieces20/ppermute | solution.py:260
  50.5 17.8 %collective-permute-start.12 = (bf16[128,2048]{1,0:T(8,128)(2,1)S(1)}, bf16[128,2048]{1,0:T(8,128)(2,1)S(1)}, u32[]{:S(2)}, u32[]{:S(2)}) collective-permute-start(bf16[128,2048]{1,0:T(8,128)(2,1)S(1)} %get-tuple-element.44), channel_id=1, source_target_pairs={{0,1},{1,0},{2,3},{3,2},{4,5},{5,4},{6,7},{7,6},{8,9},{9,8},{10,11... | collective-permute-start | bytes 1572872 | tf_op jit(solution)/shard_map/pieces01/ppermute | solution.py:260
  68.3 4.0 %copy-start.4 = (bf16[128,2048]{1,0:T(8,128)(2,1)}, bf16[128,2048]{1,0:T(8,128)(2,1)S(1)}, u32[]{:S(2)}) copy-start(bf16[128,2048]{1,0:T(8,128)(2,1)S(1)} %collective-permute-done.11.refs_1_) | copy-start | bytes 1572868
  68.4 4.0 %copy-start.6 = (bf16[128,2048]{1,0:T(8,128)(2,1)}, bf16[128,2048]{1,0:T(8,128)(2,1)S(1)}, u32[]{:S(2)}) copy-start(bf16[128,2048]{1,0:T(8,128)(2,1)S(1)} %collective-permute-done.12.refs_2_) | copy-start | bytes 1572868
  68.4 2.0 %copy-start.1 = (bf16[128,8192]{1,0:T(8,128)(2,1)S(1)}, bf16[128,8192]{1,0:T(8,128)(2,1)}, u32[]{:S(2)}) copy-start(bf16[128,8192]{1,0:T(8,128)(2,1)} %x.1) | copy-start | bytes 6291460
  72.4 7.5 %copy-start.10 = (s32[16]{0:T(128)S(1)}, s32[16]{0:T(128)}, u32[]{:S(2)}) copy-start(s32[16]{0:T(128)} %table.1) | copy-start | bytes 196
  72.4 33.8 %all-to-all-start.2 = ((bf16[32,144,128]{2,1,0:T(8,128)(2,1)}), bf16[32,144,128]{2,1,0:T(8,128)(2,1)S(1)}, u32[]{:S(2)}, u32[]{:S(2)}) async-start(bf16[32,144,128]{2,1,0:T(8,128)(2,1)} %get-tuple-element.46), calls=%async_computation.2 | async-start | bytes 2359296 | tf_op jit(solution)/shard_map/gradients_back/all_to_all | solution.py:368
  77.1 29.1 %collective-permute-start.14 = (bf16[128,2048]{1,0:T(8,128)(2,1)}, bf16[128,2048]{1,0:T(8,128)(2,1)}, u32[]{:S(2)}, u32[]{:S(2)}) collective-permute-start(bf16[128,2048]{1,0:T(8,128)(2,1)} %copy-done.11), channel_id=1, source_target_pairs={{0,5},{1,4},{2,7},{3,6},{4,1},{5,0},{6,3},{7,2},{8,13},{9,12},{10,... | collective-permute-start | bytes 1572872 | tf_op jit(solution)/shard_map/pieces21/ppermute | solution.py:260
  80.0 24.3 %collective-permute-start.13 = (s32[16]{0:T(128)S(1)}, s32[16]{0:T(128)S(1)}, u32[]{:S(2)}, u32[]{:S(2)}) collective-permute-start(s32[16]{0:T(128)S(1)} %select_reduce_fusion.refs_0_), channel_id=1, source_target_pairs={{0,1},{1,0},{2,3},{3,2},{4,5},{5,4},{6,7},{7,6},{8,9},{9,8},{10,11... | collective-permute-start | bytes 200 | tf_op jit(solution)/shard_map/slots_dp/ppermute | solution.py:260
  106.1 3.6 %copy-start.5 = (bf16[128,2048]{1,0:T(8,128)(2,1)S(1)}, bf16[128,2048]{1,0:T(8,128)(2,1)}, u32[]{:S(2)}) copy-start(bf16[128,2048]{1,0:T(8,128)(2,1)} %copy-done.4) | copy-start | bytes 1572868
  106.2 3.6 %copy-start.7 = (bf16[128,2048]{1,0:T(8,128)(2,1)S(1)}, bf16[128,2048]{1,0:T(8,128)(2,1)}, u32[]{:S(2)}) copy-start(bf16[128,2048]{1,0:T(8,128)(2,1)} %copy-done.6) | copy-start | bytes 1572868
  108.2 8.0 %collective-permute-start.15 = (bf16[8,64,256]{2,1,0:T(8,128)(2,1)S(1)}, bf16[8,64,256]{2,1,0:T(8,128)(2,1)S(1)}, u32[]{:S(2)}, u32[]{:S(2)}) collective-permute-start(bf16[8,64,256]{2,1,0:T(8,128)(2,1)S(1)} %get-tuple-element.55), channel_id=1, source_target_pairs={{0,1},{1,0},{2,3},{3,2},{4,5},{5,4},{6,7},{7,6},{8,9},{9,8},{10,11... | collective-permute-start | bytes 786440 | tf_op jit(solution)/shard_map/grads_dp/ppermute | solution.py:260

commit v4 on v3

--- a/solution.py
+++ b/solution.py
@@ -64,26 +64,33 @@
     )
 
 
-def select_kernel(dp_count, ids, table, *refs):
-    downs, ups, out = refs[:dp_count], refs[dp_count : 2 * dp_count], refs[-1]
+def select_kernel(dp_count, slots, *refs):
+    downs, ups, (out, held, sems) = (
+        refs[:dp_count], refs[dp_count : 2 * dp_count], refs[2 * dp_count :],
+    )
     own, rank, rows = downs[0].shape
     here = lax.axis_index("dp")
     cut = rows // lanes * rank
 
     @pl.loop(0, out.shape[0])
     def _(k):
-        slot = table[ids[k]]
-        place = slot % own
-        step = (slot // own) ^ here
+        place = slots[k] % own
+        step = (slots[k] // own) ^ here
         for j in range(dp_count):
 
             @pl.when(step == j)
             def _():
                 for c in range(rows // lanes):
-                    out[k, c * rank : (c + 1) * rank, :] = downs[j][
+                    held[k, c * rank : (c + 1) * rank, :] = downs[j][
                         place, :, c * lanes : (c + 1) * lanes
                     ]
-                out[k, cut:, :] = pack_up(ups[j][place])
+                held[k, cut:, :] = pack_up(ups[j][place])
+
+        pltpu.make_async_copy(held.at[k], out.at[k], sems.at[k]).start()
+
+    @pl.loop(0, out.shape[0])
+    def _(k):
+        pltpu.make_async_copy(held.at[k], out.at[k], sems.at[k]).wait()
 
 
 def middle_kernel(kv_rows, rank, halves, x, g, got, hidden_out, back, out, up_out, sems):
@@ -165,12 +172,12 @@
             ).astype(BF16)
 
 
-def sort_kernel(dp_count, own, ids, table, got, *sends):
+def sort_kernel(dp_count, own, slots, got, *sends):
     here = lax.axis_index("dp")
 
     @pl.loop(0, got.shape[0])
     def _(k):
-        slot = table[ids[k]]
+        slot = slots[k]
         place = slot % own
         step = (slot // own) ^ here
         for j in range(1, dp_count):
@@ -180,7 +187,7 @@
                 sends[j - 1][place] = got[k]
 
 
-def sum_kernel(dp_count, kv_rows, ids, table, got, *refs):
+def sum_kernel(dp_count, kv_rows, slots, got, *refs):
     received, (down, up) = refs[: dp_count - 1], refs[dp_count - 1 :]
     own, rank, rows = down.shape
     here = lax.axis_index("dp")
@@ -188,7 +195,7 @@
 
     @pl.loop(0, got.shape[0])
     def _(k):
-        slot = table[ids[k]]
+        slot = slots[k]
         place = slot % own
 
         @pl.when(slot // own == here)
@@ -202,11 +209,9 @@
             up[place] = unpack_up(total[tiles * rank :], kv_rows, rank)
 
 
-def sum_halves_kernel(dp_count, kv_rows, *refs):
-    slots, got, (own_down, *sends, up, place_of) = (
-        refs[:dp_count], refs[dp_count], refs[dp_count + 1 :],
-    )
-    own, rank, width = own_down.shape
+def sum_halves_kernel(dp_count, kv_rows, first, steps, *refs):
+    slots, got, outs, place_of = refs[:dp_count], refs[dp_count], refs[dp_count + 1 : -1], refs[-1]
+    own, rank, width = outs[0].shape
     tiles = width // lanes
     here = lax.axis_index("dp")
 
@@ -215,7 +220,7 @@
         for j in range(dp_count):
             place_of[j, slots[j][k]] = k * dp_count + (here ^ j)
 
-    for step, out in enumerate([own_down, *sends]):
+    for step, out in zip(range(first, first + steps), outs):
 
         @pl.loop(0, own)
         def _(place):
@@ -227,7 +232,7 @@
             for c in range(tiles):
                 out[place, :, c * lanes : (c + 1) * lanes] = total[c * rank : (c + 1) * rank]
             if step == 0:
-                up[place] = unpack_up(total[tiles * rank :], kv_rows, rank)
+                outs[-1][place] = unpack_up(total[tiles * rank :], kv_rows, rank)
 
 
 def join_kernel(dp_count, *refs):
@@ -295,27 +300,35 @@
     ws = [w_here] + [None] * (layers - 1)
     for bit in bits(layers):
         ws[bit] = exchange("w_layers", w_here, "fsdp", bit * inner_count)
-    gs, g_counts, rels, held = [grad_value], [1], [(0, 0)], grad_value
+    gs, rels = [grad_value], [(0, 0)]
     stages = [("fsdp", bit) for bit in bits(inner_count)[1:]] + [("dp", bit) for bit in bits(split)]
-    for n, (axis, bit) in enumerate(stages):
-        new = exchange("g_" + axis, held, axis, bit)
-        gs, g_counts = gs + [new], g_counts + [len(rels)]
+    for axis, bit in stages:
+        gs = gs + [exchange("g_" + axis, g, axis, bit) for g in gs]
         rels = rels + [(i | bit, d) if axis == "fsdp" else (i, d | bit) for i, d in rels]
-        if n + 1 < len(stages):
-            held = jnp.concatenate([held, new], axis=0)
-    ids, downs, ups, gs = lax.optimization_barrier((ids, downs, ups, gs))
+    g_counts = [1] * len(rels)
+    ids, downs, ups, ws, gs[1] = lax.optimization_barrier((ids, downs, ups, ws, gs[1]))
 
     box = jax.ShapeDtypeStruct((fsdp_count, tall, lanes), BF16)
     box_bytes = 2 * fsdp_count * tall * lanes
+    slots = jnp.sum(
+        jnp.where(
+            ids[:, None] == jnp.arange(slot_table.shape[0])[None, :], slot_table[None, :], 0
+        ),
+        axis=1,
+    )
+    ups[0] = pltpu.with_memory_space_constraint(ups[0], pltpu.HBM)
     sent = pl.pallas_call(
         functools.partial(select_kernel, dp_count),
-        out_shape=box,
-        in_specs=smem(2) + vmem(2 * dp_count),
-        out_specs=pl.BlockSpec(memory_space=pltpu.VMEM),
+        out_shape=pltpu.HBM(box.shape, BF16),
+        in_specs=smem(1) + vmem(2 * dp_count),
+        out_specs=pl.BlockSpec(memory_space=pltpu.HBM),
+        scratch_shapes=[
+            pltpu.VMEM(box.shape, BF16), pltpu.SemaphoreType.DMA((fsdp_count,)),
+        ],
         compiler_params=params(),
         cost_estimate=cost(0, 2 * box_bytes),
         name="select",
-    )(ids, slot_table, *downs, *ups)
+    )(slots, *downs, *ups)
     with jax.named_scope("adapters_to_blocks"):
         got = lax.all_to_all(sent, "fsdp", 0, 0, tiled=True)
     for bit in reversed(bits(layers)):
@@ -331,7 +344,7 @@
         out_specs=vmem(len(rels)),
         compiler_params=params(),
         cost_estimate=cost(
-            12 * 2 * tokens * width * kv_width, 12 * 4 * tokens * width
+            base_weight * 2 * tokens * width * kv_width, base_weight * 4 * tokens * width
         ),
         name="base",
     )(*gs, *ws)
@@ -367,12 +380,6 @@
         axes = "fsdp" if halves == 1 else ("fsdp", "dp")
         returned = lax.all_to_all(back, axes, 0, 0, tiled=True)
     if halves > 1:
-        slots = jnp.sum(
-            jnp.where(
-                ids[:, None] == jnp.arange(slot_table.shape[0])[None, :], slot_table[None, :], 0
-            ),
-            axis=1,
-        )
         all_slots = [slots] + [exchange("slots_dp", slots, "dp", j) for j in range(1, dp_count)]
         returned, all_slots = lax.optimization_barrier((returned, all_slots))
     returned, pieces = lax.optimization_barrier((returned, pieces))
@@ -389,19 +396,24 @@
 
     if halves > 1:
         part = (own, rank, rows // halves)
-        *sums, grad_up = pl.pallas_call(
-            functools.partial(sum_halves_kernel, dp_count, kv_rows),
-            out_shape=[jax.ShapeDtypeStruct(part, BF16)] * dp_count
-            + [jax.ShapeDtypeStruct(adapter_up.shape, BF16)],
-            in_specs=smem(dp_count) + vmem(1),
-            out_specs=vmem(dp_count + 1),
-            scratch_shapes=[pltpu.SMEM((dp_count, own * dp_count), jnp.int32)],
-            compiler_params=params(),
-            cost_estimate=cost(0, 2 * box_bytes),
-            name="sum_halves",
-        )(*all_slots, returned)
+
+        def sum_halves(first, steps, extra, name):
+            return pl.pallas_call(
+                functools.partial(sum_halves_kernel, dp_count, kv_rows, first, steps),
+                out_shape=[jax.ShapeDtypeStruct(shape, BF16) for shape in [part] * steps + extra],
+                in_specs=smem(dp_count) + vmem(1),
+                out_specs=vmem(steps + len(extra)),
+                scratch_shapes=[pltpu.SMEM((dp_count, own * dp_count), jnp.int32)],
+                compiler_params=params(),
+                cost_estimate=cost(0, 2 * box_bytes),
+                name=name,
+            )(*all_slots, returned)
+
+        *sums, grad_up = sum_halves(0, dp_count, [adapter_up.shape], "sum_all")
         received = [exchange("grads_dp", s, "dp", j) for j, s in enumerate(sums[1:], 1)]
-        received, input_gradient_rows = lax.optimization_barrier((received, input_gradient_rows))
+        received, input_gradient_rows, sums[0], grad_up = lax.optimization_barrier(
+            (received, input_gradient_rows, sums[0], grad_up)
+        )
         grad_down_t = pl.pallas_call(
             functools.partial(join_kernel, dp_count),
             out_shape=jax.ShapeDtypeStruct((own, rank, rows), BF16),
@@ -415,12 +427,12 @@
         sends = pl.pallas_call(
             functools.partial(sort_kernel, dp_count, own),
             out_shape=[jax.ShapeDtypeStruct((own, tall, lanes), BF16)] * (dp_count - 1),
-            in_specs=smem(2) + vmem(1),
+            in_specs=smem(1) + vmem(1),
             out_specs=vmem(dp_count - 1),
             compiler_params=params(),
             cost_estimate=cost(0, 2 * box_bytes),
             name="sort",
-        )(ids, slot_table, returned)
+        )(slots, returned)
         received = [
             exchange("grads_dp", s, "dp", j + 1) for j, s in enumerate(sends)
         ]
@@ -431,12 +443,12 @@
                 jax.ShapeDtypeStruct((own, rank, rows), BF16),
                 jax.ShapeDtypeStruct(adapter_up.shape, BF16),
             ],
-            in_specs=smem(2) + vmem(dp_count),
+            in_specs=smem(1) + vmem(dp_count),
             out_specs=vmem(2),
             compiler_params=params(),
             cost_estimate=cost(0, 2 * box_bytes),
             name="sums",
-        )(ids, slot_table, returned, *received)
+        )(slots, returned, *received)
 
     return (input_gradient_rows, grad_down_t.transpose(0, 2, 1), grad_up)
 

time: 118 us -> 109 us (0.924)
  local copies, waits for them, and re-layouts: 7.78 us -> 4.03 us
  waiting for transfers between devices: 58.8 us -> 55.2 us
    unnamed x32 -> x18, local copies, waits for them, and re-layouts: 6.78 us -> 3.03 us
    ppermute x16 -> x17, waiting for transfers between devices: 51.6 us -> 48.1 us  [exchange(): return lax.ppermute(array, axis, xor_pairs(axis_count(axis), bits))]
    concatenate x1 -> x0, other arithmetic: 1.62 us -> none  [on_device(): held = jnp.concatenate([held, new], axis=0)]
    all_to_all x1, starting transfers between devices: 4.82 us -> 3.47 us  [on_device(): lax.all_to_all(jnp.broadcast_to(tenant_ids[:, None, None], (fsdp_count, 1...]
    ppermute x16 -> x17, starting transfers between devices: 20.3 us -> 21 us  [exchange(): return lax.ppermute(array, axis, xor_pairs(axis_count(axis), bits))]
  transfers between devices with their start and end apart: 19 -> 20, of which waited for: 7 -> 7; matrix products, arithmetic and copies ran while one was open for 2% -> 2% of each run, Pallas kernels for 7% -> 8%
where the time goes in v4:
time: 109 us
  waiting for transfers between devices  55.2 us (51%)
  starting transfers between devices  33.7 us (31%)
  Pallas kernels  13.6 us (12%)
  local copies, waits for them, and re-layouts  4.03 us (4%)
  between operations  1.48 us (1%)
    ppermute x17, waiting for transfers between devices, exchange(): return lax.ppermute(array, axis, xor_pairs(axis_count(axis), bits))  48.1 us
    ppermute x17, starting transfers between devices, exchange(): return lax.ppermute(array, axis, xor_pairs(axis_count(axis), bits))  21 us
    all_to_all x1, starting transfers between devices, on_device(): returned = lax.all_to_all(back, axes, 0, 0, tiled=True)  5.27 us
    all_to_all x1, waiting for transfers between devices, on_device(): lax.all_to_all(jnp.broadcast_to(tenant_ids[:, None, None], (fsdp_count, 1...  5.26 us
    all_to_all x1, starting transfers between devices, on_device(): got = lax.all_to_all(sent, 'fsdp', 0, 0, tiled=True)  3.95 us
    all_to_all x1, starting transfers between devices, on_device(): lax.all_to_all(jnp.broadcast_to(tenant_ids[:, None, None], (fsdp_count, 1...  3.47 us
    pallas_call x1, Pallas kernels, on_device(): pl.pallas_call(functools.partial(out_kernel, rels, layers, inner_count, s...  3.11 us
    unnamed x18, local copies, waits for them, and re-layouts  3.03 us
  transfers between devices with their start and end apart: 20, of which 7 were waited for; matrix products, arithmetic and copies ran while one was open for 2% of the time, Pallas kernels for 8%

profile of v4, /device:TPU:0, one launch (start us, length us, event | category | flops | bytes accessed | tf_op | source)
XLA Modules:
  0.0 108.9 jit_solution(4471625528220211661)
XLA Ops:
  0.6 0.0 copy-start
  0.6 3.0 %collective-permute-start = (bf16[8,64,512]{2,1,0:T(8,128)(2,1)}, bf16[8,64,512]{2,1,0:T(8,128)(2,1)S(1)}, u32[]{:S(2)}, u32[]{:S(2)}) collective-permute-start(bf16[8,64,512]{2,1,0:T(8,128)(2,1)} %bitcast.4), channel_id=1, source_target_pairs={{0,1},{1,0},{2,3},{3,2},{4,5},{5,4},{6,7},{7,6},{8,9},{9,8},{10,11... | collective-permute-start | bytes 1572872 | tf_op jit(solution)/shard_map/down_dp/ppermute | solution.py:265
  3.7 2.7 %collective-permute-start.3 = (bf16[256,512]{1,0:T(8,128)(2,1)S(1)}, bf16[256,512]{1,0:T(8,128)(2,1)S(1)}, u32[]{:S(2)}, u32[]{:S(2)}) collective-permute-start(bf16[256,512]{1,0:T(8,128)(2,1)S(1)} %constant_dynamic-slice_fusion.refs_4_), channel_id=1, source_target_pairs={{0,16},{2,18},{4,20},{6,22},{8,24},{10,26},{12,28},{14,30},{16,0},... | collective-permute-start | bytes 786440 | tf_op jit(solution)/shard_map/w_layers/ppermute | solution.py:265
  6.3 1.6 %collective-permute-start.2 = (bf16[256,512]{1,0:T(8,128)(2,1)S(1)}, bf16[256,512]{1,0:T(8,128)(2,1)S(1)}, u32[]{:S(2)}, u32[]{:S(2)}) collective-permute-start(bf16[256,512]{1,0:T(8,128)(2,1)S(1)} %constant_dynamic-slice_fusion.refs_4_), channel_id=1, source_target_pairs={{0,8},{2,10},{4,12},{6,14},{8,0},{10,2},{12,4},{14,6},{16,24},{18,... | collective-permute-start | bytes 786440 | tf_op jit(solution)/shard_map/w_layers/ppermute | solution.py:265
  7.9 1.5 %collective-permute-start.4 = (bf16[128,512]{1,0:T(8,128)(2,1)}, bf16[128,512]{1,0:T(8,128)(2,1)S(1)}, u32[]{:S(2)}, u32[]{:S(2)}) collective-permute-start(bf16[128,512]{1,0:T(8,128)(2,1)} %g.1), channel_id=1, source_target_pairs={{0,4},{2,6},{4,0},{6,2},{8,12},{10,14},{12,8},{14,10},{16,20},{18,... | collective-permute-start | bytes 393224 | tf_op jit(solution)/shard_map/g_fsdp/ppermute | solution.py:265
  10.1 0.6 broadcast_in_dim.24
  10.7 3.5 %all-to-all-start = ((s32[16,1,128]{2,1,0:T(1,128)}), s32[16,1,128]{2,1,0:T(1,128)S(1)}, u32[]{:S(2)}, u32[]{:S(2)}) async-start(s32[16,1,128]{2,1,0:T(1,128)} %broadcast_in_dim.24), calls=%async_computation | async-start | bytes 16384 | tf_op jit(solution)/shard_map/ids/all_to_all | solution.py:295
  14.2 1.0 collective-permute-start.1
  15.2 5.3 %all-to-all-done = s32[16,1,128]{2,1,0:T(1,128)S(1)} async-done(((s32[16,1,128]{2,1,0:T(1,128)}), s32[16,1,128]{2,1,0:T(1,128)S(1)}, u32[]{:S(2)}, u32[]{:S(2)}) %all-to-all-start) | async-done | bytes 8224 | tf_op jit(solution)/shard_map/ids/all_to_all | solution.py:295
  20.5 0.4 slice_reduce_fusion
  20.8 0.0 collective-permute-done.1.refs_3_
  20.8 0.0 collective-permute-done.4.refs_1_
  20.9 0.0 collective-permute-done.3.refs_6_
  20.9 0.6 collective-permute-start.7
  21.5 0.8 select_reduce_fusion.slots.refs_0_
  22.3 1.0 copy-done.2
  23.3 2.8 %select.3 = bf16[16,272,128]{2,1,0:T(8,128)(2,1)} custom-call(s32[16]{0:T(128)S(1)} %select_reduce_fusion.slots.refs_0_, bf16[8,64,512]{2,1,0:T(8,128)(2,1)S(1)} %bitcast.5, bf16[8,64,512]{2,1,0:T(8,128)(2,1)S(1)} %collective-permute-done.refs_1_, bf16[8,32,64]{2,1,0:T(8,128)(2,1)} %refs_2_, bf16[8,32,64]{2,1,0:T(8,128)(2,1)S(1)} %collective-permute-done.1.refs_3_), custom_call_target="tpu_custom_call" | custom-call | bytes 2228224 | tf_op jit(solution)/shard_map/select/pallas_call | solution.py:320
  26.1 0.0 copy-start.7
  26.1 3.9 %all-to-all-start.1 = ((bf16[16,272,128]{2,1,0:T(8,128)(2,1)}), bf16[16,272,128]{2,1,0:T(8,128)(2,1)S(1)}, u32[]{:S(2)}, u32[]{:S(2)}) async-start(bf16[16,272,128]{2,1,0:T(8,128)(2,1)} %select.3), calls=%async_computation.1 | async-start | bytes 2228224 | tf_op jit(solution)/shard_map/adapters_to_blocks/all_to_all | solution.py:333
  30.1 1.1 %collective-permute-start.5 = (bf16[128,512]{1,0:T(8,128)(2,1)S(1)}, bf16[128,512]{1,0:T(8,128)(2,1)S(1)}, u32[]{:S(2)}, u32[]{:S(2)}) collective-permute-start(bf16[128,512]{1,0:T(8,128)(2,1)S(1)} %copy-done.7), channel_id=1, source_target_pairs={{0,1},{1,0},{2,3},{3,2},{4,5},{5,4},{6,7},{7,6},{8,9},{9,8},{10,11... | collective-permute-start | bytes 393224 | tf_op jit(solution)/shard_map/g_dp/ppermute | solution.py:265
  31.2 0.1 collective-permute-start.10
  31.4 0.4 collective-permute-start.8
  31.7 0.1 collective-permute-start.9
  31.9 0.0 collective-permute-done.7.refs_7_
  31.9 0.4 collective-permute-start.11
  32.3 3.8 %collective-permute-done.5.refs_2_ = bf16[128,512]{1,0:T(8,128)(2,1)S(1)} collective-permute-done((bf16[128,512]{1,0:T(8,128)(2,1)S(1)}, bf16[128,512]{1,0:T(8,128)(2,1)S(1)}, u32[]{:S(2)}, u32[]{:S(2)}) %collective-permute-start.5) | collective-permute-done | bytes 131104 | tf_op jit(solution)/shard_map/g_dp/ppermute | solution.py:265
  36.0 1.0 collective-permute-start.6
  37.1 4.0 %collective-permute-done.6.refs_3_ = bf16[128,512]{1,0:T(8,128)(2,1)S(1)} collective-permute-done((bf16[128,512]{1,0:T(8,128)(2,1)S(1)}, bf16[128,512]{1,0:T(8,128)(2,1)S(1)}, u32[]{:S(2)}, u32[]{:S(2)}) %collective-permute-start.6) | collective-permute-done | bytes 131104 | tf_op jit(solution)/shard_map/g_dp/ppermute | solution.py:265
  41.1 0.0 collective-permute-done.10.refs_10_
  41.1 0.0 collective-permute-done.11.refs_11_
  41.1 2.8 %base.1 = (bf16[128,2048]{1,0:T(8,128)(2,1)S(1)}, bf16[128,2048]{1,0:T(8,128)(2,1)S(1)}, bf16[128,2048]{1,0:T(8,128)(2,1)S(1)}, bf16[128,2048]{1,0:T(8,128)(2,1)S(1)}) custom-call(bf16[128,512]{1,0:T(8,128)(2,1)S(1)} %copy-done.7, bf16[128,512]{1,0:T(8,128)(2,1)S(1)} %collective-permute-done.4.refs_1_, bf16[128,512]{1,0:T(8,128)(2,1)S(1)} %collective-permute-done.5.refs_2_, ...), custom_call_target="tpu_custom_call" | custom-call | flops 11811160064 | bytes 46137344 | tf_op jit(solution)/shard_map/base/pallas_call | solution.py:340
  43.9 1.6 %collective-permute-start.12 = (bf16[128,2048]{1,0:T(8,128)(2,1)S(1)}, bf16[128,2048]{1,0:T(8,128)(2,1)S(1)}, u32[]{:S(2)}, u32[]{:S(2)}) collective-permute-start(bf16[128,2048]{1,0:T(8,128)(2,1)S(1)} %get-tuple-element.47), channel_id=1, source_target_pairs={{0,4},{1,5},{2,6},{3,7},{4,0},{5,1},{6,2},{7,3},{8,12},{9,13},{10,... | collective-permute-start | bytes 1572872 | tf_op jit(solution)/shard_map/pieces20/ppermute | solution.py:265
  45.5 1.1 collective-permute-start.13
  46.6 13.1 %collective-permute-done.12.refs_1_ = bf16[128,2048]{1,0:T(8,128)(2,1)S(1)} collective-permute-done((bf16[128,2048]{1,0:T(8,128)(2,1)S(1)}, bf16[128,2048]{1,0:T(8,128)(2,1)S(1)}, u32[]{:S(2)}, u32[]{:S(2)}) %collective-permute-start.12) | collective-permute-done | bytes 524320 | tf_op jit(solution)/shard_map/pieces20/ppermute | solution.py:265
  59.7 0.0 collective-permute-done.13.refs_2_
  59.7 0.0 copy-start.1
  59.7 1.9 %copy-done.1 = bf16[128,8192]{1,0:T(8,128)(2,1)S(1)} copy-done((bf16[128,8192]{1,0:T(8,128)(2,1)S(1)}, bf16[128,8192]{1,0:T(8,128)(2,1)}, u32[]{:S(2)}) %copy-start.1) | copy-done | bytes 2097176
  61.7 2.0 %middle.1 = (bf16[128,64]{1,0:T(8,128)(2,1)S(1)}, bf16[32,144,128]{2,1,0:T(8,128)(2,1)}) custom-call(bf16[128,8192]{1,0:T(8,128)(2,1)S(1)} %copy-done.1, bf16[128,512]{1,0:T(8,128)(2,1)S(1)} %copy-done.7, bf16[16,272,128]{2,1,0:T(8,128)(2,1)S(1)} %all-to-all-done.1.got), custom_call_target="tpu_custom_call" | custom-call | flops 268435456 | bytes 4325376 | tf_op jit(solution)/shard_map/middle/pallas_call | solution.py:362
  63.7 5.3 %all-to-all-start.2 = ((bf16[32,144,128]{2,1,0:T(8,128)(2,1)}), bf16[32,144,128]{2,1,0:T(8,128)(2,1)S(1)}, u32[]{:S(2)}, u32[]{:S(2)}) async-start(bf16[32,144,128]{2,1,0:T(8,128)(2,1)} %get-tuple-element.50), calls=%async_computation.2 | async-start | bytes 2359296 | tf_op jit(solution)/shard_map/gradients_back/all_to_all | solution.py:381
  69.0 2.7 %collective-permute-start.15 = (bf16[128,2048]{1,0:T(8,128)(2,1)}, bf16[128,2048]{1,0:T(8,128)(2,1)}, u32[]{:S(2)}, u32[]{:S(2)}) collective-permute-start(bf16[128,2048]{1,0:T(8,128)(2,1)} %copy-done.8), channel_id=1, source_target_pairs={{0,5},{1,4},{2,7},{3,6},{4,1},{5,0},{6,3},{7,2},{8,13},{9,12},{10,... | collective-permute-start | bytes 1572872 | tf_op jit(solution)/shard_map/pieces21/ppermute | solution.py:265
  71.8 0.6 collective-permute-start.14
  72.3 23.9 %collective-permute-done.14.refs_1_ = s32[16]{0:T(128)S(1)} collective-permute-done((s32[16]{0:T(128)S(1)}, s32[16]{0:T(128)S(1)}, u32[]{:S(2)}, u32[]{:S(2)}) %collective-permute-start.14) | collective-permute-done | bytes 96 | tf_op jit(solution)/shard_map/slots_dp/ppermute | solution.py:265
  96.2 1.8 %all-to-all-done.2.refs_2_ = bf16[32,144,128]{2,1,0:T(8,128)(2,1)S(1)} async-done(((bf16[32,144,128]{2,1,0:T(8,128)(2,1)}), bf16[32,144,128]{2,1,0:T(8,128)(2,1)S(1)}, u32[]{:S(2)}, u32[]{:S(2)}) %all-to-all-start.2) | async-done | bytes 1179680 | tf_op jit(solution)/shard_map/gradients_back/all_to_all | solution.py:381
  98.1 2.0 %sum_all.1 = (bf16[8,64,256]{2,1,0:T(8,128)(2,1)S(1)}, bf16[8,64,256]{2,1,0:T(8,128)(2,1)S(1)}, bf16[8,32,64]{2,1,0:T(8,128)(2,1)}) custom-call(s32[16]{0:T(128)S(1)} %select_reduce_fusion.slots.refs_0_, s32[16]{0:T(128)S(1)} %collective-permute-done.14.refs_1_, bf16[32,144,128]{2,1,0:T(8,128)(2,1)S(1)} %all-to-all-done.2.refs_2_), custom_call_target="tpu_custom_call" | custom-call | bytes 2228224 | tf_op jit(solution)/shard_map/sum_all/pallas_call | solution.py:401
  100.1 1.5 %collective-permute-start.16 = (bf16[8,64,256]{2,1,0:T(8,128)(2,1)S(1)}, bf16[8,64,256]{2,1,0:T(8,128)(2,1)S(1)}, u32[]{:S(2)}, u32[]{:S(2)}) collective-permute-start(bf16[8,64,256]{2,1,0:T(8,128)(2,1)S(1)} %get-tuple-element.59), channel_id=1, source_target_pairs={{0,1},{1,0},{2,3},{3,2},{4,5},{5,4},{6,7},{7,6},{8,9},{9,8},{10,11... | collective-permute-start | bytes 786440 | tf_op jit(solution)/shard_map/grads_dp/ppermute | solution.py:265
  101.6 3.1 %rows.1 = bf16[128,8192]{1,0:T(8,128)(2,1)} custom-call(bf16[128,64]{1,0:T(8,128)(2,1)S(1)} %get-tuple-element.60.hidden, bf16[16,272,128]{2,1,0:T(8,128)(2,1)S(1)} %all-to-all-done.1.got, bf16[128,2048]{1,0:T(8,128)(2,1)S(1)} %get-tuple-element.61.refs_0_, bf16[128,2048]{1,0:T(8,128)(2,1)S(1)} %copy-done.4, bf16[128,2048]{1,0:T(8,128)(2,1)S(1)} %copy-done.6, ...), custom_call_target="tpu_custom_call" | custom-call | flops 134217728 | bytes 5308416 | tf_op jit(solution)/shard_map/rows/pallas_call | solution.py:387
  104.7 3.3 %collective-permute-done.16.refs_1_ = bf16[8,64,256]{2,1,0:T(8,128)(2,1)S(1)} collective-permute-done((bf16[8,64,256]{2,1,0:T(8,128)(2,1)S(1)}, bf16[8,64,256]{2,1,0:T(8,128)(2,1)S(1)}, u32[]{:S(2)}, u32[]{:S(2)}) %collective-permute-start.16) | collective-permute-done | bytes 262176 | tf_op jit(solution)/shard_map/grads_dp/ppermute | solution.py:265
  108.1 0.8 join.1
  (20 shorter events, 0.1 us)
Async XLA Ops:
  0.6 3.0 %copy-start = (bf16[512,512]{1,0:T(8,128)(2,1)S(1)}, bf16[512,512]{1,0:T(8,128)(2,1)}, u32[]{:S(2)}) copy-start(bf16[512,512]{1,0:T(8,128)(2,1)} %param.9) | copy-start | bytes 1572868
  0.6 20.2 %collective-permute-start = (bf16[8,64,512]{2,1,0:T(8,128)(2,1)}, bf16[8,64,512]{2,1,0:T(8,128)(2,1)S(1)}, u32[]{:S(2)}, u32[]{:S(2)}) collective-permute-start(bf16[8,64,512]{2,1,0:T(8,128)(2,1)} %bitcast.4), channel_id=1, source_target_pairs={{0,1},{1,0},{2,3},{3,2},{4,5},{5,4},{6,7},{7,6},{8,9},{9,8},{10,11... | collective-permute-start | bytes 1572872 | tf_op jit(solution)/shard_map/down_dp/ppermute | solution.py:265
  3.7 17.2 %collective-permute-start.3 = (bf16[256,512]{1,0:T(8,128)(2,1)S(1)}, bf16[256,512]{1,0:T(8,128)(2,1)S(1)}, u32[]{:S(2)}, u32[]{:S(2)}) collective-permute-start(bf16[256,512]{1,0:T(8,128)(2,1)S(1)} %constant_dynamic-slice_fusion.refs_4_), channel_id=1, source_target_pairs={{0,16},{2,18},{4,20},{6,22},{8,24},{10,26},{12,28},{14,30},{16,0},... | collective-permute-start | bytes 786440 | tf_op jit(solution)/shard_map/w_layers/ppermute | solution.py:265
  6.3 14.5 %collective-permute-start.2 = (bf16[256,512]{1,0:T(8,128)(2,1)S(1)}, bf16[256,512]{1,0:T(8,128)(2,1)S(1)}, u32[]{:S(2)}, u32[]{:S(2)}) collective-permute-start(bf16[256,512]{1,0:T(8,128)(2,1)S(1)} %constant_dynamic-slice_fusion.refs_4_), channel_id=1, source_target_pairs={{0,8},{2,10},{4,12},{6,14},{8,0},{10,2},{12,4},{14,6},{16,24},{18,... | collective-permute-start | bytes 786440 | tf_op jit(solution)/shard_map/w_layers/ppermute | solution.py:265
  7.9 12.9 %collective-permute-start.4 = (bf16[128,512]{1,0:T(8,128)(2,1)}, bf16[128,512]{1,0:T(8,128)(2,1)S(1)}, u32[]{:S(2)}, u32[]{:S(2)}) collective-permute-start(bf16[128,512]{1,0:T(8,128)(2,1)} %g.1), channel_id=1, source_target_pairs={{0,4},{2,6},{4,0},{6,2},{8,12},{10,14},{12,8},{14,10},{16,20},{18,... | collective-permute-start | bytes 393224 | tf_op jit(solution)/shard_map/g_fsdp/ppermute | solution.py:265
  10.7 9.8 %all-to-all-start = ((s32[16,1,128]{2,1,0:T(1,128)}), s32[16,1,128]{2,1,0:T(1,128)S(1)}, u32[]{:S(2)}, u32[]{:S(2)}) async-start(s32[16,1,128]{2,1,0:T(1,128)} %broadcast_in_dim.24), calls=%async_computation | async-start | bytes 16384 | tf_op jit(solution)/shard_map/ids/all_to_all | solution.py:295
  14.2 6.7 %collective-permute-start.1 = (bf16[8,32,64]{2,1,0:T(8,128)(2,1)}, bf16[8,32,64]{2,1,0:T(8,128)(2,1)S(1)}, u32[]{:S(2)}, u32[]{:S(2)}) collective-permute-start(bf16[8,32,64]{2,1,0:T(8,128)(2,1)} %refs_2_), channel_id=1, source_target_pairs={{0,1},{1,0},{2,3},{3,2},{4,5},{5,4},{6,7},{7,6},{8,9},{9,8},{10,11... | collective-permute-start | bytes 98312 | tf_op jit(solution)/shard_map/up_dp/ppermute | solution.py:265
  20.9 11.0 %collective-permute-start.7 = (bf16[256,512]{1,0:T(8,128)(2,1)S(1)}, bf16[256,512]{1,0:T(8,128)(2,1)S(1)}, u32[]{:S(2)}, u32[]{:S(2)}) collective-permute-start(bf16[256,512]{1,0:T(8,128)(2,1)S(1)} %collective-permute-done.3.refs_6_), channel_id=1, source_target_pairs={{0,8},{2,10},{4,12},{6,14},{8,0},{10,2},{12,4},{14,6},{16,24},{18,... | collective-permute-start | bytes 786440 | tf_op jit(solution)/shard_map/w_last/ppermute | solution.py:265
  22.3 1.0 copy-start.2
  26.1 4.0 %copy-start.7 = (bf16[128,512]{1,0:T(8,128)(2,1)S(1)}, bf16[128,512]{1,0:T(8,128)(2,1)}, u32[]{:S(2)}) copy-start(bf16[128,512]{1,0:T(8,128)(2,1)} %g.1) | copy-start | bytes 393220
  26.1 33.6 %all-to-all-start.1 = ((bf16[16,272,128]{2,1,0:T(8,128)(2,1)}), bf16[16,272,128]{2,1,0:T(8,128)(2,1)S(1)}, u32[]{:S(2)}, u32[]{:S(2)}) async-start(bf16[16,272,128]{2,1,0:T(8,128)(2,1)} %select.3), calls=%async_computation.1 | async-start | bytes 2228224 | tf_op jit(solution)/shard_map/adapters_to_blocks/all_to_all | solution.py:333
  30.1 5.9 %collective-permute-start.5 = (bf16[128,512]{1,0:T(8,128)(2,1)S(1)}, bf16[128,512]{1,0:T(8,128)(2,1)S(1)}, u32[]{:S(2)}, u32[]{:S(2)}) collective-permute-start(bf16[128,512]{1,0:T(8,128)(2,1)S(1)} %copy-done.7), channel_id=1, source_target_pairs={{0,1},{1,0},{2,3},{3,2},{4,5},{5,4},{6,7},{7,6},{8,9},{9,8},{10,11... | collective-permute-start | bytes 393224 | tf_op jit(solution)/shard_map/g_dp/ppermute | solution.py:265
  31.2 9.8 %collective-permute-start.10 = (bf16[256,512]{1,0:T(8,128)(2,1)S(1)}, bf16[256,512]{1,0:T(8,128)(2,1)S(1)}, u32[]{:S(2)}, u32[]{:S(2)}) collective-permute-start(bf16[256,512]{1,0:T(8,128)(2,1)S(1)} %collective-permute-done.3.refs_6_), channel_id=1, source_target_pairs={{0,2},{2,0},{4,6},{6,4},{8,10},{10,8},{12,14},{14,12},{16,18},{18,... | collective-permute-start | bytes 786440 | tf_op jit(solution)/shard_map/w_core/ppermute | solution.py:265
  31.4 9.7 %collective-permute-start.8 = (bf16[256,512]{1,0:T(8,128)(2,1)S(1)}, bf16[256,512]{1,0:T(8,128)(2,1)S(1)}, u32[]{:S(2)}, u32[]{:S(2)}) collective-permute-start(bf16[256,512]{1,0:T(8,128)(2,1)S(1)} %constant_dynamic-slice_fusion.refs_4_), channel_id=1, source_target_pairs={{0,2},{2,0},{4,6},{6,4},{8,10},{10,8},{12,14},{14,12},{16,18},{18,... | collective-permute-start | bytes 786440 | tf_op jit(solution)/shard_map/w_core/ppermute | solution.py:265
  31.7 9.3 %collective-permute-start.9 = (bf16[256,512]{1,0:T(8,128)(2,1)S(1)}, bf16[256,512]{1,0:T(8,128)(2,1)S(1)}, u32[]{:S(2)}, u32[]{:S(2)}) collective-permute-start(bf16[256,512]{1,0:T(8,128)(2,1)S(1)} %collective-permute-done.2.refs_5_), channel_id=1, source_target_pairs={{0,2},{2,0},{4,6},{6,4},{8,10},{10,8},{12,14},{14,12},{16,18},{18,... | collective-permute-start | bytes 786440 | tf_op jit(solution)/shard_map/w_core/ppermute | solution.py:265
  31.9 9.2 %collective-permute-start.11 = (bf16[256,512]{1,0:T(8,128)(2,1)S(1)}, bf16[256,512]{1,0:T(8,128)(2,1)S(1)}, u32[]{:S(2)}, u32[]{:S(2)}) collective-permute-start(bf16[256,512]{1,0:T(8,128)(2,1)S(1)} %collective-permute-done.7.refs_7_), channel_id=1, source_target_pairs={{0,2},{2,0},{4,6},{6,4},{8,10},{10,8},{12,14},{14,12},{16,18},{18,... | collective-permute-start | bytes 786440 | tf_op jit(solution)/shard_map/w_core/ppermute | solution.py:265
  36.0 5.0 %collective-permute-start.6 = (bf16[128,512]{1,0:T(8,128)(2,1)S(1)}, bf16[128,512]{1,0:T(8,128)(2,1)S(1)}, u32[]{:S(2)}, u32[]{:S(2)}) collective-permute-start(bf16[128,512]{1,0:T(8,128)(2,1)S(1)} %collective-permute-done.4.refs_1_), channel_id=1, source_target_pairs={{0,1},{1,0},{2,3},{3,2},{4,5},{5,4},{6,7},{7,6},{8,9},{9,8},{10,11... | collective-permute-start | bytes 393224 | tf_op jit(solution)/shard_map/g_dp/ppermute | solution.py:265
  43.9 15.8 %copy-start.8 = (bf16[128,2048]{1,0:T(8,128)(2,1)}, bf16[128,2048]{1,0:T(8,128)(2,1)S(1)}, u32[]{:S(2)}) copy-start(bf16[128,2048]{1,0:T(8,128)(2,1)S(1)} %get-tuple-element.57) | copy-start | bytes 1572868
  43.9 15.8 %collective-permute-start.12 = (bf16[128,2048]{1,0:T(8,128)(2,1)S(1)}, bf16[128,2048]{1,0:T(8,128)(2,1)S(1)}, u32[]{:S(2)}, u32[]{:S(2)}) collective-permute-start(bf16[128,2048]{1,0:T(8,128)(2,1)S(1)} %get-tuple-element.47), channel_id=1, source_target_pairs={{0,4},{1,5},{2,6},{3,7},{4,0},{5,1},{6,2},{7,3},{8,12},{9,13},{10,... | collective-permute-start | bytes 1572872 | tf_op jit(solution)/shard_map/pieces20/ppermute | solution.py:265
  45.5 14.2 %collective-permute-start.13 = (bf16[128,2048]{1,0:T(8,128)(2,1)S(1)}, bf16[128,2048]{1,0:T(8,128)(2,1)S(1)}, u32[]{:S(2)}, u32[]{:S(2)}) collective-permute-start(bf16[128,2048]{1,0:T(8,128)(2,1)S(1)} %get-tuple-element.48), channel_id=1, source_target_pairs={{0,1},{1,0},{2,3},{3,2},{4,5},{5,4},{6,7},{7,6},{8,9},{9,8},{10,11... | collective-permute-start | bytes 1572872 | tf_op jit(solution)/shard_map/pieces01/ppermute | solution.py:265
  59.7 4.0 %copy-start.3 = (bf16[128,2048]{1,0:T(8,128)(2,1)}, bf16[128,2048]{1,0:T(8,128)(2,1)S(1)}, u32[]{:S(2)}) copy-start(bf16[128,2048]{1,0:T(8,128)(2,1)S(1)} %collective-permute-done.12.refs_1_) | copy-start | bytes 1572868
  59.7 4.0 %copy-start.5 = (bf16[128,2048]{1,0:T(8,128)(2,1)}, bf16[128,2048]{1,0:T(8,128)(2,1)S(1)}, u32[]{:S(2)}) copy-start(bf16[128,2048]{1,0:T(8,128)(2,1)S(1)} %collective-permute-done.13.refs_2_) | copy-start | bytes 1572868
  59.7 2.0 %copy-start.1 = (bf16[128,8192]{1,0:T(8,128)(2,1)S(1)}, bf16[128,8192]{1,0:T(8,128)(2,1)}, u32[]{:S(2)}) copy-start(bf16[128,8192]{1,0:T(8,128)(2,1)} %x.1) | copy-start | bytes 6291460
  63.7 34.3 %all-to-all-start.2 = ((bf16[32,144,128]{2,1,0:T(8,128)(2,1)}), bf16[32,144,128]{2,1,0:T(8,128)(2,1)S(1)}, u32[]{:S(2)}, u32[]{:S(2)}) async-start(bf16[32,144,128]{2,1,0:T(8,128)(2,1)} %get-tuple-element.50), calls=%async_computation.2 | async-start | bytes 2359296 | tf_op jit(solution)/shard_map/gradients_back/all_to_all | solution.py:381
  69.0 29.1 %collective-permute-start.15 = (bf16[128,2048]{1,0:T(8,128)(2,1)}, bf16[128,2048]{1,0:T(8,128)(2,1)}, u32[]{:S(2)}, u32[]{:S(2)}) collective-permute-start(bf16[128,2048]{1,0:T(8,128)(2,1)} %copy-done.8), channel_id=1, source_target_pairs={{0,5},{1,4},{2,7},{3,6},{4,1},{5,0},{6,3},{7,2},{8,13},{9,12},{10,... | collective-permute-start | bytes 1572872 | tf_op jit(solution)/shard_map/pieces21/ppermute | solution.py:265
  71.8 24.5 %collective-permute-start.14 = (s32[16]{0:T(128)S(1)}, s32[16]{0:T(128)S(1)}, u32[]{:S(2)}, u32[]{:S(2)}) collective-permute-start(s32[16]{0:T(128)S(1)} %select_reduce_fusion.slots.refs_0_), channel_id=1, source_target_pairs={{0,1},{1,0},{2,3},{3,2},{4,5},{5,4},{6,7},{7,6},{8,9},{9,8},{10,11... | collective-permute-start | bytes 200 | tf_op jit(solution)/shard_map/slots_dp/ppermute | solution.py:265
  98.1 3.6 %copy-start.4 = (bf16[128,2048]{1,0:T(8,128)(2,1)S(1)}, bf16[128,2048]{1,0:T(8,128)(2,1)}, u32[]{:S(2)}) copy-start(bf16[128,2048]{1,0:T(8,128)(2,1)} %copy-done.3) | copy-start | bytes 1572868
  98.1 3.6 %copy-start.6 = (bf16[128,2048]{1,0:T(8,128)(2,1)S(1)}, bf16[128,2048]{1,0:T(8,128)(2,1)}, u32[]{:S(2)}) copy-start(bf16[128,2048]{1,0:T(8,128)(2,1)} %copy-done.5) | copy-start | bytes 1572868
  100.1 8.0 %collective-permute-start.16 = (bf16[8,64,256]{2,1,0:T(8,128)(2,1)S(1)}, bf16[8,64,256]{2,1,0:T(8,128)(2,1)S(1)}, u32[]{:S(2)}, u32[]{:S(2)}) collective-permute-start(bf16[8,64,256]{2,1,0:T(8,128)(2,1)S(1)} %get-tuple-element.59), channel_id=1, source_target_pairs={{0,1},{1,0},{2,3},{3,2},{4,5},{5,4},{6,7},{7,6},{8,9},{9,8},{10,11... | collective-permute-start | bytes 786440 | tf_op jit(solution)/shard_map/grads_dp/ppermute | solution.py:265

commit v5 on v4

--- a/solution.py
+++ b/solution.py
@@ -138,19 +138,29 @@
         store.wait()
 
 
-def base_kernel(g_counts, w_count, *refs):
-    gs, ws = refs[: len(g_counts)], refs[len(g_counts) : len(g_counts) + w_count]
-    outs = refs[len(g_counts) + w_count :]
-    at = 0
+def base_kernel(rels, near_count, layers, own, *refs):
+    near, refs = refs[:near_count], refs[near_count:]
+    outs, refs = refs[-len(rels) :], refs[: -len(rels)]
+    ws, near_other, others = (
+        refs[: 2 * layers],
+        refs[2 * layers : 2 * layers + near_count],
+        refs[2 * layers + near_count :],
+    )
+    tokens = own.shape[0]
     cols = ws[0].shape[0]
-    for ref, count in zip(gs, g_counts):
-        rows = ref.shape[0] // count
-        for n in range(count):
-            for k in range(w_count):
-                outs[at][:, k * cols : (k + 1) * cols] = dot(
-                    ref[n * rows : (n + 1) * rows, :], ws[k][...], NT
-                ).astype(BF16)
-            at += 1
+    here = [w[...] for w in ws]
+    beside = [ref[tokens:, :] for pair in zip(near, near_other) for ref in pair]
+    gs = [own[...]] + [ref[:tokens, :] for ref in near]
+    gs += [
+        ref[n * tokens : (n + 1) * tokens, :] for ref in others for n in range(near_count + 1)
+    ]
+    for (i, _), g, out in zip(rels, gs, outs):
+        if i == 0:
+            parts = here + beside
+        else:
+            parts = here[1:layers] + here[layers + 1 :]
+        for k, w in enumerate(parts):
+            out[:, k * cols : (k + 1) * cols] = dot(g, w, NT).astype(BF16)
 
 
 def out_kernel(rels, layers, inner_count, split, rows, rank, hidden, got, *refs):
@@ -160,12 +170,14 @@
     cols = rows // split
     tiles = cols // lanes
     h = hidden[...]
+    far = [k * inner_count + core for core in range(2) for k in range(1, layers)]
+    every = [k * inner_count + core for core in range(2) for k in range(layers)]
+    every += [i + core for i in range(2, inner_count, 2) for core in range(2)]
     for (i_rel, d_rel), piece in zip(rels, pieces):
         d = d_here ^ d_rel
-        for k in range(2 * layers):
-            f = f_here ^ (k % layers * inner_count + k // layers + i_rel)
-            adapter = wide(got, f, d * tiles, tiles, rank)
-            low = adapter_scale_factor * dot(h, adapter, NN)
+        for k, f_rel in enumerate(every if i_rel == 0 else far):
+            f = f_here ^ (f_rel ^ i_rel)
+            low = adapter_scale_factor * dot(h, wide(got, f, d * tiles, tiles, rank), NN)
             start = pl.multiple_of(f * rows + d * cols, lanes)
             out[:, pl.ds(start, cols)] = (
                 piece[:, k * cols : (k + 1) * cols].astype(F32) + low
@@ -300,13 +312,13 @@
     ws = [w_here] + [None] * (layers - 1)
     for bit in bits(layers):
         ws[bit] = exchange("w_layers", w_here, "fsdp", bit * inner_count)
-    gs, rels = [grad_value], [(0, 0)]
-    stages = [("fsdp", bit) for bit in bits(inner_count)[1:]] + [("dp", bit) for bit in bits(split)]
-    for axis, bit in stages:
-        gs = gs + [exchange("g_" + axis, g, axis, bit) for g in gs]
-        rels = rels + [(i | bit, d) if axis == "fsdp" else (i, d | bit) for i, d in rels]
-    g_counts = [1] * len(rels)
-    ids, downs, ups, ws, gs[1] = lax.optimization_barrier((ids, downs, ups, ws, gs[1]))
+    rels = [(i, 0) for i in range(0, inner_count, 2)]
+    beside = jnp.concatenate([grad_value, w_here], axis=0)
+    near = [exchange("g_w_layer", beside, "fsdp", i) for i, _ in rels[1:]]
+    ids, downs, ups, ws, near = lax.optimization_barrier((ids, downs, ups, ws, near))
+    held = jnp.concatenate([grad_value] + [n[:tokens] for n in near], axis=0)
+    others = [exchange("g_dp", held, "dp", d) for d in range(1, split)]
+    rels = rels + [(i, d) for d in range(1, split) for i, _ in rels]
 
     box = jax.ShapeDtypeStruct((fsdp_count, tall, lanes), BF16)
     box_bytes = 2 * fsdp_count * tall * lanes
@@ -317,6 +329,7 @@
         axis=1,
     )
     ups[0] = pltpu.with_memory_space_constraint(ups[0], pltpu.HBM)
+    downs[0] = pltpu.with_memory_space_constraint(downs[0], pltpu.HBM)
     sent = pl.pallas_call(
         functools.partial(select_kernel, dp_count),
         out_shape=pltpu.HBM(box.shape, BF16),
@@ -336,18 +349,23 @@
             if ws[k + bit] is None:
                 ws[k + bit] = exchange("w_last", ws[k], "fsdp", bit * inner_count)
     ws = ws + [exchange("w_core", w, "fsdp", 1) for w in ws]
-
+    near_other = [exchange("w_core", n, "fsdp", 1) for n in near]
+
+    wide_cols = (2 * layers + 2 * len(near)) * cols
     pieces = pl.pallas_call(
-        functools.partial(base_kernel, g_counts, len(ws)),
-        out_shape=[jax.ShapeDtypeStruct((tokens, len(ws) * cols), BF16)] * len(rels),
-        in_specs=vmem(len(gs) + len(ws)),
+        functools.partial(base_kernel, rels, len(near), layers),
+        out_shape=[
+            jax.ShapeDtypeStruct((tokens, wide_cols if i == 0 else (2 * layers - 2) * cols), BF16)
+            for i, _ in rels
+        ],
+        in_specs=vmem(1 + 2 * len(near) + len(ws) + len(others)),
         out_specs=vmem(len(rels)),
         compiler_params=params(),
         cost_estimate=cost(
             base_weight * 2 * tokens * width * kv_width, base_weight * 4 * tokens * width
         ),
         name="base",
-    )(*gs, *ws)
+    )(grad_value, *near, *ws, *near_other, *others)
     pieces = [pieces[0]] + [
         exchange("pieces%d%d" % (i, d), p, ("fsdp", "dp"), i * dp_count + d)
         for (i, d), p in zip(rels[1:], pieces[1:])

time: 109 us -> 108 us (level)
  waiting for transfers between devices: 55.2 us -> 50.6 us
  Pallas kernels: 13.6 us -> 14.8 us
    ppermute x17, waiting for transfers between devices: 48.1 us -> 39.8 us  [exchange(): return lax.ppermute(array, axis, xor_pairs(axis_count(axis), bits))]
    all_to_all x1, waiting for transfers between devices: 1.82 us -> 5.52 us  [on_device(): returned = lax.all_to_all(back, axes, 0, 0, tiled=True)]
    concatenate x0 -> x2, other arithmetic: none -> 1.73 us  [the longest x1 0.93 us: on_device(): beside = jnp.concatenate([grad_value, w_here], axis=0)]
    unnamed x18 -> x28, local copies, waits for them, and re-layouts: 3.03 us -> 3.78 us
  transfers between devices with their start and end apart: 20 -> 20, of which waited for: 7 -> 10; matrix products, arithmetic and copies ran while one was open for 2% -> 2% of each run, Pallas kernels for 8% -> 9%
where the time goes in v5:
time: 108 us; the launch traced here: 107 us
  waiting for transfers between devices  50.6 us (47%)
  starting transfers between devices  33.5 us (31%)
  Pallas kernels  14.8 us (14%)
  local copies, waits for them, and re-layouts  4.8 us (4%)
  other arithmetic  1.91 us (2%)
  between operations  1.5 us (1%)
    ppermute x17, waiting for transfers between devices, exchange(): return lax.ppermute(array, axis, xor_pairs(axis_count(axis), bits))  39.8 us
    ppermute x17, starting transfers between devices, exchange(): return lax.ppermute(array, axis, xor_pairs(axis_count(axis), bits))  20.3 us
    all_to_all x1, waiting for transfers between devices, on_device(): returned = lax.all_to_all(back, axes, 0, 0, tiled=True)  5.52 us
    all_to_all x1, waiting for transfers between devices, on_device(): lax.all_to_all(jnp.broadcast_to(tenant_ids[:, None, None], (fsdp_count, 1...  5.26 us
    all_to_all x1, starting transfers between devices, on_device(): returned = lax.all_to_all(back, axes, 0, 0, tiled=True)  4.96 us
    all_to_all x1, starting transfers between devices, on_device(): got = lax.all_to_all(sent, 'fsdp', 0, 0, tiled=True)  4.72 us
    pallas_call x1, Pallas kernels, on_device(): pl.pallas_call(functools.partial(base_kernel, rels, len(near), layers), o...  3.84 us
    unnamed x28, local copies, waits for them, and re-layouts  3.78 us
  transfers between devices with their start and end apart: 20, of which 10 were waited for; matrix products, arithmetic and copies ran while one was open for 2% of the time, Pallas kernels for 9%

profile of v5, /device:TPU:0, one launch (start us, length us, event | category | flops | bytes accessed | tf_op | source)
XLA Modules:
  0.0 107.0 jit_solution(14390934026291551974)
XLA Ops:
  0.6 0.0 copy-start
  0.6 0.0 copy-start.2
  0.7 0.0 copy-start.12
  0.7 3.0 %collective-permute-start = (bf16[8,64,512]{2,1,0:T(8,128)(2,1)}, bf16[8,64,512]{2,1,0:T(8,128)(2,1)S(1)}, u32[]{:S(2)}, u32[]{:S(2)}) collective-permute-start(bf16[8,64,512]{2,1,0:T(8,128)(2,1)} %bitcast.4), channel_id=1, source_target_pairs={{0,1},{1,0},{2,3},{3,2},{4,5},{5,4},{6,7},{7,6},{8,9},{9,8},{10,11... | collective-permute-start | bytes 1572872 | tf_op jit(solution)/shard_map/down_dp/ppermute | solution.py:277
  3.7 0.9 pad_maximum_fusion
  4.6 1.6 %collective-permute-start.4 = (bf16[384,512]{1,0:T(8,128)(2,1)S(1)}, bf16[384,512]{1,0:T(8,128)(2,1)S(1)}, u32[]{:S(2)}, u32[]{:S(2)}) collective-permute-start(bf16[384,512]{1,0:T(8,128)(2,1)S(1)} %pad_maximum_fusion), channel_id=1, source_target_pairs={{0,4},{2,6},{4,0},{6,2},{8,12},{10,14},{12,8},{14,10},{16,20},{18,... | collective-permute-start | bytes 1179656 | tf_op jit(solution)/shard_map/g_w_layer/ppermute | solution.py:277
  6.2 2.6 %collective-permute-start.3 = (bf16[256,512]{1,0:T(8,128)(2,1)S(1)}, bf16[256,512]{1,0:T(8,128)(2,1)S(1)}, u32[]{:S(2)}, u32[]{:S(2)}) collective-permute-start(bf16[256,512]{1,0:T(8,128)(2,1)S(1)} %constant_dynamic-slice_fusion.refs_1_), channel_id=1, source_target_pairs={{0,16},{2,18},{4,20},{6,22},{8,24},{10,26},{12,28},{14,30},{16,0},... | collective-permute-start | bytes 786440 | tf_op jit(solution)/shard_map/w_layers/ppermute | solution.py:277
  8.8 1.6 %collective-permute-start.2 = (bf16[256,512]{1,0:T(8,128)(2,1)S(1)}, bf16[256,512]{1,0:T(8,128)(2,1)S(1)}, u32[]{:S(2)}, u32[]{:S(2)}) collective-permute-start(bf16[256,512]{1,0:T(8,128)(2,1)S(1)} %constant_dynamic-slice_fusion.refs_1_), channel_id=1, source_target_pairs={{0,8},{2,10},{4,12},{6,14},{8,0},{10,2},{12,4},{14,6},{16,24},{18,... | collective-permute-start | bytes 786440 | tf_op jit(solution)/shard_map/w_layers/ppermute | solution.py:277
  11.0 0.6 broadcast_in_dim.24
  11.7 3.5 %all-to-all-start = ((s32[16,1,128]{2,1,0:T(1,128)}), s32[16,1,128]{2,1,0:T(1,128)S(1)}, u32[]{:S(2)}, u32[]{:S(2)}) async-start(s32[16,1,128]{2,1,0:T(1,128)} %broadcast_in_dim.24), calls=%async_computation | async-start | bytes 16384 | tf_op jit(solution)/shard_map/ids/all_to_all | solution.py:307
  15.1 1.0 collective-permute-start.1
  16.2 5.3 %all-to-all-done = s32[16,1,128]{2,1,0:T(1,128)S(1)} async-done(((s32[16,1,128]{2,1,0:T(1,128)}), s32[16,1,128]{2,1,0:T(1,128)S(1)}, u32[]{:S(2)}, u32[]{:S(2)}) %all-to-all-start) | async-done | bytes 8224 | tf_op jit(solution)/shard_map/ids/all_to_all | solution.py:307
  21.4 0.4 slice_reduce_fusion
  21.8 0.0 collective-permute-done.3.refs_3_
  21.8 0.0 copy-start.10
  21.9 0.8 pad_maximum_fusion.1
  22.7 1.2 %collective-permute-start.11 = (bf16[256,512]{1,0:T(8,128)(2,1)}, bf16[256,512]{1,0:T(8,128)(2,1)}, u32[]{:S(2)}, u32[]{:S(2)}) collective-permute-start(bf16[256,512]{1,0:T(8,128)(2,1)} %pad_maximum_fusion.1), channel_id=1, source_target_pairs={{0,1},{1,0},{2,3},{3,2},{4,5},{5,4},{6,7},{7,6},{8,9},{9,8},{10,11... | collective-permute-start | bytes 786440 | tf_op jit(solution)/shard_map/g_dp/ppermute | solution.py:277
  23.9 0.8 collective-permute-start.5
  24.6 0.2 select_reduce_fusion.slots.refs_0_
  24.8 3.0 %select.3 = bf16[16,272,128]{2,1,0:T(8,128)(2,1)} custom-call(s32[16]{0:T(128)S(1)} %select_reduce_fusion.slots.refs_0_, bf16[8,64,512]{2,1,0:T(8,128)(2,1)} %bitcast.5, bf16[8,64,512]{2,1,0:T(8,128)(2,1)S(1)} %collective-permute-done.refs_1_, bf16[8,32,64]{2,1,0:T(8,128)(2,1)} %refs_2_, bf16[8,32,64]{2,1,0:T(8,128)(2,1)S(1)} %collective-permute-done.1.refs_3_), custom_call_target="tpu_custom_call" | custom-call | bytes 2228224 | tf_op jit(solution)/shard_map/select/pallas_call | solution.py:333
  27.8 4.7 %all-to-all-start.1 = ((bf16[16,272,128]{2,1,0:T(8,128)(2,1)}), bf16[16,272,128]{2,1,0:T(8,128)(2,1)S(1)}, u32[]{:S(2)}, u32[]{:S(2)}) async-start(bf16[16,272,128]{2,1,0:T(8,128)(2,1)} %select.3), calls=%async_computation.1 | async-start | bytes 2228224 | tf_op jit(solution)/shard_map/adapters_to_blocks/all_to_all | solution.py:346
  32.5 0.4 collective-permute-start.6
  32.9 0.2 collective-permute-start.7
  33.1 0.3 collective-permute-start.8
  33.5 0.2 collective-permute-start.9
  33.6 0.5 collective-permute-done.6.refs_5_
  34.1 0.4 collective-permute-done.7.refs_6_
  34.5 0.7 collective-permute-done.8.refs_7_
  35.2 0.2 collective-permute-done.9.refs_8_
  35.5 0.9 copy-done.9
  36.4 0.9 copy-done.11
  37.4 3.8 %base.1 = (bf16[128,2560]{1,0:T(8,128)(2,1)S(1)}, bf16[128,1536]{1,0:T(8,128)(2,1)S(1)}, bf16[128,2560]{1,0:T(8,128)(2,1)S(1)}, bf16[128,1536]{1,0:T(8,128)(2,1)S(1)}) custom-call(bf16[128,512]{1,0:T(8,128)(2,1)S(1)} %copy-done.2, bf16[384,512]{1,0:T(8,128)(2,1)S(1)} %collective-permute-done.4.refs_0_, ...), custom_call_target="tpu_custom_call" | custom-call | flops 11811160064 | bytes 46137344 | tf_op jit(solution)/shard_map/base/pallas_call | solution.py:355
  41.2 0.8 collective-permute-start.13
  42.1 1.9 %collective-permute-start.12 = (bf16[128,1536]{1,0:T(8,128)(2,1)S(1)}, bf16[128,1536]{1,0:T(8,128)(2,1)S(1)}, u32[]{:S(2)}, u32[]{:S(2)}) collective-permute-start(bf16[128,1536]{1,0:T(8,128)(2,1)S(1)} %get-tuple-element.47), channel_id=1, source_target_pairs={{0,4},{1,5},{2,6},{3,7},{4,0},{5,1},{6,2},{7,3},{8,12},{9,13},{10,... | collective-permute-start | bytes 1179656 | tf_op jit(solution)/shard_map/pieces20/ppermute | solution.py:277
  43.9 14.1 %collective-permute-done.12.refs_1_ = bf16[128,1536]{1,0:T(8,128)(2,1)S(1)} collective-permute-done((bf16[128,1536]{1,0:T(8,128)(2,1)S(1)}, bf16[128,1536]{1,0:T(8,128)(2,1)S(1)}, u32[]{:S(2)}, u32[]{:S(2)}) %collective-permute-start.12) | collective-permute-done | bytes 393248 | tf_op jit(solution)/shard_map/pieces20/ppermute | solution.py:277
  58.1 0.2 collective-permute-done.13.refs_2_
  58.3 1.8 %copy-done.1 = bf16[128,8192]{1,0:T(8,128)(2,1)S(1)} copy-done((bf16[128,8192]{1,0:T(8,128)(2,1)S(1)}, bf16[128,8192]{1,0:T(8,128)(2,1)}, u32[]{:S(2)}) %copy-start.1) | copy-done | bytes 2097176
  60.1 2.0 %middle.1 = (bf16[128,64]{1,0:T(8,128)(2,1)S(1)}, bf16[32,144,128]{2,1,0:T(8,128)(2,1)}) custom-call(bf16[128,8192]{1,0:T(8,128)(2,1)S(1)} %copy-done.1, bf16[128,512]{1,0:T(8,128)(2,1)S(1)} %copy-done.2, bf16[16,272,128]{2,1,0:T(8,128)(2,1)S(1)} %all-to-all-done.1.got), custom_call_target="tpu_custom_call" | custom-call | flops 268435456 | bytes 4325376 | tf_op jit(solution)/shard_map/middle/pallas_call | solution.py:380
  62.1 5.0 %all-to-all-start.2 = ((bf16[32,144,128]{2,1,0:T(8,128)(2,1)}), bf16[32,144,128]{2,1,0:T(8,128)(2,1)S(1)}, u32[]{:S(2)}, u32[]{:S(2)}) async-start(bf16[32,144,128]{2,1,0:T(8,128)(2,1)} %get-tuple-element.50), calls=%async_computation.2 | async-start | bytes 2359296 | tf_op jit(solution)/shard_map/gradients_back/all_to_all | solution.py:399
  67.1 2.7 %collective-permute-start.15 = (bf16[128,1536]{1,0:T(8,128)(2,1)}, bf16[128,1536]{1,0:T(8,128)(2,1)}, u32[]{:S(2)}, u32[]{:S(2)}) collective-permute-start(bf16[128,1536]{1,0:T(8,128)(2,1)} %copy-done.7), channel_id=1, source_target_pairs={{0,5},{1,4},{2,7},{3,6},{4,1},{5,0},{6,3},{7,2},{8,13},{9,12},{10,... | collective-permute-start | bytes 1179656 | tf_op jit(solution)/shard_map/pieces21/ppermute | solution.py:277
  69.9 0.6 collective-permute-start.14
  70.4 20.2 %collective-permute-done.14.refs_1_ = s32[16]{0:T(128)S(1)} collective-permute-done((s32[16]{0:T(128)S(1)}, s32[16]{0:T(128)S(1)}, u32[]{:S(2)}, u32[]{:S(2)}) %collective-permute-start.14) | collective-permute-done | bytes 96 | tf_op jit(solution)/shard_map/slots_dp/ppermute | solution.py:277
  90.6 5.5 %all-to-all-done.2.refs_2_ = bf16[32,144,128]{2,1,0:T(8,128)(2,1)S(1)} async-done(((bf16[32,144,128]{2,1,0:T(8,128)(2,1)}), bf16[32,144,128]{2,1,0:T(8,128)(2,1)S(1)}, u32[]{:S(2)}, u32[]{:S(2)}) %all-to-all-start.2) | async-done | bytes 1179680 | tf_op jit(solution)/shard_map/gradients_back/all_to_all | solution.py:399
  96.2 2.0 %sum_all.1 = (bf16[8,64,256]{2,1,0:T(8,128)(2,1)S(1)}, bf16[8,64,256]{2,1,0:T(8,128)(2,1)S(1)}, bf16[8,32,64]{2,1,0:T(8,128)(2,1)}) custom-call(s32[16]{0:T(128)S(1)} %select_reduce_fusion.slots.refs_0_, s32[16]{0:T(128)S(1)} %collective-permute-done.14.refs_1_, bf16[32,144,128]{2,1,0:T(8,128)(2,1)S(1)} %all-to-all-done.2.refs_2_), custom_call_target="tpu_custom_call" | custom-call | bytes 2228224 | tf_op jit(solution)/shard_map/sum_all/pallas_call | solution.py:419
  98.2 1.5 %collective-permute-start.16 = (bf16[8,64,256]{2,1,0:T(8,128)(2,1)S(1)}, bf16[8,64,256]{2,1,0:T(8,128)(2,1)S(1)}, u32[]{:S(2)}, u32[]{:S(2)}) collective-permute-start(bf16[8,64,256]{2,1,0:T(8,128)(2,1)S(1)} %get-tuple-element.59), channel_id=1, source_target_pairs={{0,1},{1,0},{2,3},{3,2},{4,5},{5,4},{6,7},{7,6},{8,9},{9,8},{10,11... | collective-permute-start | bytes 786440 | tf_op jit(solution)/shard_map/grads_dp/ppermute | solution.py:277
  99.7 3.1 %rows.1 = bf16[128,8192]{1,0:T(8,128)(2,1)} custom-call(bf16[128,64]{1,0:T(8,128)(2,1)S(1)} %get-tuple-element.60.hidden, bf16[16,272,128]{2,1,0:T(8,128)(2,1)S(1)} %all-to-all-done.1.got, bf16[128,2560]{1,0:T(8,128)(2,1)S(1)} %get-tuple-element.61.refs_0_, bf16[128,1536]{1,0:T(8,128)(2,1)S(1)} %copy-done.6, bf16[128,2560]{1,0:T(8,128)(2,1)S(1)} %copy-done.4, ...), custom_call_target="tpu_custom_call" | custom-call | flops 134217728 | bytes 5308416 | tf_op jit(solution)/shard_map/rows/pallas_call | solution.py:405
  102.8 3.4 %collective-permute-done.16.refs_1_ = bf16[8,64,256]{2,1,0:T(8,128)(2,1)S(1)} collective-permute-done((bf16[8,64,256]{2,1,0:T(8,128)(2,1)S(1)}, bf16[8,64,256]{2,1,0:T(8,128)(2,1)S(1)}, u32[]{:S(2)}, u32[]{:S(2)}) %collective-permute-start.16) | collective-permute-done | bytes 262176 | tf_op jit(solution)/shard_map/grads_dp/ppermute | solution.py:277
  106.2 0.8 join.1
  (33 shorter events, 0.1 us)
Async XLA Ops:
  0.6 3.1 %copy-start = (bf16[512,512]{1,0:T(8,128)(2,1)S(1)}, bf16[512,512]{1,0:T(8,128)(2,1)}, u32[]{:S(2)}) copy-start(bf16[512,512]{1,0:T(8,128)(2,1)} %param.9) | copy-start | bytes 1572868
  0.6 21.3 %copy-start.2 = (bf16[128,512]{1,0:T(8,128)(2,1)S(1)}, bf16[128,512]{1,0:T(8,128)(2,1)}, u32[]{:S(2)}) copy-start(bf16[128,512]{1,0:T(8,128)(2,1)} %g.1) | copy-start | bytes 393220
  0.7 14.5 %copy-start.12 = (bf16[8,32,64]{2,1,0:T(8,128)(2,1)S(1)}, bf16[8,32,64]{2,1,0:T(8,128)(2,1)}, u32[]{:S(2)}) copy-start(bf16[8,32,64]{2,1,0:T(8,128)(2,1)} %refs_2_) | copy-start | bytes 98308
  0.7 24.0 %copy-start.13 = (s32[16]{0:T(128)S(1)}, s32[16]{0:T(128)}, u32[]{:S(2)}) copy-start(s32[16]{0:T(128)} %param.13) | copy-start | bytes 196
  0.7 21.2 %collective-permute-start = (bf16[8,64,512]{2,1,0:T(8,128)(2,1)}, bf16[8,64,512]{2,1,0:T(8,128)(2,1)S(1)}, u32[]{:S(2)}, u32[]{:S(2)}) collective-permute-start(bf16[8,64,512]{2,1,0:T(8,128)(2,1)} %bitcast.4), channel_id=1, source_target_pairs={{0,1},{1,0},{2,3},{3,2},{4,5},{5,4},{6,7},{7,6},{8,9},{9,8},{10,11... | collective-permute-start | bytes 1572872 | tf_op jit(solution)/shard_map/down_dp/ppermute | solution.py:277
  4.6 17.2 %collective-permute-start.4 = (bf16[384,512]{1,0:T(8,128)(2,1)S(1)}, bf16[384,512]{1,0:T(8,128)(2,1)S(1)}, u32[]{:S(2)}, u32[]{:S(2)}) collective-permute-start(bf16[384,512]{1,0:T(8,128)(2,1)S(1)} %pad_maximum_fusion), channel_id=1, source_target_pairs={{0,4},{2,6},{4,0},{6,2},{8,12},{10,14},{12,8},{14,10},{16,20},{18,... | collective-permute-start | bytes 1179656 | tf_op jit(solution)/shard_map/g_w_layer/ppermute | solution.py:277
  6.2 15.6 %collective-permute-start.3 = (bf16[256,512]{1,0:T(8,128)(2,1)S(1)}, bf16[256,512]{1,0:T(8,128)(2,1)S(1)}, u32[]{:S(2)}, u32[]{:S(2)}) collective-permute-start(bf16[256,512]{1,0:T(8,128)(2,1)S(1)} %constant_dynamic-slice_fusion.refs_1_), channel_id=1, source_target_pairs={{0,16},{2,18},{4,20},{6,22},{8,24},{10,26},{12,28},{14,30},{16,0},... | collective-permute-start | bytes 786440 | tf_op jit(solution)/shard_map/w_layers/ppermute | solution.py:277
  8.8 13.0 %collective-permute-start.2 = (bf16[256,512]{1,0:T(8,128)(2,1)S(1)}, bf16[256,512]{1,0:T(8,128)(2,1)S(1)}, u32[]{:S(2)}, u32[]{:S(2)}) collective-permute-start(bf16[256,512]{1,0:T(8,128)(2,1)S(1)} %constant_dynamic-slice_fusion.refs_1_), channel_id=1, source_target_pairs={{0,8},{2,10},{4,12},{6,14},{8,0},{10,2},{12,4},{14,6},{16,24},{18,... | collective-permute-start | bytes 786440 | tf_op jit(solution)/shard_map/w_layers/ppermute | solution.py:277
  11.7 9.8 %all-to-all-start = ((s32[16,1,128]{2,1,0:T(1,128)}), s32[16,1,128]{2,1,0:T(1,128)S(1)}, u32[]{:S(2)}, u32[]{:S(2)}) async-start(s32[16,1,128]{2,1,0:T(1,128)} %broadcast_in_dim.24), calls=%async_computation | async-start | bytes 16384 | tf_op jit(solution)/shard_map/ids/all_to_all | solution.py:307
  15.1 6.7 %collective-permute-start.1 = (bf16[8,32,64]{2,1,0:T(8,128)(2,1)S(1)}, bf16[8,32,64]{2,1,0:T(8,128)(2,1)S(1)}, u32[]{:S(2)}, u32[]{:S(2)}) collective-permute-start(bf16[8,32,64]{2,1,0:T(8,128)(2,1)S(1)} %copy-done.12), channel_id=1, source_target_pairs={{0,1},{1,0},{2,3},{3,2},{4,5},{5,4},{6,7},{7,6},{8,9},{9,8},{10,11... | collective-permute-start | bytes 98312 | tf_op jit(solution)/shard_map/up_dp/ppermute | solution.py:277
  21.8 11.3 %copy-start.8 = (bf16[256,512]{1,0:T(8,128)(2,1)}, bf16[256,512]{1,0:T(8,128)(2,1)S(1)}, u32[]{:S(2)}) copy-start(bf16[256,512]{1,0:T(8,128)(2,1)S(1)} %collective-permute-done.3.refs_3_) | copy-start | bytes 786436
  21.8 11.1 %copy-start.10 = (bf16[256,512]{1,0:T(8,128)(2,1)}, bf16[256,512]{1,0:T(8,128)(2,1)S(1)}, u32[]{:S(2)}) copy-start(bf16[256,512]{1,0:T(8,128)(2,1)S(1)} %collective-permute-done.2.refs_2_) | copy-start | bytes 786436
  22.7 10.4 %collective-permute-start.11 = (bf16[256,512]{1,0:T(8,128)(2,1)}, bf16[256,512]{1,0:T(8,128)(2,1)}, u32[]{:S(2)}, u32[]{:S(2)}) collective-permute-start(bf16[256,512]{1,0:T(8,128)(2,1)} %pad_maximum_fusion.1), channel_id=1, source_target_pairs={{0,1},{1,0},{2,3},{3,2},{4,5},{5,4},{6,7},{7,6},{8,9},{9,8},{10,11... | collective-permute-start | bytes 786440 | tf_op jit(solution)/shard_map/g_dp/ppermute | solution.py:277
  23.9 9.6 %collective-permute-start.5 = (bf16[256,512]{1,0:T(8,128)(2,1)S(1)}, bf16[256,512]{1,0:T(8,128)(2,1)}, u32[]{:S(2)}, u32[]{:S(2)}) collective-permute-start(bf16[256,512]{1,0:T(8,128)(2,1)S(1)} %collective-permute-done.3.refs_3_), channel_id=1, source_target_pairs={{0,8},{2,10},{4,12},{6,14},{8,0},{10,2},{12,4},{14,6},{16,24},{18,... | collective-permute-start | bytes 786440 | tf_op jit(solution)/shard_map/w_last/ppermute | solution.py:277
  24.6 10.6 %collective-permute-start.10 = (bf16[384,512]{1,0:T(8,128)(2,1)S(1)}, bf16[384,512]{1,0:T(8,128)(2,1)S(1)}, u32[]{:S(2)}, u32[]{:S(2)}) collective-permute-start(bf16[384,512]{1,0:T(8,128)(2,1)S(1)} %collective-permute-done.4.refs_0_), channel_id=1, source_target_pairs={{0,2},{2,0},{4,6},{6,4},{8,10},{10,8},{12,14},{14,12},{16,18},{18,... | collective-permute-start | bytes 1179656 | tf_op jit(solution)/shard_map/w_core/ppermute | solution.py:277
  27.8 30.5 %all-to-all-start.1 = ((bf16[16,272,128]{2,1,0:T(8,128)(2,1)}), bf16[16,272,128]{2,1,0:T(8,128)(2,1)S(1)}, u32[]{:S(2)}, u32[]{:S(2)}) async-start(bf16[16,272,128]{2,1,0:T(8,128)(2,1)} %select.3), calls=%async_computation.1 | async-start | bytes 2228224 | tf_op jit(solution)/shard_map/adapters_to_blocks/all_to_all | solution.py:346
  32.5 1.6 %collective-permute-start.6 = (bf16[256,512]{1,0:T(8,128)(2,1)S(1)}, bf16[256,512]{1,0:T(8,128)(2,1)S(1)}, u32[]{:S(2)}, u32[]{:S(2)}) collective-permute-start(bf16[256,512]{1,0:T(8,128)(2,1)S(1)} %constant_dynamic-slice_fusion.refs_1_), channel_id=1, source_target_pairs={{0,2},{2,0},{4,6},{6,4},{8,10},{10,8},{12,14},{14,12},{16,18},{18,... | collective-permute-start | bytes 786440 | tf_op jit(solution)/shard_map/w_core/ppermute | solution.py:277
  32.9 1.6 %collective-permute-start.7 = (bf16[256,512]{1,0:T(8,128)(2,1)S(1)}, bf16[256,512]{1,0:T(8,128)(2,1)S(1)}, u32[]{:S(2)}, u32[]{:S(2)}) collective-permute-start(bf16[256,512]{1,0:T(8,128)(2,1)S(1)} %collective-permute-done.2.refs_2_), channel_id=1, source_target_pairs={{0,2},{2,0},{4,6},{6,4},{8,10},{10,8},{12,14},{14,12},{16,18},{18,... | collective-permute-start | bytes 786440 | tf_op jit(solution)/shard_map/w_core/ppermute | solution.py:277
  33.1 2.1 %collective-permute-start.8 = (bf16[256,512]{1,0:T(8,128)(2,1)S(1)}, bf16[256,512]{1,0:T(8,128)(2,1)S(1)}, u32[]{:S(2)}, u32[]{:S(2)}) collective-permute-start(bf16[256,512]{1,0:T(8,128)(2,1)S(1)} %collective-permute-done.3.refs_3_), channel_id=1, source_target_pairs={{0,2},{2,0},{4,6},{6,4},{8,10},{10,8},{12,14},{14,12},{16,18},{18,... | collective-permute-start | bytes 786440 | tf_op jit(solution)/shard_map/w_core/ppermute | solution.py:277
  33.5 2.0 %collective-permute-start.9 = (bf16[256,512]{1,0:T(8,128)(2,1)}, bf16[256,512]{1,0:T(8,128)(2,1)S(1)}, u32[]{:S(2)}, u32[]{:S(2)}) collective-permute-start(bf16[256,512]{1,0:T(8,128)(2,1)} %collective-permute-done.5.refs_4_), channel_id=1, source_target_pairs={{0,2},{2,0},{4,6},{6,4},{8,10},{10,8},{12,14},{14,12},{16,18},{18,... | collective-permute-start | bytes 786440 | tf_op jit(solution)/shard_map/w_core/ppermute | solution.py:277
  35.5 1.0 copy-start.9
  36.4 0.9 copy-start.11
  41.2 16.9 %copy-start.7 = (bf16[128,1536]{1,0:T(8,128)(2,1)}, bf16[128,1536]{1,0:T(8,128)(2,1)S(1)}, u32[]{:S(2)}) copy-start(bf16[128,1536]{1,0:T(8,128)(2,1)S(1)} %get-tuple-element.57) | copy-start | bytes 1179652
  41.2 17.0 %collective-permute-start.13 = (bf16[128,2560]{1,0:T(8,128)(2,1)S(1)}, bf16[128,2560]{1,0:T(8,128)(2,1)S(1)}, u32[]{:S(2)}, u32[]{:S(2)}) collective-permute-start(bf16[128,2560]{1,0:T(8,128)(2,1)S(1)} %get-tuple-element.48), channel_id=1, source_target_pairs={{0,1},{1,0},{2,3},{3,2},{4,5},{5,4},{6,7},{7,6},{8,9},{9,8},{10,11... | collective-permute-start | bytes 1966088 | tf_op jit(solution)/shard_map/pieces01/ppermute | solution.py:277
  42.1 16.0 %collective-permute-start.12 = (bf16[128,1536]{1,0:T(8,128)(2,1)S(1)}, bf16[128,1536]{1,0:T(8,128)(2,1)S(1)}, u32[]{:S(2)}, u32[]{:S(2)}) collective-permute-start(bf16[128,1536]{1,0:T(8,128)(2,1)S(1)} %get-tuple-element.47), channel_id=1, source_target_pairs={{0,4},{1,5},{2,6},{3,7},{4,0},{5,1},{6,2},{7,3},{8,12},{9,13},{10,... | collective-permute-start | bytes 1179656 | tf_op jit(solution)/shard_map/pieces20/ppermute | solution.py:277
  58.1 4.0 %copy-start.5 = (bf16[128,1536]{1,0:T(8,128)(2,1)}, bf16[128,1536]{1,0:T(8,128)(2,1)S(1)}, u32[]{:S(2)}) copy-start(bf16[128,1536]{1,0:T(8,128)(2,1)S(1)} %collective-permute-done.12.refs_1_) | copy-start | bytes 1179652
  58.3 3.9 %copy-start.3 = (bf16[128,2560]{1,0:T(8,128)(2,1)}, bf16[128,2560]{1,0:T(8,128)(2,1)S(1)}, u32[]{:S(2)}) copy-start(bf16[128,2560]{1,0:T(8,128)(2,1)S(1)} %collective-permute-done.13.refs_2_) | copy-start | bytes 1966084
  58.3 1.8 %copy-start.1 = (bf16[128,8192]{1,0:T(8,128)(2,1)S(1)}, bf16[128,8192]{1,0:T(8,128)(2,1)}, u32[]{:S(2)}) copy-start(bf16[128,8192]{1,0:T(8,128)(2,1)} %x.1) | copy-start | bytes 6291460
  62.1 34.0 %all-to-all-start.2 = ((bf16[32,144,128]{2,1,0:T(8,128)(2,1)}), bf16[32,144,128]{2,1,0:T(8,128)(2,1)S(1)}, u32[]{:S(2)}, u32[]{:S(2)}) async-start(bf16[32,144,128]{2,1,0:T(8,128)(2,1)} %get-tuple-element.50), calls=%async_computation.2 | async-start | bytes 2359296 | tf_op jit(solution)/shard_map/gradients_back/all_to_all | solution.py:399
  67.1 29.1 %collective-permute-start.15 = (bf16[128,1536]{1,0:T(8,128)(2,1)}, bf16[128,1536]{1,0:T(8,128)(2,1)}, u32[]{:S(2)}, u32[]{:S(2)}) collective-permute-start(bf16[128,1536]{1,0:T(8,128)(2,1)} %copy-done.7), channel_id=1, source_target_pairs={{0,5},{1,4},{2,7},{3,6},{4,1},{5,0},{6,3},{7,2},{8,13},{9,12},{10,... | collective-permute-start | bytes 1179656 | tf_op jit(solution)/shard_map/pieces21/ppermute | solution.py:277
  69.9 20.8 %collective-permute-start.14 = (s32[16]{0:T(128)S(1)}, s32[16]{0:T(128)S(1)}, u32[]{:S(2)}, u32[]{:S(2)}) collective-permute-start(s32[16]{0:T(128)S(1)} %select_reduce_fusion.slots.refs_0_), channel_id=1, source_target_pairs={{0,1},{1,0},{2,3},{3,2},{4,5},{5,4},{6,7},{7,6},{8,9},{9,8},{10,11... | collective-permute-start | bytes 200 | tf_op jit(solution)/shard_map/slots_dp/ppermute | solution.py:277
  96.2 3.6 %copy-start.4 = (bf16[128,2560]{1,0:T(8,128)(2,1)S(1)}, bf16[128,2560]{1,0:T(8,128)(2,1)}, u32[]{:S(2)}) copy-start(bf16[128,2560]{1,0:T(8,128)(2,1)} %copy-done.3) | copy-start | bytes 1966084
  96.2 3.6 %copy-start.6 = (bf16[128,1536]{1,0:T(8,128)(2,1)S(1)}, bf16[128,1536]{1,0:T(8,128)(2,1)}, u32[]{:S(2)}) copy-start(bf16[128,1536]{1,0:T(8,128)(2,1)} %copy-done.5) | copy-start | bytes 1179652
  98.2 8.0 %collective-permute-start.16 = (bf16[8,64,256]{2,1,0:T(8,128)(2,1)S(1)}, bf16[8,64,256]{2,1,0:T(8,128)(2,1)S(1)}, u32[]{:S(2)}, u32[]{:S(2)}) collective-permute-start(bf16[8,64,256]{2,1,0:T(8,128)(2,1)S(1)} %get-tuple-element.59), channel_id=1, source_target_pairs={{0,1},{1,0},{2,3},{3,2},{4,5},{5,4},{6,7},{7,6},{8,9},{9,8},{10,11... | collective-permute-start | bytes 786440 | tf_op jit(solution)/shard_map/grads_dp/ppermute | solution.py:277

commit v6 on v5

--- a/solution.py
+++ b/solution.py
@@ -10,7 +10,7 @@
 
 adapter_scale_factor = 2.0
 lanes = 128
-base_weight = 11
+base_weight = 10
 store_parts = 4
 BF16, F32 = jnp.bfloat16, jnp.float32
 NT = (((1,), (1,)), ((), ()))
@@ -351,6 +351,7 @@
     ws = ws + [exchange("w_core", w, "fsdp", 1) for w in ws]
     near_other = [exchange("w_core", n, "fsdp", 1) for n in near]
 
+    ws = [pltpu.with_memory_space_constraint(w, pltpu.HBM) for w in ws[:layers]] + ws[layers:]
     wide_cols = (2 * layers + 2 * len(near)) * cols
     pieces = pl.pallas_call(
         functools.partial(base_kernel, rels, len(near), layers),

time: 108 us -> 106 us (0.981)
  local copies, waits for them, and re-layouts: 4.8 us -> 2.9 us
    unnamed x28 -> x24, local copies, waits for them, and re-layouts: 3.78 us -> 1.88 us
where the time goes in v6:
time: 106 us
  waiting for transfers between devices  50.8 us (48%)
  starting transfers between devices  34.4 us (32%)
  Pallas kernels  15 us (14%)
  local copies, waits for them, and re-layouts  2.9 us (3%)
  between operations  1.51 us (1%)
  other arithmetic  1.23 us (1%)
    ppermute x17, waiting for transfers between devices, exchange(): return lax.ppermute(array, axis, xor_pairs(axis_count(axis), bits))  40 us
    ppermute x17, starting transfers between devices, exchange(): return lax.ppermute(array, axis, xor_pairs(axis_count(axis), bits))  20.7 us
    all_to_all x1, starting transfers between devices, on_device(): returned = lax.all_to_all(back, axes, 0, 0, tiled=True)  5.61 us
    all_to_all x1, waiting for transfers between devices, on_device(): returned = lax.all_to_all(back, axes, 0, 0, tiled=True)  5.52 us
    all_to_all x1, waiting for transfers between devices, on_device(): lax.all_to_all(jnp.broadcast_to(tenant_ids[:, None, None], (fsdp_count, 1...  5.26 us
    all_to_all x1, starting transfers between devices, on_device(): got = lax.all_to_all(sent, 'fsdp', 0, 0, tiled=True)  4.61 us
    pallas_call x1, Pallas kernels, on_device(): pl.pallas_call(functools.partial(base_kernel, rels, len(near), layers), o...  4 us
    all_to_all x1, starting transfers between devices, on_device(): lax.all_to_all(jnp.broadcast_to(tenant_ids[:, None, None], (fsdp_count, 1...  3.47 us
  transfers between devices with their start and end apart: 20, of which 10 were waited for; matrix products, arithmetic and copies ran while one was open for 2% of the time, Pallas kernels for 9%

profile of v6, /device:TPU:0, one launch (start us, length us, event | category | flops | bytes accessed | tf_op | source)
XLA Modules:
  0.0 105.8 jit_solution(14384551065900114241)
XLA Ops:
  0.6 0.0 copy-start
  0.6 0.0 copy-start.2
  0.7 0.0 copy-start.9
  0.7 3.0 %collective-permute-start = (bf16[8,64,512]{2,1,0:T(8,128)(2,1)}, bf16[8,64,512]{2,1,0:T(8,128)(2,1)S(1)}, u32[]{:S(2)}, u32[]{:S(2)}) collective-permute-start(bf16[8,64,512]{2,1,0:T(8,128)(2,1)} %bitcast.4), channel_id=1, source_target_pairs={{0,1},{1,0},{2,3},{3,2},{4,5},{5,4},{6,7},{7,6},{8,9},{9,8},{10,11... | collective-permute-start | bytes 1572872 | tf_op jit(solution)/shard_map/down_dp/ppermute | solution.py:277
  3.7 0.0 copy-start.8
  3.7 1.0 pad_maximum_fusion
  4.8 1.6 %collective-permute-start.4 = (bf16[384,512]{1,0:T(8,128)(2,1)S(1)}, bf16[384,512]{1,0:T(8,128)(2,1)S(1)}, u32[]{:S(2)}, u32[]{:S(2)}) collective-permute-start(bf16[384,512]{1,0:T(8,128)(2,1)S(1)} %pad_maximum_fusion), channel_id=1, source_target_pairs={{0,4},{2,6},{4,0},{6,2},{8,12},{10,14},{12,8},{14,10},{16,20},{18,... | collective-permute-start | bytes 1179656 | tf_op jit(solution)/shard_map/g_w_layer/ppermute | solution.py:277
  6.3 2.6 %collective-permute-start.3 = (bf16[256,512]{1,0:T(8,128)(2,1)S(1)}, bf16[256,512]{1,0:T(8,128)(2,1)}, u32[]{:S(2)}, u32[]{:S(2)}) collective-permute-start(bf16[256,512]{1,0:T(8,128)(2,1)S(1)} %constant_dynamic-slice_fusion.refs_1_), channel_id=1, source_target_pairs={{0,16},{2,18},{4,20},{6,22},{8,24},{10,26},{12,28},{14,30},{16,0},... | collective-permute-start | bytes 786440 | tf_op jit(solution)/shard_map/w_layers/ppermute | solution.py:277
  8.9 1.6 %collective-permute-start.2 = (bf16[256,512]{1,0:T(8,128)(2,1)S(1)}, bf16[256,512]{1,0:T(8,128)(2,1)S(1)}, u32[]{:S(2)}, u32[]{:S(2)}) collective-permute-start(bf16[256,512]{1,0:T(8,128)(2,1)S(1)} %constant_dynamic-slice_fusion.refs_1_), channel_id=1, source_target_pairs={{0,8},{2,10},{4,12},{6,14},{8,0},{10,2},{12,4},{14,6},{16,24},{18,... | collective-permute-start | bytes 786440 | tf_op jit(solution)/shard_map/w_layers/ppermute | solution.py:277
  11.2 0.6 broadcast_in_dim.24
  11.8 3.5 %all-to-all-start = ((s32[16,1,128]{2,1,0:T(1,128)}), s32[16,1,128]{2,1,0:T(1,128)S(1)}, u32[]{:S(2)}, u32[]{:S(2)}) async-start(s32[16,1,128]{2,1,0:T(1,128)} %broadcast_in_dim.24), calls=%async_computation | async-start | bytes 16384 | tf_op jit(solution)/shard_map/ids/all_to_all | solution.py:307
  15.2 1.0 collective-permute-start.1
  16.3 5.3 %all-to-all-done = s32[16,1,128]{2,1,0:T(1,128)S(1)} async-done(((s32[16,1,128]{2,1,0:T(1,128)}), s32[16,1,128]{2,1,0:T(1,128)S(1)}, u32[]{:S(2)}, u32[]{:S(2)}) %all-to-all-start) | async-done | bytes 8224 | tf_op jit(solution)/shard_map/ids/all_to_all | solution.py:307
  21.5 0.4 slice_reduce_fusion
  21.9 0.0 collective-permute-done.1.refs_3_
  21.9 0.0 collective-permute-done.3.refs_3_
  22.0 0.0 collective-permute-done.refs_1_
  22.0 1.2 %collective-permute-start.11 = (bf16[256,512]{1,0:T(8,128)(2,1)S(1)}, bf16[256,512]{1,0:T(8,128)(2,1)S(1)}, u32[]{:S(2)}, u32[]{:S(2)}) collective-permute-start(bf16[256,512]{1,0:T(8,128)(2,1)S(1)} %pad_maximum_fusion.1), channel_id=1, source_target_pairs={{0,1},{1,0},{2,3},{3,2},{4,5},{5,4},{6,7},{7,6},{8,9},{9,8},{10,11... | collective-permute-start | bytes 786440 | tf_op jit(solution)/shard_map/g_dp/ppermute | solution.py:277
  23.2 0.8 collective-permute-start.5
  24.0 0.2 select_reduce_fusion.slots.refs_0_
  24.2 3.0 %select.3 = bf16[16,272,128]{2,1,0:T(8,128)(2,1)} custom-call(s32[16]{0:T(128)S(1)} %select_reduce_fusion.slots.refs_0_, bf16[8,64,512]{2,1,0:T(8,128)(2,1)} %bitcast.5, bf16[8,64,512]{2,1,0:T(8,128)(2,1)S(1)} %collective-permute-done.refs_1_, bf16[8,32,64]{2,1,0:T(8,128)(2,1)} %refs_2_, bf16[8,32,64]{2,1,0:T(8,128)(2,1)S(1)} %collective-permute-done.1.refs_3_), custom_call_target="tpu_custom_call" | custom-call | bytes 2228224 | tf_op jit(solution)/shard_map/select/pallas_call | solution.py:333
  27.2 4.6 %all-to-all-start.1 = ((bf16[16,272,128]{2,1,0:T(8,128)(2,1)}), bf16[16,272,128]{2,1,0:T(8,128)(2,1)S(1)}, u32[]{:S(2)}, u32[]{:S(2)}) async-start(bf16[16,272,128]{2,1,0:T(8,128)(2,1)} %select.3), calls=%async_computation.1 | async-start | bytes 2228224 | tf_op jit(solution)/shard_map/adapters_to_blocks/all_to_all | solution.py:346
  31.8 0.4 collective-permute-start.10
  32.2 0.2 collective-permute-start.6
  32.4 0.3 collective-permute-start.7
  32.7 0.2 collective-permute-start.8
  32.9 0.3 collective-permute-start.9
  33.3 1.1 %collective-permute-done.6.refs_5_ = bf16[256,512]{1,0:T(8,128)(2,1)S(1)} collective-permute-done((bf16[256,512]{1,0:T(8,128)(2,1)S(1)}, bf16[256,512]{1,0:T(8,128)(2,1)S(1)}, u32[]{:S(2)}, u32[]{:S(2)}) %collective-permute-start.6) | collective-permute-done | bytes 262176 | tf_op jit(solution)/shard_map/w_core/ppermute | solution.py:277
  34.4 0.2 collective-permute-done.7.refs_6_
  34.6 0.4 collective-permute-done.8.refs_7_
  34.9 0.4 collective-permute-done.9.refs_8_
  35.3 4.0 %base.1 = (bf16[128,2560]{1,0:T(8,128)(2,1)S(1)}, bf16[128,1536]{1,0:T(8,128)(2,1)S(1)}, bf16[128,2560]{1,0:T(8,128)(2,1)S(1)}, bf16[128,1536]{1,0:T(8,128)(2,1)S(1)}) custom-call(bf16[128,512]{1,0:T(8,128)(2,1)S(1)} %copy-done.2, bf16[384,512]{1,0:T(8,128)(2,1)S(1)} %collective-permute-done.4.refs_0_, bf16[256,512]{1,0:T(8,128)(2,1)} %copy-done.8, ...), custom_call_target="tpu_custom_call" | custom-call | flops 10737418240 | bytes 41943040 | tf_op jit(solution)/shard_map/base/pallas_call | solution.py:356
  39.3 0.9 collective-permute-start.13
  40.2 1.9 %collective-permute-start.12 = (bf16[128,1536]{1,0:T(8,128)(2,1)S(1)}, bf16[128,1536]{1,0:T(8,128)(2,1)S(1)}, u32[]{:S(2)}, u32[]{:S(2)}) collective-permute-start(bf16[128,1536]{1,0:T(8,128)(2,1)S(1)} %get-tuple-element.47), channel_id=1, source_target_pairs={{0,4},{1,5},{2,6},{3,7},{4,0},{5,1},{6,2},{7,3},{8,12},{9,13},{10,... | collective-permute-start | bytes 1179656 | tf_op jit(solution)/shard_map/pieces20/ppermute | solution.py:277
  42.0 14.1 %collective-permute-done.12.refs_1_ = bf16[128,1536]{1,0:T(8,128)(2,1)S(1)} collective-permute-done((bf16[128,1536]{1,0:T(8,128)(2,1)S(1)}, bf16[128,1536]{1,0:T(8,128)(2,1)S(1)}, u32[]{:S(2)}, u32[]{:S(2)}) %collective-permute-start.12) | collective-permute-done | bytes 393248 | tf_op jit(solution)/shard_map/pieces20/ppermute | solution.py:277
  56.1 0.2 collective-permute-done.13.refs_2_
  56.4 1.8 %copy-done.1 = bf16[128,8192]{1,0:T(8,128)(2,1)S(1)} copy-done((bf16[128,8192]{1,0:T(8,128)(2,1)S(1)}, bf16[128,8192]{1,0:T(8,128)(2,1)}, u32[]{:S(2)}) %copy-start.1) | copy-done | bytes 2097176
  58.2 2.0 %middle.1 = (bf16[128,64]{1,0:T(8,128)(2,1)S(1)}, bf16[32,144,128]{2,1,0:T(8,128)(2,1)}) custom-call(bf16[128,8192]{1,0:T(8,128)(2,1)S(1)} %copy-done.1, bf16[128,512]{1,0:T(8,128)(2,1)S(1)} %copy-done.2, bf16[16,272,128]{2,1,0:T(8,128)(2,1)S(1)} %all-to-all-done.1.got), custom_call_target="tpu_custom_call" | custom-call | flops 268435456 | bytes 4325376 | tf_op jit(solution)/shard_map/middle/pallas_call | solution.py:381
  60.3 5.6 %all-to-all-start.2 = ((bf16[32,144,128]{2,1,0:T(8,128)(2,1)}), bf16[32,144,128]{2,1,0:T(8,128)(2,1)S(1)}, u32[]{:S(2)}, u32[]{:S(2)}) async-start(bf16[32,144,128]{2,1,0:T(8,128)(2,1)} %get-tuple-element.50), calls=%async_computation.2 | async-start | bytes 2359296 | tf_op jit(solution)/shard_map/gradients_back/all_to_all | solution.py:400
  65.9 2.7 %collective-permute-start.15 = (bf16[128,1536]{1,0:T(8,128)(2,1)}, bf16[128,1536]{1,0:T(8,128)(2,1)}, u32[]{:S(2)}, u32[]{:S(2)}) collective-permute-start(bf16[128,1536]{1,0:T(8,128)(2,1)} %copy-done.7), channel_id=1, source_target_pairs={{0,5},{1,4},{2,7},{3,6},{4,1},{5,0},{6,3},{7,2},{8,13},{9,12},{10,... | collective-permute-start | bytes 1179656 | tf_op jit(solution)/shard_map/pieces21/ppermute | solution.py:277
  68.6 0.6 collective-permute-start.14
  69.2 20.2 %collective-permute-done.14.refs_1_ = s32[16]{0:T(128)S(1)} collective-permute-done((s32[16]{0:T(128)S(1)}, s32[16]{0:T(128)S(1)}, u32[]{:S(2)}, u32[]{:S(2)}) %collective-permute-start.14) | collective-permute-done | bytes 96 | tf_op jit(solution)/shard_map/slots_dp/ppermute | solution.py:277
  89.4 5.5 %all-to-all-done.2.refs_2_ = bf16[32,144,128]{2,1,0:T(8,128)(2,1)S(1)} async-done(((bf16[32,144,128]{2,1,0:T(8,128)(2,1)}), bf16[32,144,128]{2,1,0:T(8,128)(2,1)S(1)}, u32[]{:S(2)}, u32[]{:S(2)}) %all-to-all-start.2) | async-done | bytes 1179680 | tf_op jit(solution)/shard_map/gradients_back/all_to_all | solution.py:400
  94.9 2.0 %sum_all.1 = (bf16[8,64,256]{2,1,0:T(8,128)(2,1)S(1)}, bf16[8,64,256]{2,1,0:T(8,128)(2,1)S(1)}, bf16[8,32,64]{2,1,0:T(8,128)(2,1)}) custom-call(s32[16]{0:T(128)S(1)} %select_reduce_fusion.slots.refs_0_, s32[16]{0:T(128)S(1)} %collective-permute-done.14.refs_1_, bf16[32,144,128]{2,1,0:T(8,128)(2,1)S(1)} %all-to-all-done.2.refs_2_), custom_call_target="tpu_custom_call" | custom-call | bytes 2228224 | tf_op jit(solution)/shard_map/sum_all/pallas_call | solution.py:420
  97.0 1.5 %collective-permute-start.16 = (bf16[8,64,256]{2,1,0:T(8,128)(2,1)S(1)}, bf16[8,64,256]{2,1,0:T(8,128)(2,1)S(1)}, u32[]{:S(2)}, u32[]{:S(2)}) collective-permute-start(bf16[8,64,256]{2,1,0:T(8,128)(2,1)S(1)} %get-tuple-element.59), channel_id=1, source_target_pairs={{0,1},{1,0},{2,3},{3,2},{4,5},{5,4},{6,7},{7,6},{8,9},{9,8},{10,11... | collective-permute-start | bytes 786440 | tf_op jit(solution)/shard_map/grads_dp/ppermute | solution.py:277
  98.5 3.1 %rows.1 = bf16[128,8192]{1,0:T(8,128)(2,1)} custom-call(bf16[128,64]{1,0:T(8,128)(2,1)S(1)} %get-tuple-element.60.hidden, bf16[16,272,128]{2,1,0:T(8,128)(2,1)S(1)} %all-to-all-done.1.got, bf16[128,2560]{1,0:T(8,128)(2,1)S(1)} %get-tuple-element.61.refs_0_, bf16[128,1536]{1,0:T(8,128)(2,1)S(1)} %copy-done.6, bf16[128,2560]{1,0:T(8,128)(2,1)S(1)} %copy-done.4, ...), custom_call_target="tpu_custom_call" | custom-call | flops 134217728 | bytes 5308416 | tf_op jit(solution)/shard_map/rows/pallas_call | solution.py:406
  101.6 3.4 %collective-permute-done.16.refs_1_ = bf16[8,64,256]{2,1,0:T(8,128)(2,1)S(1)} collective-permute-done((bf16[8,64,256]{2,1,0:T(8,128)(2,1)S(1)}, bf16[8,64,256]{2,1,0:T(8,128)(2,1)S(1)}, u32[]{:S(2)}, u32[]{:S(2)}) %collective-permute-start.16) | collective-permute-done | bytes 262176 | tf_op jit(solution)/shard_map/grads_dp/ppermute | solution.py:277
  104.9 0.8 join.1
  (29 shorter events, 0.1 us)
Async XLA Ops:
  0.6 3.1 %copy-start = (bf16[512,512]{1,0:T(8,128)(2,1)S(1)}, bf16[512,512]{1,0:T(8,128)(2,1)}, u32[]{:S(2)}) copy-start(bf16[512,512]{1,0:T(8,128)(2,1)} %param.9) | copy-start | bytes 1572868
  0.6 21.3 %copy-start.2 = (bf16[128,512]{1,0:T(8,128)(2,1)S(1)}, bf16[128,512]{1,0:T(8,128)(2,1)}, u32[]{:S(2)}) copy-start(bf16[128,512]{1,0:T(8,128)(2,1)} %g.1) | copy-start | bytes 393220
  0.7 14.6 %copy-start.9 = (bf16[8,32,64]{2,1,0:T(8,128)(2,1)S(1)}, bf16[8,32,64]{2,1,0:T(8,128)(2,1)}, u32[]{:S(2)}) copy-start(bf16[8,32,64]{2,1,0:T(8,128)(2,1)} %refs_2_) | copy-start | bytes 98308
  0.7 23.3 %copy-start.11 = (s32[16]{0:T(128)S(1)}, s32[16]{0:T(128)}, u32[]{:S(2)}) copy-start(s32[16]{0:T(128)} %param.13) | copy-start | bytes 196
  0.7 21.3 %collective-permute-start = (bf16[8,64,512]{2,1,0:T(8,128)(2,1)}, bf16[8,64,512]{2,1,0:T(8,128)(2,1)S(1)}, u32[]{:S(2)}, u32[]{:S(2)}) collective-permute-start(bf16[8,64,512]{2,1,0:T(8,128)(2,1)} %bitcast.4), channel_id=1, source_target_pairs={{0,1},{1,0},{2,3},{3,2},{4,5},{5,4},{6,7},{7,6},{8,9},{9,8},{10,11... | collective-permute-start | bytes 1572872 | tf_op jit(solution)/shard_map/down_dp/ppermute | solution.py:277
  3.7 28.5 %copy-start.8 = (bf16[256,512]{1,0:T(8,128)(2,1)}, bf16[256,512]{1,0:T(8,128)(2,1)S(1)}, u32[]{:S(2)}) copy-start(bf16[256,512]{1,0:T(8,128)(2,1)S(1)} %constant_dynamic-slice_fusion.refs_1_) | copy-start | bytes 786436
  4.8 17.2 %collective-permute-start.4 = (bf16[384,512]{1,0:T(8,128)(2,1)S(1)}, bf16[384,512]{1,0:T(8,128)(2,1)S(1)}, u32[]{:S(2)}, u32[]{:S(2)}) collective-permute-start(bf16[384,512]{1,0:T(8,128)(2,1)S(1)} %pad_maximum_fusion), channel_id=1, source_target_pairs={{0,4},{2,6},{4,0},{6,2},{8,12},{10,14},{12,8},{14,10},{16,20},{18,... | collective-permute-start | bytes 1179656 | tf_op jit(solution)/shard_map/g_w_layer/ppermute | solution.py:277
  6.3 15.6 %collective-permute-start.3 = (bf16[256,512]{1,0:T(8,128)(2,1)S(1)}, bf16[256,512]{1,0:T(8,128)(2,1)}, u32[]{:S(2)}, u32[]{:S(2)}) collective-permute-start(bf16[256,512]{1,0:T(8,128)(2,1)S(1)} %constant_dynamic-slice_fusion.refs_1_), channel_id=1, source_target_pairs={{0,16},{2,18},{4,20},{6,22},{8,24},{10,26},{12,28},{14,30},{16,0},... | collective-permute-start | bytes 786440 | tf_op jit(solution)/shard_map/w_layers/ppermute | solution.py:277
  8.9 13.0 %collective-permute-start.2 = (bf16[256,512]{1,0:T(8,128)(2,1)S(1)}, bf16[256,512]{1,0:T(8,128)(2,1)S(1)}, u32[]{:S(2)}, u32[]{:S(2)}) collective-permute-start(bf16[256,512]{1,0:T(8,128)(2,1)S(1)} %constant_dynamic-slice_fusion.refs_1_), channel_id=1, source_target_pairs={{0,8},{2,10},{4,12},{6,14},{8,0},{10,2},{12,4},{14,6},{16,24},{18,... | collective-permute-start | bytes 786440 | tf_op jit(solution)/shard_map/w_layers/ppermute | solution.py:277
  11.8 9.8 %all-to-all-start = ((s32[16,1,128]{2,1,0:T(1,128)}), s32[16,1,128]{2,1,0:T(1,128)S(1)}, u32[]{:S(2)}, u32[]{:S(2)}) async-start(s32[16,1,128]{2,1,0:T(1,128)} %broadcast_in_dim.24), calls=%async_computation | async-start | bytes 16384 | tf_op jit(solution)/shard_map/ids/all_to_all | solution.py:307
  15.2 6.7 %collective-permute-start.1 = (bf16[8,32,64]{2,1,0:T(8,128)(2,1)S(1)}, bf16[8,32,64]{2,1,0:T(8,128)(2,1)S(1)}, u32[]{:S(2)}, u32[]{:S(2)}) collective-permute-start(bf16[8,32,64]{2,1,0:T(8,128)(2,1)S(1)} %copy-done.9), channel_id=1, source_target_pairs={{0,1},{1,0},{2,3},{3,2},{4,5},{5,4},{6,7},{7,6},{8,9},{9,8},{10,11... | collective-permute-start | bytes 98312 | tf_op jit(solution)/shard_map/up_dp/ppermute | solution.py:277
  21.9 5.2 %copy-start.10 = (bf16[256,512]{1,0:T(8,128)(2,1)}, bf16[256,512]{1,0:T(8,128)(2,1)S(1)}, u32[]{:S(2)}) copy-start(bf16[256,512]{1,0:T(8,128)(2,1)S(1)} %collective-permute-done.2.refs_2_) | copy-start | bytes 786436
  22.0 10.7 %collective-permute-start.11 = (bf16[256,512]{1,0:T(8,128)(2,1)S(1)}, bf16[256,512]{1,0:T(8,128)(2,1)S(1)}, u32[]{:S(2)}, u32[]{:S(2)}) collective-permute-start(bf16[256,512]{1,0:T(8,128)(2,1)S(1)} %pad_maximum_fusion.1), channel_id=1, source_target_pairs={{0,1},{1,0},{2,3},{3,2},{4,5},{5,4},{6,7},{7,6},{8,9},{9,8},{10,11... | collective-permute-start | bytes 786440 | tf_op jit(solution)/shard_map/g_dp/ppermute | solution.py:277
  23.2 9.7 %collective-permute-start.5 = (bf16[256,512]{1,0:T(8,128)(2,1)}, bf16[256,512]{1,0:T(8,128)(2,1)}, u32[]{:S(2)}, u32[]{:S(2)}) collective-permute-start(bf16[256,512]{1,0:T(8,128)(2,1)} %collective-permute-done.3.refs_3_), channel_id=1, source_target_pairs={{0,8},{2,10},{4,12},{6,14},{8,0},{10,2},{12,4},{14,6},{16,24},{18,... | collective-permute-start | bytes 786440 | tf_op jit(solution)/shard_map/w_last/ppermute | solution.py:277
  27.2 29.2 %all-to-all-start.1 = ((bf16[16,272,128]{2,1,0:T(8,128)(2,1)}), bf16[16,272,128]{2,1,0:T(8,128)(2,1)S(1)}, u32[]{:S(2)}, u32[]{:S(2)}) async-start(bf16[16,272,128]{2,1,0:T(8,128)(2,1)} %select.3), calls=%async_computation.1 | async-start | bytes 2228224 | tf_op jit(solution)/shard_map/adapters_to_blocks/all_to_all | solution.py:346
  31.8 3.1 %collective-permute-start.10 = (bf16[384,512]{1,0:T(8,128)(2,1)S(1)}, bf16[384,512]{1,0:T(8,128)(2,1)S(1)}, u32[]{:S(2)}, u32[]{:S(2)}) collective-permute-start(bf16[384,512]{1,0:T(8,128)(2,1)S(1)} %collective-permute-done.4.refs_0_), channel_id=1, source_target_pairs={{0,2},{2,0},{4,6},{6,4},{8,10},{10,8},{12,14},{14,12},{16,18},{18,... | collective-permute-start | bytes 1179656 | tf_op jit(solution)/shard_map/w_core/ppermute | solution.py:277
  32.2 2.1 %collective-permute-start.6 = (bf16[256,512]{1,0:T(8,128)(2,1)S(1)}, bf16[256,512]{1,0:T(8,128)(2,1)S(1)}, u32[]{:S(2)}, u32[]{:S(2)}) collective-permute-start(bf16[256,512]{1,0:T(8,128)(2,1)S(1)} %constant_dynamic-slice_fusion.refs_1_), channel_id=1, source_target_pairs={{0,2},{2,0},{4,6},{6,4},{8,10},{10,8},{12,14},{14,12},{16,18},{18,... | collective-permute-start | bytes 786440 | tf_op jit(solution)/shard_map/w_core/ppermute | solution.py:277
  32.4 2.2 %collective-permute-start.7 = (bf16[256,512]{1,0:T(8,128)(2,1)}, bf16[256,512]{1,0:T(8,128)(2,1)S(1)}, u32[]{:S(2)}, u32[]{:S(2)}) collective-permute-start(bf16[256,512]{1,0:T(8,128)(2,1)} %copy-done.10), channel_id=1, source_target_pairs={{0,2},{2,0},{4,6},{6,4},{8,10},{10,8},{12,14},{14,12},{16,18},{18,... | collective-permute-start | bytes 786440 | tf_op jit(solution)/shard_map/w_core/ppermute | solution.py:277
  32.7 2.2 %collective-permute-start.8 = (bf16[256,512]{1,0:T(8,128)(2,1)}, bf16[256,512]{1,0:T(8,128)(2,1)S(1)}, u32[]{:S(2)}, u32[]{:S(2)}) collective-permute-start(bf16[256,512]{1,0:T(8,128)(2,1)} %collective-permute-done.3.refs_3_), channel_id=1, source_target_pairs={{0,2},{2,0},{4,6},{6,4},{8,10},{10,8},{12,14},{14,12},{16,18},{18,... | collective-permute-start | bytes 786440 | tf_op jit(solution)/shard_map/w_core/ppermute | solution.py:277
  32.9 2.4 %collective-permute-start.9 = (bf16[256,512]{1,0:T(8,128)(2,1)}, bf16[256,512]{1,0:T(8,128)(2,1)S(1)}, u32[]{:S(2)}, u32[]{:S(2)}) collective-permute-start(bf16[256,512]{1,0:T(8,128)(2,1)} %collective-permute-done.5.refs_4_), channel_id=1, source_target_pairs={{0,2},{2,0},{4,6},{6,4},{8,10},{10,8},{12,14},{14,12},{16,18},{18,... | collective-permute-start | bytes 786440 | tf_op jit(solution)/shard_map/w_core/ppermute | solution.py:277
  39.3 16.8 %copy-start.7 = (bf16[128,1536]{1,0:T(8,128)(2,1)}, bf16[128,1536]{1,0:T(8,128)(2,1)S(1)}, u32[]{:S(2)}) copy-start(bf16[128,1536]{1,0:T(8,128)(2,1)S(1)} %get-tuple-element.57) | copy-start | bytes 1179652
  39.3 17.1 %collective-permute-start.13 = (bf16[128,2560]{1,0:T(8,128)(2,1)S(1)}, bf16[128,2560]{1,0:T(8,128)(2,1)S(1)}, u32[]{:S(2)}, u32[]{:S(2)}) collective-permute-start(bf16[128,2560]{1,0:T(8,128)(2,1)S(1)} %get-tuple-element.48), channel_id=1, source_target_pairs={{0,1},{1,0},{2,3},{3,2},{4,5},{5,4},{6,7},{7,6},{8,9},{9,8},{10,11... | collective-permute-start | bytes 1966088 | tf_op jit(solution)/shard_map/pieces01/ppermute | solution.py:277
  40.2 16.0 %collective-permute-start.12 = (bf16[128,1536]{1,0:T(8,128)(2,1)S(1)}, bf16[128,1536]{1,0:T(8,128)(2,1)S(1)}, u32[]{:S(2)}, u32[]{:S(2)}) collective-permute-start(bf16[128,1536]{1,0:T(8,128)(2,1)S(1)} %get-tuple-element.47), channel_id=1, source_target_pairs={{0,4},{1,5},{2,6},{3,7},{4,0},{5,1},{6,2},{7,3},{8,12},{9,13},{10,... | collective-permute-start | bytes 1179656 | tf_op jit(solution)/shard_map/pieces20/ppermute | solution.py:277
  56.1 4.1 %copy-start.5 = (bf16[128,1536]{1,0:T(8,128)(2,1)}, bf16[128,1536]{1,0:T(8,128)(2,1)S(1)}, u32[]{:S(2)}) copy-start(bf16[128,1536]{1,0:T(8,128)(2,1)S(1)} %collective-permute-done.12.refs_1_) | copy-start | bytes 1179652
  56.4 3.9 %copy-start.3 = (bf16[128,2560]{1,0:T(8,128)(2,1)}, bf16[128,2560]{1,0:T(8,128)(2,1)S(1)}, u32[]{:S(2)}) copy-start(bf16[128,2560]{1,0:T(8,128)(2,1)S(1)} %collective-permute-done.13.refs_2_) | copy-start | bytes 1966084
  56.4 1.8 %copy-start.1 = (bf16[128,8192]{1,0:T(8,128)(2,1)S(1)}, bf16[128,8192]{1,0:T(8,128)(2,1)}, u32[]{:S(2)}) copy-start(bf16[128,8192]{1,0:T(8,128)(2,1)} %x.1) | copy-start | bytes 6291460
  60.3 34.7 %all-to-all-start.2 = ((bf16[32,144,128]{2,1,0:T(8,128)(2,1)}), bf16[32,144,128]{2,1,0:T(8,128)(2,1)S(1)}, u32[]{:S(2)}, u32[]{:S(2)}) async-start(bf16[32,144,128]{2,1,0:T(8,128)(2,1)} %get-tuple-element.50), calls=%async_computation.2 | async-start | bytes 2359296 | tf_op jit(solution)/shard_map/gradients_back/all_to_all | solution.py:400
  65.9 29.1 %collective-permute-start.15 = (bf16[128,1536]{1,0:T(8,128)(2,1)}, bf16[128,1536]{1,0:T(8,128)(2,1)}, u32[]{:S(2)}, u32[]{:S(2)}) collective-permute-start(bf16[128,1536]{1,0:T(8,128)(2,1)} %copy-done.7), channel_id=1, source_target_pairs={{0,5},{1,4},{2,7},{3,6},{4,1},{5,0},{6,3},{7,2},{8,13},{9,12},{10,... | collective-permute-start | bytes 1179656 | tf_op jit(solution)/shard_map/pieces21/ppermute | solution.py:277
  68.6 20.8 %collective-permute-start.14 = (s32[16]{0:T(128)S(1)}, s32[16]{0:T(128)S(1)}, u32[]{:S(2)}, u32[]{:S(2)}) collective-permute-start(s32[16]{0:T(128)S(1)} %select_reduce_fusion.slots.refs_0_), channel_id=1, source_target_pairs={{0,1},{1,0},{2,3},{3,2},{4,5},{5,4},{6,7},{7,6},{8,9},{9,8},{10,11... | collective-permute-start | bytes 200 | tf_op jit(solution)/shard_map/slots_dp/ppermute | solution.py:277
  94.9 3.6 %copy-start.4 = (bf16[128,2560]{1,0:T(8,128)(2,1)S(1)}, bf16[128,2560]{1,0:T(8,128)(2,1)}, u32[]{:S(2)}) copy-start(bf16[128,2560]{1,0:T(8,128)(2,1)} %copy-done.3) | copy-start | bytes 1966084
  94.9 3.6 %copy-start.6 = (bf16[128,1536]{1,0:T(8,128)(2,1)S(1)}, bf16[128,1536]{1,0:T(8,128)(2,1)}, u32[]{:S(2)}) copy-start(bf16[128,1536]{1,0:T(8,128)(2,1)} %copy-done.5) | copy-start | bytes 1179652
  97.0 8.0 %collective-permute-start.16 = (bf16[8,64,256]{2,1,0:T(8,128)(2,1)S(1)}, bf16[8,64,256]{2,1,0:T(8,128)(2,1)S(1)}, u32[]{:S(2)}, u32[]{:S(2)}) collective-permute-start(bf16[8,64,256]{2,1,0:T(8,128)(2,1)S(1)} %get-tuple-element.59), channel_id=1, source_target_pairs={{0,1},{1,0},{2,3},{3,2},{4,5},{5,4},{6,7},{7,6},{8,9},{9,8},{10,11... | collective-permute-start | bytes 786440 | tf_op jit(solution)/shard_map/grads_dp/ppermute | solution.py:277

commit v7 on v6

--- a/solution.py
+++ b/solution.py
@@ -227,14 +227,14 @@
     tiles = width // lanes
     here = lax.axis_index("dp")
 
-    @pl.loop(0, slots[0].shape[0])
+    @pl.loop(0, slots[0].shape[0], unroll=4)
     def _(k):
         for j in range(dp_count):
             place_of[j, slots[j][k]] = k * dp_count + (here ^ j)
 
     for step, out in zip(range(first, first + steps), outs):
 
-        @pl.loop(0, own)
+        @pl.loop(0, own, unroll=4)
         def _(place):
             slot = (here ^ step) * own + place
             total = got[place_of[0, slot]].astype(F32)

time: 106 us -> 106 us (level)
  transfers between devices with their start and end apart: 20 -> 20, of which waited for: 10 -> 10; matrix products, arithmetic and copies ran while one was open for 2% -> 2% of each run, Pallas kernels for 9% -> 10%
where the time goes in v7:
time: 106 us; the launch traced here: 105 us
  waiting for transfers between devices  50.8 us (48%)
  starting transfers between devices  34.4 us (32%)
  Pallas kernels  14.4 us (14%)
  local copies, waits for them, and re-layouts  2.9 us (3%)
  between operations  1.51 us (1%)
  other arithmetic  1.23 us (1%)
    ppermute x17, waiting for transfers between devices, exchange(): return lax.ppermute(array, axis, xor_pairs(axis_count(axis), bits))  40 us
    ppermute x17, starting transfers between devices, exchange(): return lax.ppermute(array, axis, xor_pairs(axis_count(axis), bits))  20.7 us
    all_to_all x1, starting transfers between devices, on_device(): returned = lax.all_to_all(back, axes, 0, 0, tiled=True)  5.62 us
    all_to_all x1, waiting for transfers between devices, on_device(): returned = lax.all_to_all(back, axes, 0, 0, tiled=True)  5.52 us
    all_to_all x1, waiting for transfers between devices, on_device(): lax.all_to_all(jnp.broadcast_to(tenant_ids[:, None, None], (fsdp_count, 1...  5.26 us
    all_to_all x1, starting transfers between devices, on_device(): got = lax.all_to_all(sent, 'fsdp', 0, 0, tiled=True)  4.61 us
    pallas_call x1, Pallas kernels, on_device(): pl.pallas_call(functools.partial(base_kernel, rels, len(near), layers), o...  4.01 us
    all_to_all x1, starting transfers between devices, on_device(): lax.all_to_all(jnp.broadcast_to(tenant_ids[:, None, None], (fsdp_count, 1...  3.47 us
  transfers between devices with their start and end apart: 20, of which 10 were waited for; matrix products, arithmetic and copies ran while one was open for 2% of the time, Pallas kernels for 10%

profile of v7, /device:TPU:0, one launch (start us, length us, event | category | flops | bytes accessed | tf_op | source)
XLA Modules:
  0.0 105.2 jit_solution(2211195529972435559)
XLA Ops:
  0.6 0.0 copy-start
  0.6 0.0 copy-start.2
  0.7 0.0 copy-start.9
  0.7 3.0 %collective-permute-start = (bf16[8,64,512]{2,1,0:T(8,128)(2,1)}, bf16[8,64,512]{2,1,0:T(8,128)(2,1)S(1)}, u32[]{:S(2)}, u32[]{:S(2)}) collective-permute-start(bf16[8,64,512]{2,1,0:T(8,128)(2,1)} %bitcast.4), channel_id=1, source_target_pairs={{0,1},{1,0},{2,3},{3,2},{4,5},{5,4},{6,7},{7,6},{8,9},{9,8},{10,11... | collective-permute-start | bytes 1572872 | tf_op jit(solution)/shard_map/down_dp/ppermute | solution.py:277
  3.7 0.0 copy-start.8
  3.7 1.0 pad_maximum_fusion
  4.8 1.6 %collective-permute-start.4 = (bf16[384,512]{1,0:T(8,128)(2,1)S(1)}, bf16[384,512]{1,0:T(8,128)(2,1)S(1)}, u32[]{:S(2)}, u32[]{:S(2)}) collective-permute-start(bf16[384,512]{1,0:T(8,128)(2,1)S(1)} %pad_maximum_fusion), channel_id=1, source_target_pairs={{0,4},{2,6},{4,0},{6,2},{8,12},{10,14},{12,8},{14,10},{16,20},{18,... | collective-permute-start | bytes 1179656 | tf_op jit(solution)/shard_map/g_w_layer/ppermute | solution.py:277
  6.3 2.6 %collective-permute-start.3 = (bf16[256,512]{1,0:T(8,128)(2,1)S(1)}, bf16[256,512]{1,0:T(8,128)(2,1)}, u32[]{:S(2)}, u32[]{:S(2)}) collective-permute-start(bf16[256,512]{1,0:T(8,128)(2,1)S(1)} %constant_dynamic-slice_fusion.refs_1_), channel_id=1, source_target_pairs={{0,16},{2,18},{4,20},{6,22},{8,24},{10,26},{12,28},{14,30},{16,0},... | collective-permute-start | bytes 786440 | tf_op jit(solution)/shard_map/w_layers/ppermute | solution.py:277
  8.9 1.6 %collective-permute-start.2 = (bf16[256,512]{1,0:T(8,128)(2,1)S(1)}, bf16[256,512]{1,0:T(8,128)(2,1)S(1)}, u32[]{:S(2)}, u32[]{:S(2)}) collective-permute-start(bf16[256,512]{1,0:T(8,128)(2,1)S(1)} %constant_dynamic-slice_fusion.refs_1_), channel_id=1, source_target_pairs={{0,8},{2,10},{4,12},{6,14},{8,0},{10,2},{12,4},{14,6},{16,24},{18,... | collective-permute-start | bytes 786440 | tf_op jit(solution)/shard_map/w_layers/ppermute | solution.py:277
  11.2 0.6 broadcast_in_dim.24
  11.8 3.5 %all-to-all-start = ((s32[16,1,128]{2,1,0:T(1,128)}), s32[16,1,128]{2,1,0:T(1,128)S(1)}, u32[]{:S(2)}, u32[]{:S(2)}) async-start(s32[16,1,128]{2,1,0:T(1,128)} %broadcast_in_dim.24), calls=%async_computation | async-start | bytes 16384 | tf_op jit(solution)/shard_map/ids/all_to_all | solution.py:307
  15.2 1.0 collective-permute-start.1
  16.3 5.3 %all-to-all-done = s32[16,1,128]{2,1,0:T(1,128)S(1)} async-done(((s32[16,1,128]{2,1,0:T(1,128)}), s32[16,1,128]{2,1,0:T(1,128)S(1)}, u32[]{:S(2)}, u32[]{:S(2)}) %all-to-all-start) | async-done | bytes 8224 | tf_op jit(solution)/shard_map/ids/all_to_all | solution.py:307
  21.5 0.4 slice_reduce_fusion
  21.9 0.0 collective-permute-done.1.refs_3_
  21.9 0.0 collective-permute-done.3.refs_3_
  22.0 0.0 collective-permute-done.refs_1_
  22.0 1.2 %collective-permute-start.11 = (bf16[256,512]{1,0:T(8,128)(2,1)S(1)}, bf16[256,512]{1,0:T(8,128)(2,1)S(1)}, u32[]{:S(2)}, u32[]{:S(2)}) collective-permute-start(bf16[256,512]{1,0:T(8,128)(2,1)S(1)} %pad_maximum_fusion.1), channel_id=1, source_target_pairs={{0,1},{1,0},{2,3},{3,2},{4,5},{5,4},{6,7},{7,6},{8,9},{9,8},{10,11... | collective-permute-start | bytes 786440 | tf_op jit(solution)/shard_map/g_dp/ppermute | solution.py:277
  23.2 0.8 collective-permute-start.5
  24.0 0.2 select_reduce_fusion.slots.refs_0_
  24.2 3.0 %select.3 = bf16[16,272,128]{2,1,0:T(8,128)(2,1)} custom-call(s32[16]{0:T(128)S(1)} %select_reduce_fusion.slots.refs_0_, bf16[8,64,512]{2,1,0:T(8,128)(2,1)} %bitcast.5, bf16[8,64,512]{2,1,0:T(8,128)(2,1)S(1)} %collective-permute-done.refs_1_, bf16[8,32,64]{2,1,0:T(8,128)(2,1)} %refs_2_, bf16[8,32,64]{2,1,0:T(8,128)(2,1)S(1)} %collective-permute-done.1.refs_3_), custom_call_target="tpu_custom_call" | custom-call | bytes 2228224 | tf_op jit(solution)/shard_map/select/pallas_call | solution.py:333
  27.2 4.6 %all-to-all-start.1 = ((bf16[16,272,128]{2,1,0:T(8,128)(2,1)}), bf16[16,272,128]{2,1,0:T(8,128)(2,1)S(1)}, u32[]{:S(2)}, u32[]{:S(2)}) async-start(bf16[16,272,128]{2,1,0:T(8,128)(2,1)} %select.3), calls=%async_computation.1 | async-start | bytes 2228224 | tf_op jit(solution)/shard_map/adapters_to_blocks/all_to_all | solution.py:346
  31.8 0.4 collective-permute-start.10
  32.2 0.2 collective-permute-start.6
  32.4 0.3 collective-permute-start.7
  32.7 0.2 collective-permute-start.8
  32.9 0.3 collective-permute-start.9
  33.2 1.1 %collective-permute-done.6.refs_5_ = bf16[256,512]{1,0:T(8,128)(2,1)S(1)} collective-permute-done((bf16[256,512]{1,0:T(8,128)(2,1)S(1)}, bf16[256,512]{1,0:T(8,128)(2,1)S(1)}, u32[]{:S(2)}, u32[]{:S(2)}) %collective-permute-start.6) | collective-permute-done | bytes 262176 | tf_op jit(solution)/shard_map/w_core/ppermute | solution.py:277
  34.3 0.2 collective-permute-done.7.refs_6_
  34.6 0.4 collective-permute-done.8.refs_7_
  34.9 0.4 collective-permute-done.9.refs_8_
  35.3 4.0 %base.1 = (bf16[128,2560]{1,0:T(8,128)(2,1)S(1)}, bf16[128,1536]{1,0:T(8,128)(2,1)S(1)}, bf16[128,2560]{1,0:T(8,128)(2,1)S(1)}, bf16[128,1536]{1,0:T(8,128)(2,1)S(1)}) custom-call(bf16[128,512]{1,0:T(8,128)(2,1)S(1)} %copy-done.2, bf16[384,512]{1,0:T(8,128)(2,1)S(1)} %collective-permute-done.4.refs_0_, bf16[256,512]{1,0:T(8,128)(2,1)} %copy-done.8, ...), custom_call_target="tpu_custom_call" | custom-call | flops 10737418240 | bytes 41943040 | tf_op jit(solution)/shard_map/base/pallas_call | solution.py:356
  39.3 0.9 collective-permute-start.13
  40.2 1.9 %collective-permute-start.12 = (bf16[128,1536]{1,0:T(8,128)(2,1)S(1)}, bf16[128,1536]{1,0:T(8,128)(2,1)S(1)}, u32[]{:S(2)}, u32[]{:S(2)}) collective-permute-start(bf16[128,1536]{1,0:T(8,128)(2,1)S(1)} %get-tuple-element.47), channel_id=1, source_target_pairs={{0,4},{1,5},{2,6},{3,7},{4,0},{5,1},{6,2},{7,3},{8,12},{9,13},{10,... | collective-permute-start | bytes 1179656 | tf_op jit(solution)/shard_map/pieces20/ppermute | solution.py:277
  42.0 14.1 %collective-permute-done.12.refs_1_ = bf16[128,1536]{1,0:T(8,128)(2,1)S(1)} collective-permute-done((bf16[128,1536]{1,0:T(8,128)(2,1)S(1)}, bf16[128,1536]{1,0:T(8,128)(2,1)S(1)}, u32[]{:S(2)}, u32[]{:S(2)}) %collective-permute-start.12) | collective-permute-done | bytes 393248 | tf_op jit(solution)/shard_map/pieces20/ppermute | solution.py:277
  56.2 0.2 collective-permute-done.13.refs_2_
  56.4 1.8 %copy-done.1 = bf16[128,8192]{1,0:T(8,128)(2,1)S(1)} copy-done((bf16[128,8192]{1,0:T(8,128)(2,1)S(1)}, bf16[128,8192]{1,0:T(8,128)(2,1)}, u32[]{:S(2)}) %copy-start.1) | copy-done | bytes 2097176
  58.2 2.0 %middle.1 = (bf16[128,64]{1,0:T(8,128)(2,1)S(1)}, bf16[32,144,128]{2,1,0:T(8,128)(2,1)}) custom-call(bf16[128,8192]{1,0:T(8,128)(2,1)S(1)} %copy-done.1, bf16[128,512]{1,0:T(8,128)(2,1)S(1)} %copy-done.2, bf16[16,272,128]{2,1,0:T(8,128)(2,1)S(1)} %all-to-all-done.1.got), custom_call_target="tpu_custom_call" | custom-call | flops 268435456 | bytes 4325376 | tf_op jit(solution)/shard_map/middle/pallas_call | solution.py:381
  60.3 5.6 %all-to-all-start.2 = ((bf16[32,144,128]{2,1,0:T(8,128)(2,1)}), bf16[32,144,128]{2,1,0:T(8,128)(2,1)S(1)}, u32[]{:S(2)}, u32[]{:S(2)}) async-start(bf16[32,144,128]{2,1,0:T(8,128)(2,1)} %get-tuple-element.50), calls=%async_computation.2 | async-start | bytes 2359296 | tf_op jit(solution)/shard_map/gradients_back/all_to_all | solution.py:400
  65.9 2.7 %collective-permute-start.15 = (bf16[128,1536]{1,0:T(8,128)(2,1)}, bf16[128,1536]{1,0:T(8,128)(2,1)}, u32[]{:S(2)}, u32[]{:S(2)}) collective-permute-start(bf16[128,1536]{1,0:T(8,128)(2,1)} %copy-done.7), channel_id=1, source_target_pairs={{0,5},{1,4},{2,7},{3,6},{4,1},{5,0},{6,3},{7,2},{8,13},{9,12},{10,... | collective-permute-start | bytes 1179656 | tf_op jit(solution)/shard_map/pieces21/ppermute | solution.py:277
  68.6 0.6 collective-permute-start.14
  69.2 20.2 %collective-permute-done.14.refs_1_ = s32[16]{0:T(128)S(1)} collective-permute-done((s32[16]{0:T(128)S(1)}, s32[16]{0:T(128)S(1)}, u32[]{:S(2)}, u32[]{:S(2)}) %collective-permute-start.14) | collective-permute-done | bytes 96 | tf_op jit(solution)/shard_map/slots_dp/ppermute | solution.py:277
  89.4 5.5 %all-to-all-done.2.refs_2_ = bf16[32,144,128]{2,1,0:T(8,128)(2,1)S(1)} async-done(((bf16[32,144,128]{2,1,0:T(8,128)(2,1)}), bf16[32,144,128]{2,1,0:T(8,128)(2,1)S(1)}, u32[]{:S(2)}, u32[]{:S(2)}) %all-to-all-start.2) | async-done | bytes 1179680 | tf_op jit(solution)/shard_map/gradients_back/all_to_all | solution.py:400
  94.9 1.5 %sum_all.1 = (bf16[8,64,256]{2,1,0:T(8,128)(2,1)S(1)}, bf16[8,64,256]{2,1,0:T(8,128)(2,1)S(1)}, bf16[8,32,64]{2,1,0:T(8,128)(2,1)}) custom-call(s32[16]{0:T(128)S(1)} %select_reduce_fusion.slots.refs_0_, s32[16]{0:T(128)S(1)} %collective-permute-done.14.refs_1_, bf16[32,144,128]{2,1,0:T(8,128)(2,1)S(1)} %all-to-all-done.2.refs_2_), custom_call_target="tpu_custom_call" | custom-call | bytes 2228224 | tf_op jit(solution)/shard_map/sum_all/pallas_call | solution.py:420
  96.4 1.5 %collective-permute-start.16 = (bf16[8,64,256]{2,1,0:T(8,128)(2,1)S(1)}, bf16[8,64,256]{2,1,0:T(8,128)(2,1)S(1)}, u32[]{:S(2)}, u32[]{:S(2)}) collective-permute-start(bf16[8,64,256]{2,1,0:T(8,128)(2,1)S(1)} %get-tuple-element.59), channel_id=1, source_target_pairs={{0,1},{1,0},{2,3},{3,2},{4,5},{5,4},{6,7},{7,6},{8,9},{9,8},{10,11... | collective-permute-start | bytes 786440 | tf_op jit(solution)/shard_map/grads_dp/ppermute | solution.py:277
  97.9 3.1 %rows.1 = bf16[128,8192]{1,0:T(8,128)(2,1)} custom-call(bf16[128,64]{1,0:T(8,128)(2,1)S(1)} %get-tuple-element.60.hidden, bf16[16,272,128]{2,1,0:T(8,128)(2,1)S(1)} %all-to-all-done.1.got, bf16[128,2560]{1,0:T(8,128)(2,1)S(1)} %get-tuple-element.61.refs_0_, bf16[128,1536]{1,0:T(8,128)(2,1)S(1)} %copy-done.6, bf16[128,2560]{1,0:T(8,128)(2,1)S(1)} %copy-done.4, ...), custom_call_target="tpu_custom_call" | custom-call | flops 134217728 | bytes 5308416 | tf_op jit(solution)/shard_map/rows/pallas_call | solution.py:406
  101.0 3.4 %collective-permute-done.16.refs_1_ = bf16[8,64,256]{2,1,0:T(8,128)(2,1)S(1)} collective-permute-done((bf16[8,64,256]{2,1,0:T(8,128)(2,1)S(1)}, bf16[8,64,256]{2,1,0:T(8,128)(2,1)S(1)}, u32[]{:S(2)}, u32[]{:S(2)}) %collective-permute-start.16) | collective-permute-done | bytes 262176 | tf_op jit(solution)/shard_map/grads_dp/ppermute | solution.py:277
  104.4 0.8 join.1
  (29 shorter events, 0.1 us)
Async XLA Ops:
  0.6 3.1 %copy-start = (bf16[512,512]{1,0:T(8,128)(2,1)S(1)}, bf16[512,512]{1,0:T(8,128)(2,1)}, u32[]{:S(2)}) copy-start(bf16[512,512]{1,0:T(8,128)(2,1)} %param.9) | copy-start | bytes 1572868
  0.6 21.3 %copy-start.2 = (bf16[128,512]{1,0:T(8,128)(2,1)S(1)}, bf16[128,512]{1,0:T(8,128)(2,1)}, u32[]{:S(2)}) copy-start(bf16[128,512]{1,0:T(8,128)(2,1)} %g.1) | copy-start | bytes 393220
  0.7 14.6 %copy-start.9 = (bf16[8,32,64]{2,1,0:T(8,128)(2,1)S(1)}, bf16[8,32,64]{2,1,0:T(8,128)(2,1)}, u32[]{:S(2)}) copy-start(bf16[8,32,64]{2,1,0:T(8,128)(2,1)} %refs_2_) | copy-start | bytes 98308
  0.7 23.3 %copy-start.11 = (s32[16]{0:T(128)S(1)}, s32[16]{0:T(128)}, u32[]{:S(2)}) copy-start(s32[16]{0:T(128)} %param.13) | copy-start | bytes 196
  0.7 21.3 %collective-permute-start = (bf16[8,64,512]{2,1,0:T(8,128)(2,1)}, bf16[8,64,512]{2,1,0:T(8,128)(2,1)S(1)}, u32[]{:S(2)}, u32[]{:S(2)}) collective-permute-start(bf16[8,64,512]{2,1,0:T(8,128)(2,1)} %bitcast.4), channel_id=1, source_target_pairs={{0,1},{1,0},{2,3},{3,2},{4,5},{5,4},{6,7},{7,6},{8,9},{9,8},{10,11... | collective-permute-start | bytes 1572872 | tf_op jit(solution)/shard_map/down_dp/ppermute | solution.py:277
  3.7 28.5 %copy-start.8 = (bf16[256,512]{1,0:T(8,128)(2,1)}, bf16[256,512]{1,0:T(8,128)(2,1)S(1)}, u32[]{:S(2)}) copy-start(bf16[256,512]{1,0:T(8,128)(2,1)S(1)} %constant_dynamic-slice_fusion.refs_1_) | copy-start | bytes 786436
  4.8 17.2 %collective-permute-start.4 = (bf16[384,512]{1,0:T(8,128)(2,1)S(1)}, bf16[384,512]{1,0:T(8,128)(2,1)S(1)}, u32[]{:S(2)}, u32[]{:S(2)}) collective-permute-start(bf16[384,512]{1,0:T(8,128)(2,1)S(1)} %pad_maximum_fusion), channel_id=1, source_target_pairs={{0,4},{2,6},{4,0},{6,2},{8,12},{10,14},{12,8},{14,10},{16,20},{18,... | collective-permute-start | bytes 1179656 | tf_op jit(solution)/shard_map/g_w_layer/ppermute | solution.py:277
  6.3 15.6 %collective-permute-start.3 = (bf16[256,512]{1,0:T(8,128)(2,1)S(1)}, bf16[256,512]{1,0:T(8,128)(2,1)}, u32[]{:S(2)}, u32[]{:S(2)}) collective-permute-start(bf16[256,512]{1,0:T(8,128)(2,1)S(1)} %constant_dynamic-slice_fusion.refs_1_), channel_id=1, source_target_pairs={{0,16},{2,18},{4,20},{6,22},{8,24},{10,26},{12,28},{14,30},{16,0},... | collective-permute-start | bytes 786440 | tf_op jit(solution)/shard_map/w_layers/ppermute | solution.py:277
  8.9 13.0 %collective-permute-start.2 = (bf16[256,512]{1,0:T(8,128)(2,1)S(1)}, bf16[256,512]{1,0:T(8,128)(2,1)S(1)}, u32[]{:S(2)}, u32[]{:S(2)}) collective-permute-start(bf16[256,512]{1,0:T(8,128)(2,1)S(1)} %constant_dynamic-slice_fusion.refs_1_), channel_id=1, source_target_pairs={{0,8},{2,10},{4,12},{6,14},{8,0},{10,2},{12,4},{14,6},{16,24},{18,... | collective-permute-start | bytes 786440 | tf_op jit(solution)/shard_map/w_layers/ppermute | solution.py:277
  11.8 9.8 %all-to-all-start = ((s32[16,1,128]{2,1,0:T(1,128)}), s32[16,1,128]{2,1,0:T(1,128)S(1)}, u32[]{:S(2)}, u32[]{:S(2)}) async-start(s32[16,1,128]{2,1,0:T(1,128)} %broadcast_in_dim.24), calls=%async_computation | async-start | bytes 16384 | tf_op jit(solution)/shard_map/ids/all_to_all | solution.py:307
  15.2 6.7 %collective-permute-start.1 = (bf16[8,32,64]{2,1,0:T(8,128)(2,1)S(1)}, bf16[8,32,64]{2,1,0:T(8,128)(2,1)S(1)}, u32[]{:S(2)}, u32[]{:S(2)}) collective-permute-start(bf16[8,32,64]{2,1,0:T(8,128)(2,1)S(1)} %copy-done.9), channel_id=1, source_target_pairs={{0,1},{1,0},{2,3},{3,2},{4,5},{5,4},{6,7},{7,6},{8,9},{9,8},{10,11... | collective-permute-start | bytes 98312 | tf_op jit(solution)/shard_map/up_dp/ppermute | solution.py:277
  21.9 5.2 %copy-start.10 = (bf16[256,512]{1,0:T(8,128)(2,1)}, bf16[256,512]{1,0:T(8,128)(2,1)S(1)}, u32[]{:S(2)}) copy-start(bf16[256,512]{1,0:T(8,128)(2,1)S(1)} %collective-permute-done.2.refs_2_) | copy-start | bytes 786436
  22.0 10.7 %collective-permute-start.11 = (bf16[256,512]{1,0:T(8,128)(2,1)S(1)}, bf16[256,512]{1,0:T(8,128)(2,1)S(1)}, u32[]{:S(2)}, u32[]{:S(2)}) collective-permute-start(bf16[256,512]{1,0:T(8,128)(2,1)S(1)} %pad_maximum_fusion.1), channel_id=1, source_target_pairs={{0,1},{1,0},{2,3},{3,2},{4,5},{5,4},{6,7},{7,6},{8,9},{9,8},{10,11... | collective-permute-start | bytes 786440 | tf_op jit(solution)/shard_map/g_dp/ppermute | solution.py:277
  23.2 9.7 %collective-permute-start.5 = (bf16[256,512]{1,0:T(8,128)(2,1)}, bf16[256,512]{1,0:T(8,128)(2,1)}, u32[]{:S(2)}, u32[]{:S(2)}) collective-permute-start(bf16[256,512]{1,0:T(8,128)(2,1)} %collective-permute-done.3.refs_3_), channel_id=1, source_target_pairs={{0,8},{2,10},{4,12},{6,14},{8,0},{10,2},{12,4},{14,6},{16,24},{18,... | collective-permute-start | bytes 786440 | tf_op jit(solution)/shard_map/w_last/ppermute | solution.py:277
  27.2 29.2 %all-to-all-start.1 = ((bf16[16,272,128]{2,1,0:T(8,128)(2,1)}), bf16[16,272,128]{2,1,0:T(8,128)(2,1)S(1)}, u32[]{:S(2)}, u32[]{:S(2)}) async-start(bf16[16,272,128]{2,1,0:T(8,128)(2,1)} %select.3), calls=%async_computation.1 | async-start | bytes 2228224 | tf_op jit(solution)/shard_map/adapters_to_blocks/all_to_all | solution.py:346
  31.8 3.1 %collective-permute-start.10 = (bf16[384,512]{1,0:T(8,128)(2,1)S(1)}, bf16[384,512]{1,0:T(8,128)(2,1)S(1)}, u32[]{:S(2)}, u32[]{:S(2)}) collective-permute-start(bf16[384,512]{1,0:T(8,128)(2,1)S(1)} %collective-permute-done.4.refs_0_), channel_id=1, source_target_pairs={{0,2},{2,0},{4,6},{6,4},{8,10},{10,8},{12,14},{14,12},{16,18},{18,... | collective-permute-start | bytes 1179656 | tf_op jit(solution)/shard_map/w_core/ppermute | solution.py:277
  32.2 2.1 %collective-permute-start.6 = (bf16[256,512]{1,0:T(8,128)(2,1)S(1)}, bf16[256,512]{1,0:T(8,128)(2,1)S(1)}, u32[]{:S(2)}, u32[]{:S(2)}) collective-permute-start(bf16[256,512]{1,0:T(8,128)(2,1)S(1)} %constant_dynamic-slice_fusion.refs_1_), channel_id=1, source_target_pairs={{0,2},{2,0},{4,6},{6,4},{8,10},{10,8},{12,14},{14,12},{16,18},{18,... | collective-permute-start | bytes 786440 | tf_op jit(solution)/shard_map/w_core/ppermute | solution.py:277
  32.4 2.2 %collective-permute-start.7 = (bf16[256,512]{1,0:T(8,128)(2,1)}, bf16[256,512]{1,0:T(8,128)(2,1)S(1)}, u32[]{:S(2)}, u32[]{:S(2)}) collective-permute-start(bf16[256,512]{1,0:T(8,128)(2,1)} %copy-done.10), channel_id=1, source_target_pairs={{0,2},{2,0},{4,6},{6,4},{8,10},{10,8},{12,14},{14,12},{16,18},{18,... | collective-permute-start | bytes 786440 | tf_op jit(solution)/shard_map/w_core/ppermute | solution.py:277
  32.7 2.2 %collective-permute-start.8 = (bf16[256,512]{1,0:T(8,128)(2,1)}, bf16[256,512]{1,0:T(8,128)(2,1)S(1)}, u32[]{:S(2)}, u32[]{:S(2)}) collective-permute-start(bf16[256,512]{1,0:T(8,128)(2,1)} %collective-permute-done.3.refs_3_), channel_id=1, source_target_pairs={{0,2},{2,0},{4,6},{6,4},{8,10},{10,8},{12,14},{14,12},{16,18},{18,... | collective-permute-start | bytes 786440 | tf_op jit(solution)/shard_map/w_core/ppermute | solution.py:277
  32.9 2.4 %collective-permute-start.9 = (bf16[256,512]{1,0:T(8,128)(2,1)}, bf16[256,512]{1,0:T(8,128)(2,1)S(1)}, u32[]{:S(2)}, u32[]{:S(2)}) collective-permute-start(bf16[256,512]{1,0:T(8,128)(2,1)} %collective-permute-done.5.refs_4_), channel_id=1, source_target_pairs={{0,2},{2,0},{4,6},{6,4},{8,10},{10,8},{12,14},{14,12},{16,18},{18,... | collective-permute-start | bytes 786440 | tf_op jit(solution)/shard_map/w_core/ppermute | solution.py:277
  39.3 16.8 %copy-start.7 = (bf16[128,1536]{1,0:T(8,128)(2,1)}, bf16[128,1536]{1,0:T(8,128)(2,1)S(1)}, u32[]{:S(2)}) copy-start(bf16[128,1536]{1,0:T(8,128)(2,1)S(1)} %get-tuple-element.57) | copy-start | bytes 1179652
  39.3 17.0 %collective-permute-start.13 = (bf16[128,2560]{1,0:T(8,128)(2,1)S(1)}, bf16[128,2560]{1,0:T(8,128)(2,1)S(1)}, u32[]{:S(2)}, u32[]{:S(2)}) collective-permute-start(bf16[128,2560]{1,0:T(8,128)(2,1)S(1)} %get-tuple-element.48), channel_id=1, source_target_pairs={{0,1},{1,0},{2,3},{3,2},{4,5},{5,4},{6,7},{7,6},{8,9},{9,8},{10,11... | collective-permute-start | bytes 1966088 | tf_op jit(solution)/shard_map/pieces01/ppermute | solution.py:277
  40.2 16.0 %collective-permute-start.12 = (bf16[128,1536]{1,0:T(8,128)(2,1)S(1)}, bf16[128,1536]{1,0:T(8,128)(2,1)S(1)}, u32[]{:S(2)}, u32[]{:S(2)}) collective-permute-start(bf16[128,1536]{1,0:T(8,128)(2,1)S(1)} %get-tuple-element.47), channel_id=1, source_target_pairs={{0,4},{1,5},{2,6},{3,7},{4,0},{5,1},{6,2},{7,3},{8,12},{9,13},{10,... | collective-permute-start | bytes 1179656 | tf_op jit(solution)/shard_map/pieces20/ppermute | solution.py:277
  56.2 4.1 %copy-start.5 = (bf16[128,1536]{1,0:T(8,128)(2,1)}, bf16[128,1536]{1,0:T(8,128)(2,1)S(1)}, u32[]{:S(2)}) copy-start(bf16[128,1536]{1,0:T(8,128)(2,1)S(1)} %collective-permute-done.12.refs_1_) | copy-start | bytes 1179652
  56.4 3.9 %copy-start.3 = (bf16[128,2560]{1,0:T(8,128)(2,1)}, bf16[128,2560]{1,0:T(8,128)(2,1)S(1)}, u32[]{:S(2)}) copy-start(bf16[128,2560]{1,0:T(8,128)(2,1)S(1)} %collective-permute-done.13.refs_2_) | copy-start | bytes 1966084
  56.4 1.8 %copy-start.1 = (bf16[128,8192]{1,0:T(8,128)(2,1)S(1)}, bf16[128,8192]{1,0:T(8,128)(2,1)}, u32[]{:S(2)}) copy-start(bf16[128,8192]{1,0:T(8,128)(2,1)} %x.1) | copy-start | bytes 6291460
  60.3 34.7 %all-to-all-start.2 = ((bf16[32,144,128]{2,1,0:T(8,128)(2,1)}), bf16[32,144,128]{2,1,0:T(8,128)(2,1)S(1)}, u32[]{:S(2)}, u32[]{:S(2)}) async-start(bf16[32,144,128]{2,1,0:T(8,128)(2,1)} %get-tuple-element.50), calls=%async_computation.2 | async-start | bytes 2359296 | tf_op jit(solution)/shard_map/gradients_back/all_to_all | solution.py:400
  65.9 29.1 %collective-permute-start.15 = (bf16[128,1536]{1,0:T(8,128)(2,1)}, bf16[128,1536]{1,0:T(8,128)(2,1)}, u32[]{:S(2)}, u32[]{:S(2)}) collective-permute-start(bf16[128,1536]{1,0:T(8,128)(2,1)} %copy-done.7), channel_id=1, source_target_pairs={{0,5},{1,4},{2,7},{3,6},{4,1},{5,0},{6,3},{7,2},{8,13},{9,12},{10,... | collective-permute-start | bytes 1179656 | tf_op jit(solution)/shard_map/pieces21/ppermute | solution.py:277
  68.6 20.8 %collective-permute-start.14 = (s32[16]{0:T(128)S(1)}, s32[16]{0:T(128)S(1)}, u32[]{:S(2)}, u32[]{:S(2)}) collective-permute-start(s32[16]{0:T(128)S(1)} %select_reduce_fusion.slots.refs_0_), channel_id=1, source_target_pairs={{0,1},{1,0},{2,3},{3,2},{4,5},{5,4},{6,7},{7,6},{8,9},{9,8},{10,11... | collective-permute-start | bytes 200 | tf_op jit(solution)/shard_map/slots_dp/ppermute | solution.py:277
  94.9 3.0 %copy-start.4 = (bf16[128,2560]{1,0:T(8,128)(2,1)S(1)}, bf16[128,2560]{1,0:T(8,128)(2,1)}, u32[]{:S(2)}) copy-start(bf16[128,2560]{1,0:T(8,128)(2,1)} %copy-done.3) | copy-start | bytes 1966084
  94.9 3.0 %copy-start.6 = (bf16[128,1536]{1,0:T(8,128)(2,1)S(1)}, bf16[128,1536]{1,0:T(8,128)(2,1)}, u32[]{:S(2)}) copy-start(bf16[128,1536]{1,0:T(8,128)(2,1)} %copy-done.5) | copy-start | bytes 1179652
  96.4 8.0 %collective-permute-start.16 = (bf16[8,64,256]{2,1,0:T(8,128)(2,1)S(1)}, bf16[8,64,256]{2,1,0:T(8,128)(2,1)S(1)}, u32[]{:S(2)}, u32[]{:S(2)}) collective-permute-start(bf16[8,64,256]{2,1,0:T(8,128)(2,1)S(1)} %get-tuple-element.59), channel_id=1, source_target_pairs={{0,1},{1,0},{2,3},{3,2},{4,5},{5,4},{6,7},{7,6},{8,9},{9,8},{10,11... | collective-permute-start | bytes 786440 | tf_op jit(solution)/shard_map/grads_dp/ppermute | solution.py:277

commit v8 on v7

--- a/solution.py
+++ b/solution.py
@@ -101,7 +101,7 @@
     up = jnp.concatenate(
         [unpack_up(got[f, cut:, :], kv_rows, rank) for f in range(fsdp_count)], axis=0
     )
-    hidden = dot(g[...], up, NN).astype(BF16)
+    hidden = dot(g[...], up, NN).astype(BF16) * adapter_scale_factor
     hidden_out[...] = hidden
     inner = jnp.zeros((x.shape[0], rank), F32)
     stores = []
@@ -109,7 +109,7 @@
     for f in range(fsdp_count):
         x_part = x[:, f * rows : (f + 1) * rows]
         inner += dot(x_part, wide(got, f, 0, tiles, rank), NT)
-        down = (adapter_scale_factor * dot(hidden, x_part, TN)).astype(BF16)
+        down = dot(hidden, x_part, TN).astype(BF16)
         for c in range(tiles):
             half, at = c * halves // tiles, c % (tiles // halves) * rank
             out[f * halves + half, at : at + rank, :] = down[:, c * lanes : (c + 1) * lanes]
@@ -121,7 +121,7 @@
                 )
             )
             stores[-1].start()
-    part_up = (adapter_scale_factor * dot(g[...], inner.astype(BF16), TN)).astype(BF16)
+    part_up = dot(g[...], inner.astype(BF16) * adapter_scale_factor, TN).astype(BF16)
     for f in range(fsdp_count):
         packed = pack_up(part_up[f * kv_rows : (f + 1) * kv_rows])
         for half in range(halves):
@@ -177,7 +177,7 @@
         d = d_here ^ d_rel
         for k, f_rel in enumerate(every if i_rel == 0 else far):
             f = f_here ^ (f_rel ^ i_rel)
-            low = adapter_scale_factor * dot(h, wide(got, f, d * tiles, tiles, rank), NN)
+            low = dot(h, wide(got, f, d * tiles, tiles, rank), NN)
             start = pl.multiple_of(f * rows + d * cols, lanes)
             out[:, pl.ds(start, cols)] = (
                 piece[:, k * cols : (k + 1) * cols].astype(F32) + low

time: 106 us -> 106 us (level)
  no operation moved by 1% of the time
where the time goes in v8:
time: 106 us; the launch traced here: 105 us
  waiting for transfers between devices  50.8 us (48%)
  starting transfers between devices  34.4 us (32%)
  Pallas kernels  14.4 us (14%)
  local copies, waits for them, and re-layouts  2.9 us (3%)
  between operations  1.51 us (1%)
  other arithmetic  1.23 us (1%)
    ppermute x17, waiting for transfers between devices, exchange(): return lax.ppermute(array, axis, xor_pairs(axis_count(axis), bits))  40 us
    ppermute x17, starting transfers between devices, exchange(): return lax.ppermute(array, axis, xor_pairs(axis_count(axis), bits))  20.7 us
    all_to_all x1, starting transfers between devices, on_device(): returned = lax.all_to_all(back, axes, 0, 0, tiled=True)  5.61 us
    all_to_all x1, waiting for transfers between devices, on_device(): returned = lax.all_to_all(back, axes, 0, 0, tiled=True)  5.52 us
    all_to_all x1, waiting for transfers between devices, on_device(): lax.all_to_all(jnp.broadcast_to(tenant_ids[:, None, None], (fsdp_count, 1...  5.26 us
    all_to_all x1, starting transfers between devices, on_device(): got = lax.all_to_all(sent, 'fsdp', 0, 0, tiled=True)  4.61 us
    pallas_call x1, Pallas kernels, on_device(): pl.pallas_call(functools.partial(base_kernel, rels, len(near), layers), o...  4.01 us
    all_to_all x1, starting transfers between devices, on_device(): lax.all_to_all(jnp.broadcast_to(tenant_ids[:, None, None], (fsdp_count, 1...  3.47 us
  transfers between devices with their start and end apart: 20, of which 10 were waited for; matrix products, arithmetic and copies ran while one was open for 2% of the time, Pallas kernels for 10%

profile of v8, /device:TPU:0, one launch (start us, length us, event | category | flops | bytes accessed | tf_op | source)
XLA Modules:
  0.0 105.2 jit_solution(2802112368456987825)
XLA Ops:
  0.6 0.0 copy-start
  0.6 0.0 copy-start.2
  0.7 0.0 copy-start.9
  0.7 3.0 %collective-permute-start = (bf16[8,64,512]{2,1,0:T(8,128)(2,1)}, bf16[8,64,512]{2,1,0:T(8,128)(2,1)S(1)}, u32[]{:S(2)}, u32[]{:S(2)}) collective-permute-start(bf16[8,64,512]{2,1,0:T(8,128)(2,1)} %bitcast.4), channel_id=1, source_target_pairs={{0,1},{1,0},{2,3},{3,2},{4,5},{5,4},{6,7},{7,6},{8,9},{9,8},{10,11... | collective-permute-start | bytes 1572872 | tf_op jit(solution)/shard_map/down_dp/ppermute | solution.py:277
  3.7 0.0 copy-start.8
  3.7 1.0 pad_maximum_fusion
  4.8 1.6 %collective-permute-start.4 = (bf16[384,512]{1,0:T(8,128)(2,1)S(1)}, bf16[384,512]{1,0:T(8,128)(2,1)S(1)}, u32[]{:S(2)}, u32[]{:S(2)}) collective-permute-start(bf16[384,512]{1,0:T(8,128)(2,1)S(1)} %pad_maximum_fusion), channel_id=1, source_target_pairs={{0,4},{2,6},{4,0},{6,2},{8,12},{10,14},{12,8},{14,10},{16,20},{18,... | collective-permute-start | bytes 1179656 | tf_op jit(solution)/shard_map/g_w_layer/ppermute | solution.py:277
  6.3 2.6 %collective-permute-start.3 = (bf16[256,512]{1,0:T(8,128)(2,1)S(1)}, bf16[256,512]{1,0:T(8,128)(2,1)}, u32[]{:S(2)}, u32[]{:S(2)}) collective-permute-start(bf16[256,512]{1,0:T(8,128)(2,1)S(1)} %constant_dynamic-slice_fusion.refs_1_), channel_id=1, source_target_pairs={{0,16},{2,18},{4,20},{6,22},{8,24},{10,26},{12,28},{14,30},{16,0},... | collective-permute-start | bytes 786440 | tf_op jit(solution)/shard_map/w_layers/ppermute | solution.py:277
  8.9 1.6 %collective-permute-start.2 = (bf16[256,512]{1,0:T(8,128)(2,1)S(1)}, bf16[256,512]{1,0:T(8,128)(2,1)S(1)}, u32[]{:S(2)}, u32[]{:S(2)}) collective-permute-start(bf16[256,512]{1,0:T(8,128)(2,1)S(1)} %constant_dynamic-slice_fusion.refs_1_), channel_id=1, source_target_pairs={{0,8},{2,10},{4,12},{6,14},{8,0},{10,2},{12,4},{14,6},{16,24},{18,... | collective-permute-start | bytes 786440 | tf_op jit(solution)/shard_map/w_layers/ppermute | solution.py:277
  11.2 0.6 broadcast_in_dim.24
  11.8 3.5 %all-to-all-start = ((s32[16,1,128]{2,1,0:T(1,128)}), s32[16,1,128]{2,1,0:T(1,128)S(1)}, u32[]{:S(2)}, u32[]{:S(2)}) async-start(s32[16,1,128]{2,1,0:T(1,128)} %broadcast_in_dim.24), calls=%async_computation | async-start | bytes 16384 | tf_op jit(solution)/shard_map/ids/all_to_all | solution.py:307
  15.2 1.0 collective-permute-start.1
  16.3 5.3 %all-to-all-done = s32[16,1,128]{2,1,0:T(1,128)S(1)} async-done(((s32[16,1,128]{2,1,0:T(1,128)}), s32[16,1,128]{2,1,0:T(1,128)S(1)}, u32[]{:S(2)}, u32[]{:S(2)}) %all-to-all-start) | async-done | bytes 8224 | tf_op jit(solution)/shard_map/ids/all_to_all | solution.py:307
  21.5 0.4 slice_reduce_fusion
  21.9 0.0 collective-permute-done.1.refs_3_
  21.9 0.0 collective-permute-done.3.refs_3_
  22.0 0.0 collective-permute-done.refs_1_
  22.0 1.2 %collective-permute-start.11 = (bf16[256,512]{1,0:T(8,128)(2,1)S(1)}, bf16[256,512]{1,0:T(8,128)(2,1)S(1)}, u32[]{:S(2)}, u32[]{:S(2)}) collective-permute-start(bf16[256,512]{1,0:T(8,128)(2,1)S(1)} %pad_maximum_fusion.1), channel_id=1, source_target_pairs={{0,1},{1,0},{2,3},{3,2},{4,5},{5,4},{6,7},{7,6},{8,9},{9,8},{10,11... | collective-permute-start | bytes 786440 | tf_op jit(solution)/shard_map/g_dp/ppermute | solution.py:277
  23.2 0.8 collective-permute-start.5
  24.0 0.2 select_reduce_fusion.slots.refs_0_
  24.2 3.0 %select.3 = bf16[16,272,128]{2,1,0:T(8,128)(2,1)} custom-call(s32[16]{0:T(128)S(1)} %select_reduce_fusion.slots.refs_0_, bf16[8,64,512]{2,1,0:T(8,128)(2,1)} %bitcast.5, bf16[8,64,512]{2,1,0:T(8,128)(2,1)S(1)} %collective-permute-done.refs_1_, bf16[8,32,64]{2,1,0:T(8,128)(2,1)} %refs_2_, bf16[8,32,64]{2,1,0:T(8,128)(2,1)S(1)} %collective-permute-done.1.refs_3_), custom_call_target="tpu_custom_call" | custom-call | bytes 2228224 | tf_op jit(solution)/shard_map/select/pallas_call | solution.py:333
  27.2 4.6 %all-to-all-start.1 = ((bf16[16,272,128]{2,1,0:T(8,128)(2,1)}), bf16[16,272,128]{2,1,0:T(8,128)(2,1)S(1)}, u32[]{:S(2)}, u32[]{:S(2)}) async-start(bf16[16,272,128]{2,1,0:T(8,128)(2,1)} %select.3), calls=%async_computation.1 | async-start | bytes 2228224 | tf_op jit(solution)/shard_map/adapters_to_blocks/all_to_all | solution.py:346
  31.8 0.4 collective-permute-start.10
  32.2 0.2 collective-permute-start.6
  32.4 0.3 collective-permute-start.7
  32.7 0.2 collective-permute-start.8
  32.9 0.3 collective-permute-start.9
  33.2 1.1 %collective-permute-done.6.refs_5_ = bf16[256,512]{1,0:T(8,128)(2,1)S(1)} collective-permute-done((bf16[256,512]{1,0:T(8,128)(2,1)S(1)}, bf16[256,512]{1,0:T(8,128)(2,1)S(1)}, u32[]{:S(2)}, u32[]{:S(2)}) %collective-permute-start.6) | collective-permute-done | bytes 262176 | tf_op jit(solution)/shard_map/w_core/ppermute | solution.py:277
  34.3 0.2 collective-permute-done.7.refs_6_
  34.6 0.4 collective-permute-done.8.refs_7_
  34.9 0.4 collective-permute-done.9.refs_8_
  35.3 4.0 %base.1 = (bf16[128,2560]{1,0:T(8,128)(2,1)S(1)}, bf16[128,1536]{1,0:T(8,128)(2,1)S(1)}, bf16[128,2560]{1,0:T(8,128)(2,1)S(1)}, bf16[128,1536]{1,0:T(8,128)(2,1)S(1)}) custom-call(bf16[128,512]{1,0:T(8,128)(2,1)S(1)} %copy-done.2, bf16[384,512]{1,0:T(8,128)(2,1)S(1)} %collective-permute-done.4.refs_0_, bf16[256,512]{1,0:T(8,128)(2,1)} %copy-done.8, ...), custom_call_target="tpu_custom_call" | custom-call | flops 10737418240 | bytes 41943040 | tf_op jit(solution)/shard_map/base/pallas_call | solution.py:356
  39.3 0.8 collective-permute-start.13
  40.2 1.9 %collective-permute-start.12 = (bf16[128,1536]{1,0:T(8,128)(2,1)S(1)}, bf16[128,1536]{1,0:T(8,128)(2,1)S(1)}, u32[]{:S(2)}, u32[]{:S(2)}) collective-permute-start(bf16[128,1536]{1,0:T(8,128)(2,1)S(1)} %get-tuple-element.47), channel_id=1, source_target_pairs={{0,4},{1,5},{2,6},{3,7},{4,0},{5,1},{6,2},{7,3},{8,12},{9,13},{10,... | collective-permute-start | bytes 1179656 | tf_op jit(solution)/shard_map/pieces20/ppermute | solution.py:277
  42.0 14.1 %collective-permute-done.12.refs_1_ = bf16[128,1536]{1,0:T(8,128)(2,1)S(1)} collective-permute-done((bf16[128,1536]{1,0:T(8,128)(2,1)S(1)}, bf16[128,1536]{1,0:T(8,128)(2,1)S(1)}, u32[]{:S(2)}, u32[]{:S(2)}) %collective-permute-start.12) | collective-permute-done | bytes 393248 | tf_op jit(solution)/shard_map/pieces20/ppermute | solution.py:277
  56.2 0.2 collective-permute-done.13.refs_2_
  56.4 1.8 %copy-done.1 = bf16[128,8192]{1,0:T(8,128)(2,1)S(1)} copy-done((bf16[128,8192]{1,0:T(8,128)(2,1)S(1)}, bf16[128,8192]{1,0:T(8,128)(2,1)}, u32[]{:S(2)}) %copy-start.1) | copy-done | bytes 2097176
  58.2 2.0 %middle.1 = (bf16[128,64]{1,0:T(8,128)(2,1)S(1)}, bf16[32,144,128]{2,1,0:T(8,128)(2,1)}) custom-call(bf16[128,8192]{1,0:T(8,128)(2,1)S(1)} %copy-done.1, bf16[128,512]{1,0:T(8,128)(2,1)S(1)} %copy-done.2, bf16[16,272,128]{2,1,0:T(8,128)(2,1)S(1)} %all-to-all-done.1.got), custom_call_target="tpu_custom_call" | custom-call | flops 268435456 | bytes 4325376 | tf_op jit(solution)/shard_map/middle/pallas_call | solution.py:381
  60.3 5.6 %all-to-all-start.2 = ((bf16[32,144,128]{2,1,0:T(8,128)(2,1)}), bf16[32,144,128]{2,1,0:T(8,128)(2,1)S(1)}, u32[]{:S(2)}, u32[]{:S(2)}) async-start(bf16[32,144,128]{2,1,0:T(8,128)(2,1)} %get-tuple-element.50), calls=%async_computation.2 | async-start | bytes 2359296 | tf_op jit(solution)/shard_map/gradients_back/all_to_all | solution.py:400
  65.9 2.7 %collective-permute-start.15 = (bf16[128,1536]{1,0:T(8,128)(2,1)}, bf16[128,1536]{1,0:T(8,128)(2,1)}, u32[]{:S(2)}, u32[]{:S(2)}) collective-permute-start(bf16[128,1536]{1,0:T(8,128)(2,1)} %copy-done.7), channel_id=1, source_target_pairs={{0,5},{1,4},{2,7},{3,6},{4,1},{5,0},{6,3},{7,2},{8,13},{9,12},{10,... | collective-permute-start | bytes 1179656 | tf_op jit(solution)/shard_map/pieces21/ppermute | solution.py:277
  68.6 0.6 collective-permute-start.14
  69.2 20.2 %collective-permute-done.14.refs_1_ = s32[16]{0:T(128)S(1)} collective-permute-done((s32[16]{0:T(128)S(1)}, s32[16]{0:T(128)S(1)}, u32[]{:S(2)}, u32[]{:S(2)}) %collective-permute-start.14) | collective-permute-done | bytes 96 | tf_op jit(solution)/shard_map/slots_dp/ppermute | solution.py:277
  89.4 5.5 %all-to-all-done.2.refs_2_ = bf16[32,144,128]{2,1,0:T(8,128)(2,1)S(1)} async-done(((bf16[32,144,128]{2,1,0:T(8,128)(2,1)}), bf16[32,144,128]{2,1,0:T(8,128)(2,1)S(1)}, u32[]{:S(2)}, u32[]{:S(2)}) %all-to-all-start.2) | async-done | bytes 1179680 | tf_op jit(solution)/shard_map/gradients_back/all_to_all | solution.py:400
  94.9 1.5 %sum_all.1 = (bf16[8,64,256]{2,1,0:T(8,128)(2,1)S(1)}, bf16[8,64,256]{2,1,0:T(8,128)(2,1)S(1)}, bf16[8,32,64]{2,1,0:T(8,128)(2,1)}) custom-call(s32[16]{0:T(128)S(1)} %select_reduce_fusion.slots.refs_0_, s32[16]{0:T(128)S(1)} %collective-permute-done.14.refs_1_, bf16[32,144,128]{2,1,0:T(8,128)(2,1)S(1)} %all-to-all-done.2.refs_2_), custom_call_target="tpu_custom_call" | custom-call | bytes 2228224 | tf_op jit(solution)/shard_map/sum_all/pallas_call | solution.py:420
  96.4 1.5 %collective-permute-start.16 = (bf16[8,64,256]{2,1,0:T(8,128)(2,1)S(1)}, bf16[8,64,256]{2,1,0:T(8,128)(2,1)S(1)}, u32[]{:S(2)}, u32[]{:S(2)}) collective-permute-start(bf16[8,64,256]{2,1,0:T(8,128)(2,1)S(1)} %get-tuple-element.59), channel_id=1, source_target_pairs={{0,1},{1,0},{2,3},{3,2},{4,5},{5,4},{6,7},{7,6},{8,9},{9,8},{10,11... | collective-permute-start | bytes 786440 | tf_op jit(solution)/shard_map/grads_dp/ppermute | solution.py:277
  97.9 3.1 %rows.1 = bf16[128,8192]{1,0:T(8,128)(2,1)} custom-call(bf16[128,64]{1,0:T(8,128)(2,1)S(1)} %get-tuple-element.60.hidden, bf16[16,272,128]{2,1,0:T(8,128)(2,1)S(1)} %all-to-all-done.1.got, bf16[128,2560]{1,0:T(8,128)(2,1)S(1)} %get-tuple-element.61.refs_0_, bf16[128,1536]{1,0:T(8,128)(2,1)S(1)} %copy-done.6, bf16[128,2560]{1,0:T(8,128)(2,1)S(1)} %copy-done.4, ...), custom_call_target="tpu_custom_call" | custom-call | flops 134217728 | bytes 5308416 | tf_op jit(solution)/shard_map/rows/pallas_call | solution.py:406
  101.0 3.4 %collective-permute-done.16.refs_1_ = bf16[8,64,256]{2,1,0:T(8,128)(2,1)S(1)} collective-permute-done((bf16[8,64,256]{2,1,0:T(8,128)(2,1)S(1)}, bf16[8,64,256]{2,1,0:T(8,128)(2,1)S(1)}, u32[]{:S(2)}, u32[]{:S(2)}) %collective-permute-start.16) | collective-permute-done | bytes 262176 | tf_op jit(solution)/shard_map/grads_dp/ppermute | solution.py:277
  104.4 0.8 join.1
  (29 shorter events, 0.1 us)
Async XLA Ops:
  0.6 3.1 %copy-start = (bf16[512,512]{1,0:T(8,128)(2,1)S(1)}, bf16[512,512]{1,0:T(8,128)(2,1)}, u32[]{:S(2)}) copy-start(bf16[512,512]{1,0:T(8,128)(2,1)} %param.9) | copy-start | bytes 1572868
  0.6 21.3 %copy-start.2 = (bf16[128,512]{1,0:T(8,128)(2,1)S(1)}, bf16[128,512]{1,0:T(8,128)(2,1)}, u32[]{:S(2)}) copy-start(bf16[128,512]{1,0:T(8,128)(2,1)} %g.1) | copy-start | bytes 393220
  0.7 14.6 %copy-start.9 = (bf16[8,32,64]{2,1,0:T(8,128)(2,1)S(1)}, bf16[8,32,64]{2,1,0:T(8,128)(2,1)}, u32[]{:S(2)}) copy-start(bf16[8,32,64]{2,1,0:T(8,128)(2,1)} %refs_2_) | copy-start | bytes 98308
  0.7 23.3 %copy-start.11 = (s32[16]{0:T(128)S(1)}, s32[16]{0:T(128)}, u32[]{:S(2)}) copy-start(s32[16]{0:T(128)} %param.13) | copy-start | bytes 196
  0.7 21.3 %collective-permute-start = (bf16[8,64,512]{2,1,0:T(8,128)(2,1)}, bf16[8,64,512]{2,1,0:T(8,128)(2,1)S(1)}, u32[]{:S(2)}, u32[]{:S(2)}) collective-permute-start(bf16[8,64,512]{2,1,0:T(8,128)(2,1)} %bitcast.4), channel_id=1, source_target_pairs={{0,1},{1,0},{2,3},{3,2},{4,5},{5,4},{6,7},{7,6},{8,9},{9,8},{10,11... | collective-permute-start | bytes 1572872 | tf_op jit(solution)/shard_map/down_dp/ppermute | solution.py:277
  3.7 28.5 %copy-start.8 = (bf16[256,512]{1,0:T(8,128)(2,1)}, bf16[256,512]{1,0:T(8,128)(2,1)S(1)}, u32[]{:S(2)}) copy-start(bf16[256,512]{1,0:T(8,128)(2,1)S(1)} %constant_dynamic-slice_fusion.refs_1_) | copy-start | bytes 786436
  4.8 17.2 %collective-permute-start.4 = (bf16[384,512]{1,0:T(8,128)(2,1)S(1)}, bf16[384,512]{1,0:T(8,128)(2,1)S(1)}, u32[]{:S(2)}, u32[]{:S(2)}) collective-permute-start(bf16[384,512]{1,0:T(8,128)(2,1)S(1)} %pad_maximum_fusion), channel_id=1, source_target_pairs={{0,4},{2,6},{4,0},{6,2},{8,12},{10,14},{12,8},{14,10},{16,20},{18,... | collective-permute-start | bytes 1179656 | tf_op jit(solution)/shard_map/g_w_layer/ppermute | solution.py:277
  6.3 15.6 %collective-permute-start.3 = (bf16[256,512]{1,0:T(8,128)(2,1)S(1)}, bf16[256,512]{1,0:T(8,128)(2,1)}, u32[]{:S(2)}, u32[]{:S(2)}) collective-permute-start(bf16[256,512]{1,0:T(8,128)(2,1)S(1)} %constant_dynamic-slice_fusion.refs_1_), channel_id=1, source_target_pairs={{0,16},{2,18},{4,20},{6,22},{8,24},{10,26},{12,28},{14,30},{16,0},... | collective-permute-start | bytes 786440 | tf_op jit(solution)/shard_map/w_layers/ppermute | solution.py:277
  8.9 13.0 %collective-permute-start.2 = (bf16[256,512]{1,0:T(8,128)(2,1)S(1)}, bf16[256,512]{1,0:T(8,128)(2,1)S(1)}, u32[]{:S(2)}, u32[]{:S(2)}) collective-permute-start(bf16[256,512]{1,0:T(8,128)(2,1)S(1)} %constant_dynamic-slice_fusion.refs_1_), channel_id=1, source_target_pairs={{0,8},{2,10},{4,12},{6,14},{8,0},{10,2},{12,4},{14,6},{16,24},{18,... | collective-permute-start | bytes 786440 | tf_op jit(solution)/shard_map/w_layers/ppermute | solution.py:277
  11.8 9.8 %all-to-all-start = ((s32[16,1,128]{2,1,0:T(1,128)}), s32[16,1,128]{2,1,0:T(1,128)S(1)}, u32[]{:S(2)}, u32[]{:S(2)}) async-start(s32[16,1,128]{2,1,0:T(1,128)} %broadcast_in_dim.24), calls=%async_computation | async-start | bytes 16384 | tf_op jit(solution)/shard_map/ids/all_to_all | solution.py:307
  15.2 6.7 %collective-permute-start.1 = (bf16[8,32,64]{2,1,0:T(8,128)(2,1)S(1)}, bf16[8,32,64]{2,1,0:T(8,128)(2,1)S(1)}, u32[]{:S(2)}, u32[]{:S(2)}) collective-permute-start(bf16[8,32,64]{2,1,0:T(8,128)(2,1)S(1)} %copy-done.9), channel_id=1, source_target_pairs={{0,1},{1,0},{2,3},{3,2},{4,5},{5,4},{6,7},{7,6},{8,9},{9,8},{10,11... | collective-permute-start | bytes 98312 | tf_op jit(solution)/shard_map/up_dp/ppermute | solution.py:277
  21.9 5.2 %copy-start.10 = (bf16[256,512]{1,0:T(8,128)(2,1)}, bf16[256,512]{1,0:T(8,128)(2,1)S(1)}, u32[]{:S(2)}) copy-start(bf16[256,512]{1,0:T(8,128)(2,1)S(1)} %collective-permute-done.2.refs_2_) | copy-start | bytes 786436
  22.0 10.7 %collective-permute-start.11 = (bf16[256,512]{1,0:T(8,128)(2,1)S(1)}, bf16[256,512]{1,0:T(8,128)(2,1)S(1)}, u32[]{:S(2)}, u32[]{:S(2)}) collective-permute-start(bf16[256,512]{1,0:T(8,128)(2,1)S(1)} %pad_maximum_fusion.1), channel_id=1, source_target_pairs={{0,1},{1,0},{2,3},{3,2},{4,5},{5,4},{6,7},{7,6},{8,9},{9,8},{10,11... | collective-permute-start | bytes 786440 | tf_op jit(solution)/shard_map/g_dp/ppermute | solution.py:277
  23.2 9.7 %collective-permute-start.5 = (bf16[256,512]{1,0:T(8,128)(2,1)}, bf16[256,512]{1,0:T(8,128)(2,1)}, u32[]{:S(2)}, u32[]{:S(2)}) collective-permute-start(bf16[256,512]{1,0:T(8,128)(2,1)} %collective-permute-done.3.refs_3_), channel_id=1, source_target_pairs={{0,8},{2,10},{4,12},{6,14},{8,0},{10,2},{12,4},{14,6},{16,24},{18,... | collective-permute-start | bytes 786440 | tf_op jit(solution)/shard_map/w_last/ppermute | solution.py:277
  27.2 29.2 %all-to-all-start.1 = ((bf16[16,272,128]{2,1,0:T(8,128)(2,1)}), bf16[16,272,128]{2,1,0:T(8,128)(2,1)S(1)}, u32[]{:S(2)}, u32[]{:S(2)}) async-start(bf16[16,272,128]{2,1,0:T(8,128)(2,1)} %select.3), calls=%async_computation.1 | async-start | bytes 2228224 | tf_op jit(solution)/shard_map/adapters_to_blocks/all_to_all | solution.py:346
  31.8 3.1 %collective-permute-start.10 = (bf16[384,512]{1,0:T(8,128)(2,1)S(1)}, bf16[384,512]{1,0:T(8,128)(2,1)S(1)}, u32[]{:S(2)}, u32[]{:S(2)}) collective-permute-start(bf16[384,512]{1,0:T(8,128)(2,1)S(1)} %collective-permute-done.4.refs_0_), channel_id=1, source_target_pairs={{0,2},{2,0},{4,6},{6,4},{8,10},{10,8},{12,14},{14,12},{16,18},{18,... | collective-permute-start | bytes 1179656 | tf_op jit(solution)/shard_map/w_core/ppermute | solution.py:277
  32.2 2.1 %collective-permute-start.6 = (bf16[256,512]{1,0:T(8,128)(2,1)S(1)}, bf16[256,512]{1,0:T(8,128)(2,1)S(1)}, u32[]{:S(2)}, u32[]{:S(2)}) collective-permute-start(bf16[256,512]{1,0:T(8,128)(2,1)S(1)} %constant_dynamic-slice_fusion.refs_1_), channel_id=1, source_target_pairs={{0,2},{2,0},{4,6},{6,4},{8,10},{10,8},{12,14},{14,12},{16,18},{18,... | collective-permute-start | bytes 786440 | tf_op jit(solution)/shard_map/w_core/ppermute | solution.py:277
  32.4 2.2 %collective-permute-start.7 = (bf16[256,512]{1,0:T(8,128)(2,1)}, bf16[256,512]{1,0:T(8,128)(2,1)S(1)}, u32[]{:S(2)}, u32[]{:S(2)}) collective-permute-start(bf16[256,512]{1,0:T(8,128)(2,1)} %copy-done.10), channel_id=1, source_target_pairs={{0,2},{2,0},{4,6},{6,4},{8,10},{10,8},{12,14},{14,12},{16,18},{18,... | collective-permute-start | bytes 786440 | tf_op jit(solution)/shard_map/w_core/ppermute | solution.py:277
  32.7 2.2 %collective-permute-start.8 = (bf16[256,512]{1,0:T(8,128)(2,1)}, bf16[256,512]{1,0:T(8,128)(2,1)S(1)}, u32[]{:S(2)}, u32[]{:S(2)}) collective-permute-start(bf16[256,512]{1,0:T(8,128)(2,1)} %collective-permute-done.3.refs_3_), channel_id=1, source_target_pairs={{0,2},{2,0},{4,6},{6,4},{8,10},{10,8},{12,14},{14,12},{16,18},{18,... | collective-permute-start | bytes 786440 | tf_op jit(solution)/shard_map/w_core/ppermute | solution.py:277
  32.9 2.4 %collective-permute-start.9 = (bf16[256,512]{1,0:T(8,128)(2,1)}, bf16[256,512]{1,0:T(8,128)(2,1)S(1)}, u32[]{:S(2)}, u32[]{:S(2)}) collective-permute-start(bf16[256,512]{1,0:T(8,128)(2,1)} %collective-permute-done.5.refs_4_), channel_id=1, source_target_pairs={{0,2},{2,0},{4,6},{6,4},{8,10},{10,8},{12,14},{14,12},{16,18},{18,... | collective-permute-start | bytes 786440 | tf_op jit(solution)/shard_map/w_core/ppermute | solution.py:277
  39.3 16.8 %copy-start.7 = (bf16[128,1536]{1,0:T(8,128)(2,1)}, bf16[128,1536]{1,0:T(8,128)(2,1)S(1)}, u32[]{:S(2)}) copy-start(bf16[128,1536]{1,0:T(8,128)(2,1)S(1)} %get-tuple-element.57) | copy-start | bytes 1179652
  39.3 17.0 %collective-permute-start.13 = (bf16[128,2560]{1,0:T(8,128)(2,1)S(1)}, bf16[128,2560]{1,0:T(8,128)(2,1)S(1)}, u32[]{:S(2)}, u32[]{:S(2)}) collective-permute-start(bf16[128,2560]{1,0:T(8,128)(2,1)S(1)} %get-tuple-element.48), channel_id=1, source_target_pairs={{0,1},{1,0},{2,3},{3,2},{4,5},{5,4},{6,7},{7,6},{8,9},{9,8},{10,11... | collective-permute-start | bytes 1966088 | tf_op jit(solution)/shard_map/pieces01/ppermute | solution.py:277
  40.2 16.0 %collective-permute-start.12 = (bf16[128,1536]{1,0:T(8,128)(2,1)S(1)}, bf16[128,1536]{1,0:T(8,128)(2,1)S(1)}, u32[]{:S(2)}, u32[]{:S(2)}) collective-permute-start(bf16[128,1536]{1,0:T(8,128)(2,1)S(1)} %get-tuple-element.47), channel_id=1, source_target_pairs={{0,4},{1,5},{2,6},{3,7},{4,0},{5,1},{6,2},{7,3},{8,12},{9,13},{10,... | collective-permute-start | bytes 1179656 | tf_op jit(solution)/shard_map/pieces20/ppermute | solution.py:277
  56.2 4.1 %copy-start.5 = (bf16[128,1536]{1,0:T(8,128)(2,1)}, bf16[128,1536]{1,0:T(8,128)(2,1)S(1)}, u32[]{:S(2)}) copy-start(bf16[128,1536]{1,0:T(8,128)(2,1)S(1)} %collective-permute-done.12.refs_1_) | copy-start | bytes 1179652
  56.4 3.9 %copy-start.3 = (bf16[128,2560]{1,0:T(8,128)(2,1)}, bf16[128,2560]{1,0:T(8,128)(2,1)S(1)}, u32[]{:S(2)}) copy-start(bf16[128,2560]{1,0:T(8,128)(2,1)S(1)} %collective-permute-done.13.refs_2_) | copy-start | bytes 1966084
  56.4 1.8 %copy-start.1 = (bf16[128,8192]{1,0:T(8,128)(2,1)S(1)}, bf16[128,8192]{1,0:T(8,128)(2,1)}, u32[]{:S(2)}) copy-start(bf16[128,8192]{1,0:T(8,128)(2,1)} %x.1) | copy-start | bytes 6291460
  60.3 34.7 %all-to-all-start.2 = ((bf16[32,144,128]{2,1,0:T(8,128)(2,1)}), bf16[32,144,128]{2,1,0:T(8,128)(2,1)S(1)}, u32[]{:S(2)}, u32[]{:S(2)}) async-start(bf16[32,144,128]{2,1,0:T(8,128)(2,1)} %get-tuple-element.50), calls=%async_computation.2 | async-start | bytes 2359296 | tf_op jit(solution)/shard_map/gradients_back/all_to_all | solution.py:400
  65.9 29.1 %collective-permute-start.15 = (bf16[128,1536]{1,0:T(8,128)(2,1)}, bf16[128,1536]{1,0:T(8,128)(2,1)}, u32[]{:S(2)}, u32[]{:S(2)}) collective-permute-start(bf16[128,1536]{1,0:T(8,128)(2,1)} %copy-done.7), channel_id=1, source_target_pairs={{0,5},{1,4},{2,7},{3,6},{4,1},{5,0},{6,3},{7,2},{8,13},{9,12},{10,... | collective-permute-start | bytes 1179656 | tf_op jit(solution)/shard_map/pieces21/ppermute | solution.py:277
  68.6 20.8 %collective-permute-start.14 = (s32[16]{0:T(128)S(1)}, s32[16]{0:T(128)S(1)}, u32[]{:S(2)}, u32[]{:S(2)}) collective-permute-start(s32[16]{0:T(128)S(1)} %select_reduce_fusion.slots.refs_0_), channel_id=1, source_target_pairs={{0,1},{1,0},{2,3},{3,2},{4,5},{5,4},{6,7},{7,6},{8,9},{9,8},{10,11... | collective-permute-start | bytes 200 | tf_op jit(solution)/shard_map/slots_dp/ppermute | solution.py:277
  94.9 3.0 %copy-start.4 = (bf16[128,2560]{1,0:T(8,128)(2,1)S(1)}, bf16[128,2560]{1,0:T(8,128)(2,1)}, u32[]{:S(2)}) copy-start(bf16[128,2560]{1,0:T(8,128)(2,1)} %copy-done.3) | copy-start | bytes 1966084
  94.9 3.0 %copy-start.6 = (bf16[128,1536]{1,0:T(8,128)(2,1)S(1)}, bf16[128,1536]{1,0:T(8,128)(2,1)}, u32[]{:S(2)}) copy-start(bf16[128,1536]{1,0:T(8,128)(2,1)} %copy-done.5) | copy-start | bytes 1179652
  96.4 8.0 %collective-permute-start.16 = (bf16[8,64,256]{2,1,0:T(8,128)(2,1)S(1)}, bf16[8,64,256]{2,1,0:T(8,128)(2,1)S(1)}, u32[]{:S(2)}, u32[]{:S(2)}) collective-permute-start(bf16[8,64,256]{2,1,0:T(8,128)(2,1)S(1)} %get-tuple-element.59), channel_id=1, source_target_pairs={{0,1},{1,0},{2,3},{3,2},{4,5},{5,4},{6,7},{7,6},{8,9},{9,8},{10,11... | collective-permute-start | bytes 786440 | tf_op jit(solution)/shard_map/grads_dp/ppermute | solution.py:277
